TPU v7x, 32 devices: a whole 2x2x4 slice. The times are simulated.
32 devices in a mesh: dp: 8 (over y, x, core), mp: 4 (over z).
Axes of the slice: x: 2, y: 2, z: 4, core: 2. Of those that a mesh axis runs over, the one named last changes fastest.
Arguments:
- tokens: bfloat16 [12288, 768], P(('dp', 'mp')), may hold values from -6 to 6
- w_qkv: float32 [2, 3, 768, 768], P(None, None, 'dp', 'mp'), may hold values from -0.21875 to 0.21875
- b_qkv: float32 [2, 3, 768], P(None, None, 'mp'), may hold values from -3 to 3
- w_out: float32 [2, 768, 768], P(None, 'mp', 'dp'), may hold values from -0.875 to 0.875
- vectors: float32 [2, 6, 768], replicated
- w_in: float32 [2, 768, 3072], P(None, 'dp', 'mp'), may hold values from -0.21875 to 0.21875
- b_in: float32 [2, 3072], P(None, 'mp'), may hold values from -3 to 3
- w_back: float32 [2, 3072, 768], P(None, 'mp', 'dp'), may hold values from -0.15625 to 0.15625
- cotangent: bfloat16 [12288, 768], P(('dp', 'mp')), may hold values from -6 to 6
- lengths: int32 [8, 3], P('dp'), may hold values from 0 to 1536, as said below
- buckets: int32 [8], P('dp'), may hold values from 0 to 2, as said below
Outputs:
- output: bfloat16 [12288, 768], P(('dp', 'mp'))
- grad_tokens: float32 [12288, 768], P(('dp', 'mp'))
- grad_w_qkv: float32 [2, 3, 768, 768], P(None, None, 'dp', 'mp')
- grad_b_qkv: float32 [2, 3, 768], P(None, None, 'mp')
- grad_w_out: float32 [2, 768, 768], P(None, 'mp', 'dp')
- grad_vectors: float32 [2, 6, 768], replicated
- grad_w_in: float32 [2, 768, 3072], P(None, 'dp', 'mp')
- grad_b_in: float32 [2, 3072], P(None, 'mp')
- grad_w_back: float32 [2, 3072, 768], P(None, 'mp', 'dp')
Inputs may be any that keep to these rules, and one draw needn't show every extreme that they name: `buckets`: some index of dp has bucket 2 in every draw. Row i describes slab i, held by index i // 1 of dp with bucket b: its first 3 - b entries are the lengths of its 3 - b sequences, each from half the slot 1536 // (3 - b) to the whole slot, one of them exactly the whole slot; the remaining entries are 0.
All inputs are finite; a program needn't handle non-finite values.
Results may differ from a plain program's by a relative error of at most 0.02.
Values may be sent and summed in bfloat16 or wider, within the bound.
A program may use at most 192 MiB of HBM per device.

v0:
```python
from functools import partial

import jax
import jax.numpy as jnp
from jax import lax
from jax.sharding import PartitionSpec as P

HD = 64
LEN_MAX = 1536
QBLOCK = 512


EPSILON = 1e-06
NEGATIVE = -1e30


def block_size():
    return QBLOCK


def rotary(turned, places):
    half_size = turned.shape[-1] // 2
    frequency = 10000.0 ** (-2.0 * jnp.arange(half_size, dtype=jnp.float32) / turned.shape[-1])
    angles = places.astype(jnp.float32)[:, None] * frequency[None, :]
    cosine = jnp.cos(angles)[:, None, :]
    sine_part = jnp.sin(angles)[:, None, :]
    first_half = turned[..., :half_size]
    second = turned[..., half_size:]
    return jnp.concatenate(
        [first_half * cosine - second * sine_part, second * cosine + first_half * sine_part],
        axis=-1,
    )


def layer_norm(summed, gain, shift):
    row_mean = jnp.mean(summed, axis=-1, keepdims=True)
    centred = summed - row_mean
    variance = jnp.mean(centred * centred, axis=-1, keepdims=True)
    return centred * lax.rsqrt(variance + EPSILON) * gain + shift


def slab_mask(bucket, seq_lengths, query_places, key_places):
    slot_len = LEN_MAX // (3 - bucket)
    query_seq = query_places // slot_len
    key_seq = key_places // slot_len
    choose = key_seq[:, None] == jnp.arange(3, dtype=jnp.int32)[None, :]
    key_limit = jnp.sum(jnp.where(choose, seq_lengths[None, :], 0), axis=1)
    return (query_seq[:, None] == key_seq[None, :]) & (key_places - key_seq * slot_len < key_limit)[
        None, :
    ]


def block_scores(queries, key_heads, bucket, lengths, block_at):
    block_rows = block_size()
    begin_row = block_at * block_rows
    slab_index = begin_row // LEN_MAX
    slab_start = slab_index * LEN_MAX
    query_block = lax.dynamic_slice_in_dim(queries, begin_row, block_rows, 0)
    seq_lengths = lax.dynamic_index_in_dim(lengths, slab_index, 0, keepdims=False)
    query_places = begin_row - slab_start + jnp.arange(block_rows, dtype=jnp.int32)
    key_places = jnp.arange(LEN_MAX, dtype=jnp.int32)
    visible = slab_mask(bucket, seq_lengths, query_places, key_places)
    scores = jnp.einsum(
        "qhd,khd->hqk", query_block, key_heads, preferred_element_type=jnp.float32
    ) * queries.shape[-1] ** (-0.5)
    return (
        jnp.where(visible[None], scores, NEGATIVE),
        query_block,
        key_heads,
        begin_row,
        slab_start,
    )


def attend(queries, key_heads, values, bucket, lengths):
    blocks = queries.shape[0] // block_size()

    def one_block(block_at):
        scores, query_block, key_slab, begin_row, slab_start = block_scores(
            queries, key_heads, bucket, lengths, block_at
        )
        maximum = jnp.max(scores, axis=-1, keepdims=True)
        exponent = jnp.exp(scores - maximum)
        normalizer = jnp.sum(exponent, axis=-1, keepdims=True)
        weights = (exponent / normalizer).astype(jnp.bfloat16)
        mixed_heads = jnp.einsum(
            "hqk,khd->qhd", weights, values, preferred_element_type=jnp.float32
        )
        return (mixed_heads.astype(jnp.bfloat16), maximum[..., 0] + jnp.log(normalizer[..., 0]))

    return lax.map(one_block, jnp.arange(blocks, dtype=jnp.int32))


def attend_back(queries, key_heads, values, logsum, grad_mixed, bucket, lengths):
    group_rows, head_count, head_size = queries.shape
    block_rows = block_size()
    blocks = group_rows // block_rows
    score_scale = head_size ** (-0.5)

    def one_block(carry, block_at):
        grad_keys, grad_values = carry
        scores, query_block, key_slab, begin_row, slab_start = block_scores(
            queries, key_heads, bucket, lengths, block_at
        )
        grad_block = lax.dynamic_slice_in_dim(grad_mixed, begin_row, block_rows, 0)
        softmax_rows = jnp.exp(scores - logsum[block_at][..., None])
        weights = softmax_rows.astype(jnp.bfloat16)
        grad_weights = jnp.einsum(
            "qhd,khd->hqk", grad_block, values, preferred_element_type=jnp.float32
        )
        row_delta = jnp.sum(softmax_rows * grad_weights, axis=-1, keepdims=True)
        grad_scores = (softmax_rows * (grad_weights - row_delta) * score_scale).astype(jnp.bfloat16)
        grad_queries = jnp.einsum(
            "hqk,khd->qhd", grad_scores, key_slab, preferred_element_type=jnp.float32
        )
        part_keys = jnp.einsum(
            "hqk,qhd->khd", grad_scores, query_block, preferred_element_type=jnp.float32
        )
        part_values = jnp.einsum(
            "hqk,qhd->khd", weights, grad_block, preferred_element_type=jnp.float32
        )
        grad_keys = grad_keys + part_keys
        grad_values = grad_values + part_values
        return ((grad_keys, grad_values), grad_queries)

    zero_rows = jnp.zeros((group_rows, head_count, head_size), jnp.float32)
    sums, grad_queries = lax.scan(
        one_block, (zero_rows, zero_rows), jnp.arange(blocks, dtype=jnp.int32)
    )
    return (grad_queries.reshape(group_rows, head_count, head_size), sums[0], sums[1])


def fetch(w_qkv, w_out, w_in, w_back, layer_at):
    return (
        lax.all_gather(w_qkv[layer_at].astype(jnp.bfloat16), "dp", axis=1, tiled=True),
        lax.all_gather(w_out[layer_at].astype(jnp.bfloat16), "dp", axis=1, tiled=True),
        lax.all_gather(w_in[layer_at].astype(jnp.bfloat16), "dp", axis=0, tiled=True),
        lax.all_gather(w_back[layer_at].astype(jnp.bfloat16), "dp", axis=1, tiled=True),
    )


def forward_layer(stream, weights, bias_qkv, vector, bias_in, places, bucket, lengths):
    proj_w, out_w, in_w, back_w = weights
    gathered = lax.all_gather(stream.astype(jnp.bfloat16), "mp", axis=0, tiled=True)
    group_rows = gathered.shape[0]
    head_count = proj_w.shape[2] // HD
    projected = (
        jnp.einsum("td,jdc->tjc", gathered, proj_w, preferred_element_type=jnp.float32)
        + bias_qkv[None]
    )
    queries = rotary(projected[:, 0].reshape(group_rows, head_count, HD), places).astype(
        jnp.bfloat16
    )
    key_heads = rotary(projected[:, 1].reshape(group_rows, head_count, HD), places).astype(
        jnp.bfloat16
    )
    values = projected[:, 2].reshape(group_rows, head_count, HD).astype(jnp.bfloat16)
    mixed_heads, logsum = attend(queries, key_heads, values, bucket, lengths)
    mixed_heads = mixed_heads.reshape(group_rows, head_count * HD)
    attended = (
        lax.psum_scatter(
            jnp.dot(mixed_heads, out_w, preferred_element_type=jnp.float32),
            "mp",
            scatter_dimension=0,
            tiled=True,
        )
        + vector[0]
    )
    first_sum = stream + attended
    normed = layer_norm(first_sum, vector[1], vector[2])
    normed_all = lax.all_gather(normed.astype(jnp.bfloat16), "mp", axis=0, tiled=True)
    inner_sum = jnp.dot(normed_all, in_w, preferred_element_type=jnp.float32) + bias_in
    active = jax.nn.gelu(inner_sum, approximate=False).astype(jnp.bfloat16)
    second_sum = (
        normed
        + lax.psum_scatter(
            jnp.dot(active, back_w, preferred_element_type=jnp.float32),
            "mp",
            scatter_dimension=0,
            tiled=True,
        )
        + vector[3]
    )
    result = layer_norm(second_sum, vector[4], vector[5])
    saved_state = (
        gathered,
        queries,
        key_heads,
        values,
        mixed_heads,
        logsum,
        first_sum,
        normed_all,
        inner_sum,
        active,
        second_sum,
    )
    return (result, saved_state)


def backward_layer(gradient, weights, saved_state, vector, places, bucket, lengths):
    proj_w, out_w, in_w, back_w = weights
    (
        gathered,
        queries,
        key_heads,
        values,
        mixed_heads,
        logsum,
        first_sum,
        normed_all,
        inner_sum,
        active,
        second_sum,
    ) = saved_state
    group_rows, head_count = (queries.shape[0], queries.shape[1])
    contract_rows = (((0,), (0,)), ((), ()))
    contract_cols = (((1,), (1,)), ((), ()))
    _, second_back = jax.vjp(layer_norm, second_sum, vector[4], vector[5])
    grad_second, grad_gain_two, grad_shift_two = second_back(gradient)
    grad_bias_back = jnp.sum(grad_second, axis=0)
    grad_fed = lax.all_gather(grad_second.astype(jnp.bfloat16), "mp", axis=0, tiled=True)
    grad_w_back = lax.dot_general(
        active, grad_fed, contract_rows, preferred_element_type=jnp.float32
    )
    grad_active = lax.dot_general(
        grad_fed, back_w, contract_cols, preferred_element_type=jnp.float32
    )
    _, gelu_back = jax.vjp(partial(jax.nn.gelu, approximate=False), inner_sum)
    grad_inner = gelu_back(grad_active)[0]
    grad_bias_in = jnp.sum(grad_inner, axis=0)
    grad_inner_low = grad_inner.astype(jnp.bfloat16)
    grad_w_in = lax.dot_general(
        normed_all, grad_inner_low, contract_rows, preferred_element_type=jnp.float32
    )
    grad_normed = grad_second + lax.psum_scatter(
        lax.dot_general(grad_inner_low, in_w, contract_cols, preferred_element_type=jnp.float32),
        "mp",
        scatter_dimension=0,
        tiled=True,
    )
    _, first_back = jax.vjp(layer_norm, first_sum, vector[1], vector[2])
    grad_first, grad_gain_one, grad_shift_one = first_back(grad_normed)
    grad_bias_out = jnp.sum(grad_first, axis=0)
    grad_attended = lax.all_gather(grad_first.astype(jnp.bfloat16), "mp", axis=0, tiled=True)
    grad_w_out = lax.dot_general(
        mixed_heads, grad_attended, contract_rows, preferred_element_type=jnp.float32
    )
    grad_mixed = lax.dot_general(
        grad_attended, out_w, contract_cols, preferred_element_type=jnp.float32
    )
    grad_mixed = grad_mixed.astype(jnp.bfloat16).reshape(group_rows, head_count, HD)
    grad_queries, grad_keys, grad_values = attend_back(
        queries, key_heads, values, logsum, grad_mixed, bucket, lengths
    )
    _, rotate_back = jax.vjp(
        lambda turned: rotary(turned, places), jnp.zeros((group_rows, head_count, HD), jnp.float32)
    )
    grad_proj = jnp.stack(
        [
            rotate_back(grad_queries)[0].reshape(group_rows, head_count * HD),
            rotate_back(grad_keys)[0].reshape(group_rows, head_count * HD),
            grad_values.reshape(group_rows, head_count * HD),
        ],
        axis=1,
    )
    grad_bias_qkv = jnp.sum(grad_proj, axis=0)
    grad_proj_low = grad_proj.astype(jnp.bfloat16)
    grad_w_qkv = jnp.einsum(
        "tjc,td->jdc", grad_proj_low, gathered, preferred_element_type=jnp.float32
    )
    grad_stream = grad_first + lax.psum_scatter(
        jnp.einsum("tjc,jdc->td", grad_proj_low, proj_w, preferred_element_type=jnp.float32),
        "mp",
        scatter_dimension=0,
        tiled=True,
    )
    matrices = (grad_w_qkv[None], grad_w_out[None], grad_w_in[None], grad_w_back[None])
    columns = (grad_bias_qkv[None], grad_bias_in[None])
    vector_grads = jnp.stack(
        [
            grad_bias_out,
            grad_gain_one,
            grad_shift_one,
            grad_bias_back,
            grad_gain_two,
            grad_shift_two,
        ]
    )[None]
    return (grad_stream, (matrices, columns, vector_grads))


def reduce_grads(matrices, columns, vector_grads):
    summed = (
        lax.psum_scatter(matrices[0], "dp", scatter_dimension=2, tiled=True),
        lax.psum_scatter(matrices[1], "dp", scatter_dimension=2, tiled=True),
        lax.psum_scatter(matrices[2], "dp", scatter_dimension=1, tiled=True),
        lax.psum_scatter(matrices[3], "dp", scatter_dimension=2, tiled=True),
    )
    column_sums = lax.psum(columns, "dp")
    vector_sums = lax.psum(vector_grads, ("dp", "mp"))
    return (summed, column_sums, vector_sums)


def join(entries):
    matrices = tuple(
        (jnp.concatenate([entry[0][member] for entry in entries], axis=0) for member in range(4))
    )
    columns = tuple(
        (jnp.concatenate([entry[1][member] for entry in entries], axis=0) for member in range(2))
    )
    vector_grads = jnp.concatenate([entry[2] for entry in entries], axis=0)
    return (matrices, columns, vector_grads)


def per_device(
    tokens, w_qkv, b_qkv, w_out, vectors, w_in, b_in, w_back, cotangent, lengths, buckets
):
    layers = w_qkv.shape[0]
    group_rows = tokens.shape[0] * lax.axis_size("mp")
    bucket = buckets[0]
    slot_len = LEN_MAX // (3 - bucket)
    places = jnp.arange(group_rows, dtype=jnp.int32) % LEN_MAX % slot_len
    stream = tokens.astype(jnp.float32)
    states = []
    for layer_at in range(layers):
        weights = fetch(w_qkv, w_out, w_in, w_back, layer_at)
        stream, saved_state = forward_layer(
            stream,
            weights,
            b_qkv[layer_at],
            vectors[layer_at],
            b_in[layer_at],
            places,
            bucket,
            lengths,
        )
        states.append(saved_state)
    result = stream.astype(jnp.bfloat16)
    gradient = cotangent.astype(jnp.float32)
    pending = []
    for layer_at in reversed(range(layers)):
        weights = fetch(w_qkv, w_out, w_in, w_back, layer_at)
        gradient, local_grads = backward_layer(
            gradient, weights, states[layer_at], vectors[layer_at], places, bucket, lengths
        )
        pending.insert(0, reduce_grads(local_grads[0], local_grads[1], local_grads[2]))
    matrices, columns, vector_grads = join(pending)
    return (
        result,
        gradient,
        matrices[0],
        columns[0],
        matrices[1],
        vector_grads,
        matrices[2],
        columns[1],
        matrices[3],
    )


def solution(mesh):
    return jax.shard_map(
        per_device,
        mesh=mesh,
        in_specs=(
            P(("dp", "mp"), None),
            P(None, None, "dp", "mp"),
            P(None, None, "mp"),
            P(None, "mp", "dp"),
            P(),
            P(None, "dp", "mp"),
            P(None, "mp"),
            P(None, "mp", "dp"),
            P(("dp", "mp"), None),
            P("dp", None),
            P("dp"),
        ),
        out_specs=(
            P(("dp", "mp"), None),
            P(("dp", "mp"), None),
            P(None, None, "dp", "mp"),
            P(None, None, "mp"),
            P(None, "mp", "dp"),
            P(),
            P(None, "dp", "mp"),
            P(None, "mp"),
            P(None, "mp", "dp"),
        ),
        check_vma=False,
    )
```

profile of v0, /device:TPU:0, one launch (start us, length us, event | category | flops | bytes accessed | tf_op | source)
XLA Modules:
  0.0 1839.7 jit_solution(3210445214985032689)
XLA Ops:
  42.7 21.0 %all-gather.21.cloned.1.call-done = bf16[1536,768]{1,0:T(8,128)(2,1)} async-done(((bf16[384,768]{1,0:T(8,128)(2,1)}), bf16[1536,768]{1,0:T(8,128)(2,1)}) %all-gather.21.cloned.1.call-update) | async-done | bytes 2359312 | tf_op jit(solution)/shard_map/all_gather | solution.py:144
  68.5 32.3 %while.66 = (s32[]{:T(128)}, bf16[3,512,3,64]{1,3,2,0:T(8,128)(2,1)S(1)}, f32[3,3,512]{2,1,0:T(4,128)S(1)}, s32[3]{0:T(128)S(1)}, s32[]{:T(128)}, /*index=5*/s32...) while((s32[]{:T(128)}, ...), condition=%wide.region_4.5_spmd, body=%wide.region_0.4_spmd.sunk | while | flops 634007040 | bytes 33127784 | solution.py:91
  108.0 81.7 %reduce-scatter.23.cloned.1.call-done = f32[384,768]{1,0:T(8,128)} async-done(((f32[1536,768]{1,0:T(8,128)}), f32[384,768]{1,0:T(8,128)}) %reduce-scatter.23.cloned.1.call-update) | async-done | bytes 1179664 | tf_op jit(solution)/shard_map/reduce_scatter | solution.py:161
  194.3 48.9 %all-gather.23.cloned.1.call-done = bf16[1536,768]{1,0:T(8,128)(2,1)} async-done(((bf16[384,768]{1,0:T(8,128)(2,1)}), bf16[1536,768]{1,0:T(8,128)(2,1)}) %all-gather.23.cloned.1.call-update) | async-done | bytes 2359312 | tf_op jit(solution)/shard_map/all_gather | solution.py:171
  243.2 14.8 multiply_convert_fusion.3
  273.1 85.2 %reduce-scatter.25.cloned.1.call-done = f32[384,768]{1,0:T(8,128)} async-done(((f32[1536,768]{1,0:T(8,128)}), f32[384,768]{1,0:T(8,128)}) %reduce-scatter.25.cloned.1.call-update) | async-done | bytes 1179664 | tf_op jit(solution)/shard_map/reduce_scatter | solution.py:176
  373.6 14.8 all-gather.4
  391.0 21.7 %all-gather.25.cloned.1.call-done = bf16[1536,768]{1,0:T(8,128)(2,1)} async-done(((bf16[384,768]{1,0:T(8,128)(2,1)}), bf16[1536,768]{1,0:T(8,128)(2,1)}) %all-gather.25.cloned.1.call-update) | async-done | bytes 2359312 | tf_op jit(solution)/shard_map/all_gather | solution.py:144
  418.5 34.1 %while.67 = (s32[]{:T(128)}, bf16[3,512,3,64]{1,3,2,0:T(8,128)(2,1)S(1)}, f32[3,3,512]{2,1,0:T(4,128)}, s32[3]{0:T(128)S(1)}, s32[]{:T(128)}, /*index=5*/s32[]{:...) while((s32[]{:T(128)}, ...), condition=%wide.region_15.16_spmd, body=%wide.region_11.15_spmd.sunk | while | flops 634007040 | bytes 33123688 | solution.py:91
  457.9 83.4 %reduce-scatter.27.cloned.1.call-done = f32[384,768]{1,0:T(8,128)} async-done(((f32[1536,768]{1,0:T(8,128)}), f32[384,768]{1,0:T(8,128)}) %reduce-scatter.27.cloned.1.call-update) | async-done | bytes 1179664 | tf_op jit(solution)/shard_map/reduce_scatter | solution.py:161
  545.4 49.8 %all-gather.27.cloned.1.call-done = bf16[1536,768]{1,0:T(8,128)(2,1)} async-done(((bf16[384,768]{1,0:T(8,128)(2,1)}), bf16[1536,768]{1,0:T(8,128)(2,1)}) %all-gather.27.cloned.1.call-update) | async-done | bytes 2359312 | tf_op jit(solution)/shard_map/all_gather | solution.py:171
  595.2 15.1 multiply_convert_fusion.2
  626.3 85.2 %reduce-scatter.29.cloned.1.call-done = f32[384,768]{1,0:T(8,128)} async-done(((f32[1536,768]{1,0:T(8,128)}), f32[384,768]{1,0:T(8,128)}) %reduce-scatter.29.cloned.1.call-update) | async-done | bytes 1179664 | tf_op jit(solution)/shard_map/reduce_scatter | solution.py:176
  718.8 51.1 %all-gather.29.cloned.1.call-done = bf16[1536,768]{1,0:T(8,128)(2,1)} async-done(((bf16[384,768]{1,0:T(8,128)(2,1)}), bf16[1536,768]{1,0:T(8,128)(2,1)}) %all-gather.29.cloned.1.call-update) | async-done | bytes 2359312 | tf_op jit(solution)/shard_map/all_gather | solution.py:222
  784.3 84.2 %reduce-scatter.31.cloned.1.call-done = f32[384,768]{1,0:T(8,128)} async-done(((f32[1536,768]{1,0:T(8,128)}), f32[384,768]{1,0:T(8,128)}) %reduce-scatter.31.cloned.1.call-update) | async-done | bytes 1179664 | tf_op jit(solution)/shard_map/reduce_scatter | solution.py:236
  874.0 50.6 %all-gather.31.cloned.1.call-done = bf16[1536,768]{1,0:T(8,128)(2,1)} async-done(((bf16[384,768]{1,0:T(8,128)(2,1)}), bf16[1536,768]{1,0:T(8,128)(2,1)}) %all-gather.31.cloned.1.call-update) | async-done | bytes 2359312 | tf_op jit(solution)/shard_map/all_gather | solution.py:245
  929.4 163.5 %while.68 = (s32[]{:T(128)}, f32[1536,3,64]{0,2,1:T(8,128)}, f32[1536,3,64]{0,2,1:T(8,128)S(1)}, f32[3,512,3,64]{1,0,3,2:T(4,128)}, s32[3]{0:T(128)S(1)}, /*inde...) while((s32[]{:T(128)}, f32[1536,3,64]{0,2,1:T(8,128)}, ...), condition=%wide.region_30.31_spmd.clone, body=%wide.region_27.30_spmd.clone.sunk | while | flops 1545784320 | bytes 135912976 | solution.py:127
  959.6 15.2 fusion.303
  1013.8 15.5 fusion.303
  1068.4 15.5 fusion.303
  1103.7 83.5 %reduce-scatter.33.cloned.1.call-done = f32[384,768]{1,0:T(8,128)} async-done(((f32[1536,768]{1,0:T(8,128)}), f32[384,768]{1,0:T(8,128)}) %reduce-scatter.33.cloned.1.call-update) | async-done | bytes 1179664 | tf_op jit(solution)/shard_map/reduce_scatter | solution.py:272
  1191.9 51.1 %all-gather.33.cloned.1.call-done = bf16[1536,768]{1,0:T(8,128)(2,1)} async-done(((bf16[384,768]{1,0:T(8,128)(2,1)}), bf16[1536,768]{1,0:T(8,128)(2,1)}) %all-gather.33.cloned.1.call-update) | async-done | bytes 2359312 | tf_op jit(solution)/shard_map/all_gather | solution.py:222
  1256.8 84.2 %reduce-scatter.35.cloned.1.call-done = f32[384,768]{1,0:T(8,128)} async-done(((f32[1536,768]{1,0:T(8,128)}), f32[384,768]{1,0:T(8,128)}) %reduce-scatter.35.cloned.1.call-update) | async-done | bytes 1179664 | tf_op jit(solution)/shard_map/reduce_scatter | solution.py:236
  1402.1 170.0 %while.69 = (s32[]{:T(128)}, f32[1536,3,64]{0,2,1:T(8,128)}, f32[1536,3,64]{0,2,1:T(8,128)S(1)}, f32[3,512,3,64]{1,0,3,2:T(4,128)}, s32[3]{0:T(128)S(1)}, /*inde...) while((s32[]{:T(128)}, f32[1536,3,64]{0,2,1:T(8,128)}, ...), condition=%wide.region_40.41_spmd.clone, body=%wide.region_37.40_spmd.clone.sunk | while | flops 1545784320 | bytes 133553632 | solution.py:127
  1433.5 15.5 fusion.317
  1476.2 14.0 fusion.319
  1490.2 16.1 fusion.317
  1546.8 16.3 fusion.317
  1623.7 36.1 %reduce-scatter.39.cloned.1.call-done = f32[1,96,768]{2,1,0:T(8,128)} async-done(((f32[1,768,768]{2,1,0:T(8,128)}), f32[1,96,768]{2,1,0:T(8,128)}) %reduce-scatter.39.cloned.1.call-update) | async-done | bytes 294928 | tf_op jit(solution)/shard_map/reduce_scatter | solution.py:297
  1665.5 40.4 %all-reduce.10 = (f32[1,6,768]{2,1,0:T(8,128)}, f32[1,6,768]{2,1,0:T(8,128)}) all-reduce(f32[1,6,768]{2,1,0:T(8,128)} %bitcast.347, f32[1,6,768]{2,1,0:T(8,128)} %bitcast.348), channel_id=1, replica_groups=mesh['dp'=8,'mp'=4] {'dp','mp'}, use_global_device_ids=true, to_apply=%region_63.64 | all-reduce | flops 9216 | bytes 73728 | tf_op jit(solution)/shard_map/psum | solution.py:301
  1707.6 23.4 %all-reduce.11 = (f32[1,3,192]{2,1,0:T(4,128)S(1)}, f32[1,3,192]{2,1,0:T(4,128)S(1)}, f32[1,768]{1,0:T(1,128)S(1)}, f32[1,768]{1,0:T(1,128)S(1)}) all-reduce(f32[1,3,192]{2,1,0:T(4,128)S(1)} %bitcast.351, f32[1,3,192]{2,1,0:T(4,128)S(1)} %bitcast.352, f32[1,768]{1,0:T(1,128)S(1)} %copy-done.98, ...), channel_id=1, replica_groups=mesh['dp'=8,'mp'=4] {'dp'}, use_global_device_ids=true, to_apply=%region_47.48 | all-reduce | flops 2688 | bytes 21504 | tf_op jit(solution)/shard_map/psum | solution.py:300
  1744.1 85.0 %reduce-scatter.37.cloned.1.call-done = f32[384,768]{1,0:T(8,128)} async-done(((f32[1536,768]{1,0:T(8,128)}), f32[384,768]{1,0:T(8,128)}) %reduce-scatter.37.cloned.1.call-update) | async-done | bytes 1179664 | tf_op jit(solution)/shard_map/reduce_scatter | solution.py:272
  (603 shorter events, 581.7 us)
Async XLA Ops:
  8.0 55.6 %all-gather.21.cloned.1.call-start = ((), (), s32[]{:S(2)}) async-start(), calls=%async_computation.14 | async-start | bytes 2949120 | tf_op jit(solution)/shard_map/all_gather | solution.py:144
  8.7 180.9 %reduce-scatter.23.cloned.1.call-start = ((), (), s32[]{:S(2)}) async-start(), calls=%async_computation.15 | async-start | bytes 5898240 | tf_op jit(solution)/shard_map/reduce_scatter | solution.py:161
  105.4 88.9 %all-gather.37.cloned.1.call-start = ((), (), s32[]{:S(2)}) async-start(), calls=%async_computation.32 | async-start | bytes 1327104 | tf_op jit(solution)/shard_map/all_gather | solution.py:137
  107.2 136.0 %all-gather.23.cloned.1.call-start = ((), (), s32[]{:S(2)}) async-start(), calls=%async_computation.16 | async-start | bytes 2949120 | tf_op jit(solution)/shard_map/all_gather | solution.py:171
  108.0 250.3 %copy-start.63 = (f32[768]{0:T(1024)}, f32[768]{0:T(1024)S(1)}, u32[]{:S(2)}) copy-start(f32[768]{0:T(1024)S(1)} %get-tuple-element.967) | copy-start | bytes 9220
  108.0 433.4 %copy-start.65 = (f32[768]{0:T(1024)}, f32[768]{0:T(1024)S(1)}, u32[]{:S(2)}) copy-start(f32[768]{0:T(1024)S(1)} %get-tuple-element.964) | copy-start | bytes 9220
  191.2 167.1 %copy-start.4 = (f32[384,768]{1,0:T(8,128)}, f32[384,768]{1,0:T(8,128)S(1)}, u32[]{:S(2)}) copy-start(f32[384,768]{1,0:T(8,128)S(1)} %get-tuple-element.1094) | copy-start | bytes 3538948
  192.6 75.0 %all-gather.39.cloned.1.call-start = ((), (), s32[]{:S(2)}) async-start(), calls=%async_computation.33 | async-start | bytes 1327104 | tf_op jit(solution)/shard_map/all_gather | solution.py:138
  193.4 164.9 %reduce-scatter.25.cloned.1.call-start = ((), (), s32[]{:S(2)}) async-start(), calls=%async_computation.17 | async-start | bytes 5898240 | tf_op jit(solution)/shard_map/reduce_scatter | solution.py:176
  273.0 139.7 %all-gather.25.cloned.1.call-start = ((), (), s32[]{:S(2)}) async-start(), calls=%async_computation.18 | async-start | bytes 2949120 | tf_op jit(solution)/shard_map/all_gather | solution.py:144
  360.1 181.3 %copy-start.6 = (f32[384,768]{1,0:T(8,128)}, f32[384,768]{1,0:T(8,128)S(1)}, u32[]{:S(2)}) copy-start(f32[384,768]{1,0:T(8,128)S(1)} %get-tuple-element.1090) | copy-start | bytes 3538948
  360.1 181.3 %copy-start.70 = (f32[384]{0:T(512)}, f32[384]{0:T(512)S(1)}, u32[]{:S(2)}) copy-start(f32[384]{0:T(512)S(1)} %broadcast_multiply_fusion.2) | copy-start | bytes 4612
  361.5 179.8 %reduce-scatter.27.cloned.1.call-start = ((), (), s32[]{:S(2)}) async-start(), calls=%async_computation.19 | async-start | bytes 5898240 | tf_op jit(solution)/shard_map/reduce_scatter | solution.py:161
  457.1 88.2 %all-gather.41.cloned.1.call-start = ((), (), s32[]{:S(2)}) async-start(), calls=%async_computation.34 | async-start | bytes 1327104 | tf_op jit(solution)/shard_map/all_gather | solution.py:137
  457.9 137.3 %all-gather.27.cloned.1.call-start = ((), (), s32[]{:S(2)}) async-start(), calls=%async_computation.20 | async-start | bytes 2949120 | tf_op jit(solution)/shard_map/all_gather | solution.py:171
  544.5 75.5 %all-gather.43.cloned.1.call-start = ((), (), s32[]{:S(2)}) async-start(), calls=%async_computation.35 | async-start | bytes 1327104 | tf_op jit(solution)/shard_map/all_gather | solution.py:138
  545.1 166.5 %reduce-scatter.29.cloned.1.call-start = ((), (), s32[]{:S(2)}) async-start(), calls=%async_computation.21 | async-start | bytes 5898240 | tf_op jit(solution)/shard_map/reduce_scatter | solution.py:176
  626.3 143.6 %all-gather.29.cloned.1.call-start = ((), (), s32[]{:S(2)}) async-start(), calls=%async_computation.22 | async-start | bytes 2949120 | tf_op jit(solution)/shard_map/all_gather | solution.py:222
  718.7 149.8 %reduce-scatter.31.cloned.1.call-start = ((), (), s32[]{:S(2)}) async-start(), calls=%async_computation.23 | async-start | bytes 5898240 | tf_op jit(solution)/shard_map/reduce_scatter | solution.py:236
  784.3 140.3 %all-gather.31.cloned.1.call-start = ((), (), s32[]{:S(2)}) async-start(), calls=%async_computation.24 | async-start | bytes 2949120 | tf_op jit(solution)/shard_map/all_gather | solution.py:245
  873.9 313.3 %reduce-scatter.33.cloned.1.call-start = ((), (), s32[]{:S(2)}) async-start(), calls=%async_computation.25 | async-start | bytes 5898240 | tf_op jit(solution)/shard_map/reduce_scatter | solution.py:272
  1103.3 139.7 %all-gather.33.cloned.1.call-start = ((), (), s32[]{:S(2)}) async-start(), calls=%async_computation.26 | async-start | bytes 2949120 | tf_op jit(solution)/shard_map/all_gather | solution.py:222
  1191.8 149.1 %reduce-scatter.35.cloned.1.call-start = ((), (), s32[]{:S(2)}) async-start(), calls=%async_computation.27 | async-start | bytes 5898240 | tf_op jit(solution)/shard_map/reduce_scatter | solution.py:236
  1256.8 140.5 %all-gather.35.cloned.1.call-start = ((), (), s32[]{:S(2)}) async-start(), calls=%async_computation.28 | async-start | bytes 2949120 | tf_op jit(solution)/shard_map/all_gather | solution.py:245
  1346.6 266.0 %reduce-scatter.49.cloned.1.call-start = ((), (), s32[]{:S(2)}) async-start(), calls=%async_computation.39 | async-start | bytes 884736
  1350.5 263.8 %reduce-scatter.45.cloned.1.call-start = ((), (), s32[]{:S(2)}) async-start(), calls=%async_computation.37 | async-start | bytes 2211840
  1360.9 259.2 %all-reduce.15.cloned.1.call-start = ((), (), s32[]{:S(2)}) async-start(), calls=%async_computation.40 | async-start | bytes 9437184
  1378.9 244.9 %reduce-scatter.41.cloned.1.call-start = ((), (), s32[]{:S(2)}) async-start(), calls=%async_computation.31 | async-start | bytes 2654208 | tf_op jit(solution)/shard_map/reduce_scatter | solution.py:297
  1385.7 274.1 %reduce-scatter.39.cloned.1.call-start = ((), (), s32[]{:S(2)}) async-start(), calls=%async_computation.30 | async-start | bytes 2654208 | tf_op jit(solution)/shard_map/reduce_scatter | solution.py:297
  1391.7 340.6 %reduce-scatter.47.cloned.1.call-start = ((), (), s32[]{:S(2)}) async-start(), calls=%async_computation.38 | async-start | bytes 884736
  1582.7 159.0 %reduce-scatter.43.cloned.1.call-start = ((), (), s32[]{:S(2)}) async-start(), calls=%async_computation.36 | async-start | bytes 2211840
  1597.1 232.1 %reduce-scatter.37.cloned.1.call-start = ((), (), s32[]{:S(2)}) async-start(), calls=%async_computation.29 | async-start | bytes 5898240 | tf_op jit(solution)/shard_map/reduce_scatter | solution.py:272
  (109 other events, 3059.3 us)
Sparse Core Ops, SparseCore 0:
  10.4 53.1 all-gather.20
  105.5 84.0 reduce-scatter.22
  361.7 50.9 all-gather.24
  457.3 84.0 reduce-scatter.26
  718.8 50.9 all-gather.28
  784.4 84.0 reduce-scatter.30
  1192.0 50.9 all-gather.32
  1256.9 84.0 reduce-scatter.34
Sparse Core Ops, SparseCore 1:
  108.4 22.7 all-gather.36
  192.7 50.5 all-gather.22
  245.0 22.5 all-gather.38
  273.1 85.1 reduce-scatter.24
  460.4 22.7 all-gather.40
  544.6 50.5 all-gather.26
  597.5 22.5 all-gather.42
  626.4 85.1 reduce-scatter.28
  874.0 50.5 all-gather.30
  1103.4 83.8 reduce-scatter.32
  1346.7 50.5 all-gather.34
  1400.4 33.6 reduce-scatter.48
  1437.3 40.1 reduce-scatter.44
  1481.3 86.6 all-reduce.14
  1571.3 42.4 reduce-scatter.40
  1617.4 42.3 reduce-scatter.38
  1663.0 34.9 reduce-scatter.46
  1701.4 40.3 reduce-scatter.42
  1744.0 85.1 reduce-scatter.36
where the time goes:
time: 1850 us; the launch traced here: 1840 us
  waiting for transfers between devices  1040 us (56%)
  matrix products  400 us (22%)
  local copies, waits for them, and re-layouts  169 us (9%)
  blocking collectives  114 us (6%)
  other arithmetic  77.8 us (4%)
  loops' own time  19.6 us (1%)
  between operations  19.2 us (1%)
    reduce_scatter x2, waiting for transfers between devices, forward_layer(): lax.psum_scatter(jnp.dot(active, back_w, preferred_element_type=jnp.float...  170 us
    reduce_scatter x2, waiting for transfers between devices, backward_layer(): lax.psum_scatter(jnp.einsum('tjc,jdc->td', grad_proj_low, proj_w, preferr...  169 us
    reduce_scatter x2, waiting for transfers between devices, backward_layer(): lax.psum_scatter(lax.dot_general(grad_inner_low, in_w, contract_cols, pre...  168 us
    reduce_scatter x2, waiting for transfers between devices, forward_layer(): lax.psum_scatter(jnp.dot(mixed_heads, out_w, preferred_element_type=jnp.f...  165 us
    all_gather x2, waiting for transfers between devices, backward_layer(): lax.all_gather(grad_second.astype(jnp.bfloat16), 'mp', axis=0, tiled=True)  102 us
    all_gather x2, waiting for transfers between devices, forward_layer(): lax.all_gather(normed.astype(jnp.bfloat16), 'mp', axis=0, tiled=True)  98.7 us
    dot_general x6, matrix products, one_block(): jnp.einsum('hqk,qhd->khd', grad_scores, query_block, preferred_element_ty...  94.1 us
    dot_general x6, matrix products, one_block(): jnp.einsum('hqk,khd->qhd', grad_scores, key_slab, preferred_element_type=...  79.8 us
  transfers between devices with their start and end apart: 27, of which 20 were waited for; matrix products, arithmetic and copies ran while one was open for 17% of the time, Pallas kernels for 0%

commit v1 on v0

v1 whole, which is shorter than its diff:
```python
from functools import partial

import jax
import jax.numpy as jnp
from jax import lax
from jax.experimental import pallas as pl
from jax.experimental.pallas import tpu as pltpu
from jax.sharding import PartitionSpec as P

HD = 64
LEN_MAX = 1536
EPSILON = 1e-06
NEGATIVE = -1e30
F32 = jnp.float32
BF16 = jnp.bfloat16
LANES = 128
MP = 4
VMEM_LIMIT = 60 * 1024 * 1024


def nn(a, b):
    return lax.dot_general(a, b, (((1,), (0,)), ((), ())), preferred_element_type=F32)


def nt(a, b):
    return lax.dot_general(a, b, (((1,), (1,)), ((), ())), preferred_element_type=F32)


def core_swap(x):
    n = lax.axis_size("dp")
    return lax.ppermute(x, "dp", [(i, i ^ 1) for i in range(n)])


def plane_swap(x, first):
    n = lax.axis_size("dp")
    hops = (2, 4) if first else (4, 2)
    return lax.ppermute(x, "dp", [(i, i ^ hops[i % 2]) for i in range(n)])


def column_shift(x, k):
    return lax.ppermute(x, "mp", [(i, (i + k) % MP) for i in range(MP)])


def pair_swap(x):
    return lax.ppermute(x, "mp", [(i, i ^ 1) for i in range(MP)])


def relayout(x):
    n = lax.axis_size("dp")
    pairs = []
    for d in range(n):
        for z in range(MP):
            if (d % 2) != (z // 2):
                pairs.append((d * MP + z, (d ^ 1) * MP + (z ^ 2)))
            else:
                pairs.append((d * MP + z, d * MP + z))
    return lax.ppermute(x, ("dp", "mp"), pairs)


def turn_columns(x, z):
    return jnp.stack([lax.dynamic_index_in_dim(x, (z - k) % MP, 0, False) for k in range(MP)])


def gather_small(x):
    return jnp.stack([x] + [column_shift(x, k) for k in range(1, MP)])


def gather_bundle(block):
    if lax.axis_size("dp") != 8:
        z = lax.axis_index("mp")
        whole = lax.all_gather(block, "dp", axis=0, tiled=True)
        whole = lax.all_gather(whole, "mp", axis=0, tiled=False)
        return [turn_columns(whole, z)]
    own = gather_small(block)
    one = plane_swap(own, True)
    two = plane_swap(own, False)
    three = plane_swap(one, False)
    mine = [own, one, two, three]
    return mine + [core_swap(m) for m in mine]


def row_offsets(g, c, rows):
    if lax.axis_size("dp") != 8:
        return [jnp.int32(0)]
    result = []
    for core in (c, 1 - c):
        first = jnp.where(core == 0, 1, 2)
        for hop in (0, first, 3 - first, 3):
            result.append(((g ^ hop) * 2 + core) * rows)
    return result


def send_columns(v):
    total = v[0].astype(F32)
    for k in range(1, MP):
        total = total + column_shift(v[k], -k).astype(F32)
    return total


def reduce_all(keep, away):
    if lax.axis_size("dp") != 8:
        z = lax.axis_index("mp")
        whole = turn_columns(keep[0], z).astype(F32)
        part = lax.psum_scatter(whole, "mp", scatter_dimension=0, tiled=False)
        return lax.psum_scatter(part, "dp", scatter_dimension=0, tiled=True)
    other = core_swap(away)

    def add(i):
        return keep[i].astype(F32) + other[i].astype(F32)

    got = plane_swap(jnp.stack([add(0), add(1)]).astype(BF16), True)
    got_two = plane_swap((add(2) + got[1].astype(F32)).astype(BF16), False)
    v = (add(3) + got[0].astype(F32) + got_two.astype(F32)).astype(BF16)
    return send_columns(v)


def reduce_heads(parts):
    c = lax.axis_index("dp") % 2
    n = lax.axis_size("dp")
    if n != 8:
        z = lax.axis_index("mp")
        wide = jnp.concatenate([parts[0], jnp.zeros_like(parts[0])], axis=0)
        wide = jnp.where(c == 0, wide, jnp.roll(wide, 2, axis=0))
        whole = turn_columns(wide, z).astype(F32)
        part = lax.psum_scatter(whole, "mp", scatter_dimension=0, tiled=False)
        return lax.psum_scatter(part, "dp", scatter_dimension=0, tiled=True)
    got = plane_swap(parts[0:2], True)
    got_two = plane_swap((parts[2].astype(F32) + got[1].astype(F32)).astype(BF16), False)
    v = (parts[3].astype(F32) + got[0].astype(F32) + got_two.astype(F32)).astype(BF16)

    total = column_turn(v[0], 0).astype(F32) + column_turn(v[1], 1).astype(F32)
    rows = total.shape[0] // 2
    kept = lax.dynamic_slice_in_dim(total, c * rows, rows, 0)
    sent = lax.dynamic_slice_in_dim(total, (1 - c) * rows, rows, 0).astype(BF16)
    return kept + core_swap(sent).astype(F32)


def sum_head_biases(v):
    c = lax.axis_index("dp") % 2
    n = lax.axis_size("dp")
    if n != 8:
        z = lax.axis_index("mp")
        zero = jnp.zeros_like(v)
        wide = jnp.where(c == 0, jnp.concatenate([v, zero]), jnp.concatenate([zero, v]))
        total = lax.psum(turn_columns(wide, z), ("dp", "mp"))
        return lax.dynamic_index_in_dim(total, z, 0, False)
    v = v + plane_swap(v, True)
    v = v + plane_swap(v, False)
    total = column_turn(v[0], 0) + column_turn(v[1], 1)
    return total + core_swap(total)


def column_turn(x, k):
    n = lax.axis_size("dp")
    pairs = []
    for d in range(n):
        for z in range(MP):
            pairs.append((d * MP + z, d * MP + (z - k - 2 * (d % 2)) % MP))
    return lax.ppermute(x, ("dp", "mp"), pairs)


def sum_vectors(vectors, columns):
    if lax.axis_size("dp") != 8:
        z = lax.axis_index("mp")
        vectors, columns = lax.psum((vectors, turn_columns(columns, z)), ("dp", "mp"))
        return vectors, lax.dynamic_index_in_dim(columns, z, 0, False)
    n = vectors.shape[0]
    m = columns.shape[1]
    both = jnp.concatenate([vectors, columns.reshape(MP * m, -1)])
    both = both + core_swap(both)
    both = both + plane_swap(both, True)
    both = both + plane_swap(both, False)
    total = both[: n + m]
    for k in range(1, MP):
        at = n + m * (MP - k)
        total = total + column_shift(jnp.concatenate([both[:n], both[at : at + m]]), k)
    return total[:n], total[n:]


def lane_index(shape):
    return lax.broadcasted_iota(jnp.int32, shape, len(shape) - 1)


def half_swap(x):
    lane = lane_index(x.shape)
    return jnp.where(
        lane % HD < HD // 2,
        pltpu.roll(x, LANES - HD // 2, x.ndim - 1),
        pltpu.roll(x, HD // 2, x.ndim - 1),
    )


def norm_parts(r):
    mean = jnp.mean(r, axis=-1, keepdims=True)
    centred = r - mean
    scale = lax.rsqrt(jnp.mean(centred * centred, axis=-1, keepdims=True) + EPSILON)
    return centred * scale, scale


def norm_back(dy, n, scale, gain):
    gdy = dy * gain
    mean_one = jnp.mean(gdy, axis=-1, keepdims=True)
    mean_two = jnp.mean(gdy * n, axis=-1, keepdims=True)
    return (gdy - mean_one - n * mean_two) * scale


def start_pieces(scal, pieces, sems, base, copies):
    started = []
    for i, piece in enumerate(pieces):
        offset = pl.multiple_of(scal[i], 32)
        source, target = copies(piece, offset)
        copy = pltpu.make_async_copy(source, target, sems.at[base + i])
        copy.start()
        started.append(copy)
    return started


def attend_kernel(n_pieces, rows, *refs):
    scal, x_ref, bias_ref, cos_ref, sin_ref, qcode_ref, kcode_ref = refs[:7]
    pieces = refs[7 : 7 + n_pieces]
    q_ref, k_ref, v_ref, own_ref, sib_ref, lse_ref = refs[7 + n_pieces : 13 + n_pieces]
    w_ref, lse_cols, sems = refs[13 + n_pieces :]
    first_z = scal[n_pieces]

    copies = start_pieces(
        scal,
        pieces,
        sems,
        0,
        lambda piece, offset: (
            piece.at[pl.ds(first_z, 2)],
            w_ref.at[:, pl.ds(offset, rows), :],
        ),
    )
    for copy in copies:
        copy.wait()
    keys = x_ref.shape[0]
    queries = keys // 2
    block = queries // 2

    for z in range(2):

        def project(i, _, z=z):
            at = pl.ds(pl.multiple_of(i * block, block), block)
            cos, sin = cos_ref[at, :], sin_ref[at, :]
            p = nn(x_ref[at, :], w_ref[z, :, LANES : 5 * LANES]) + bias_ref[z, :, LANES:]
            low_half = lane_index((block, LANES)) < HD
            mixed = p[:, 0:LANES]
            mixed = mixed * cos + half_swap(mixed) * sin
            pair = p[:, LANES : 2 * LANES]
            pair = pair * cos + half_swap(pair) * sin
            k_ref[z, 0, at, :] = pair.astype(BF16)
            k_ref[z, 1, at, :] = jnp.where(low_half, pltpu.roll(mixed, HD, 1), 0.0).astype(BF16)
            v_ref[z, 0, at, :] = p[:, 2 * LANES : 3 * LANES].astype(BF16)
            v_ref[z, 1, at, :] = jnp.where(low_half, p[:, 3 * LANES :], 0.0).astype(BF16)

            @pl.when(i < 2)
            def _():
                q = nn(x_ref[at, :], w_ref[z, :, 0:LANES]) + bias_ref[z, :, 0:LANES]
                q = q * cos + half_swap(q) * sin
                q_ref[z, 0, at, :] = q.astype(BF16) * BF16(HD**-0.5)
                q_ref[z, 1, at, :] = jnp.where(low_half, mixed, 0.0).astype(BF16) * BF16(HD**-0.5)

            return 0

        lax.fori_loop(0, 4, project, 0)

    lse_cols[...] = jnp.zeros_like(lse_cols)
    qblock = 256

    def one_block(i, _):
        at = pl.ds(pl.multiple_of(i * qblock, qblock), qblock)
        visible = qcode_ref[at, :] == kcode_ref[...]
        low_half = lane_index((qblock, LANES)) < HD
        lane = lane_index((qblock, LANES))
        for z in range(2):
            outs = []
            for h in range(3):
                tile = h // 2
                q = q_ref[z, tile, at, :]
                if h < 2:
                    q = jnp.where(low_half == (h == 0), q, BF16(0))
                s = nt(q, k_ref[z, tile])
                s = jnp.where(visible, s, NEGATIVE)
                m = jnp.max(s, axis=-1, keepdims=True)
                p = jnp.exp(s - m)
                l = jnp.sum(p, axis=-1, keepdims=True)
                o = nn(p.astype(BF16), v_ref[z, tile])
                outs.append(o / l)
                lse_cols[at, :] = jnp.where(lane == 3 * z + h, m + jnp.log(l), lse_cols[at, :])
            single = pltpu.roll(outs[2], HD, 1).astype(BF16)
            pair = jnp.where(low_half, outs[0], outs[1]).astype(BF16)
            mixed_ref[at, pl.ds(z * 256, LANES)] = single
            mixed_ref[at, pl.ds(z * 256 + LANES, LANES)] = pair
        return 0

    mixed_ref = own_ref
    lax.fori_loop(0, queries // qblock, one_block, 0)
    sib_ref[...] = own_ref[pl.ds(block, block), :]
    lse_ref[...] = jnp.transpose(lse_cols[...])[0:8, :]


def vmem():
    return pl.BlockSpec(memory_space=pltpu.VMEM)


def smem():
    return pl.BlockSpec(memory_space=pltpu.SMEM)


def anywhere():
    return pl.BlockSpec(memory_space=pl.ANY)


def params():
    return pltpu.CompilerParams(vmem_limit_bytes=VMEM_LIMIT)


def shape(dims, dtype):
    return jax.ShapeDtypeStruct(dims, dtype)


def piece_rows(pieces):
    return pieces[0].shape[1]


def attend(scal, x_full, bias, tables, pieces):
    cos, sin, qcode, kcode = tables[:4]
    keys, width = x_full.shape
    queries = keys // 2
    return pl.pallas_call(
        partial(attend_kernel, len(pieces), piece_rows(pieces)),
        out_shape=(
            shape((2, 2, queries, LANES), BF16),
            shape((2, 2, keys, LANES), BF16),
            shape((2, 2, keys, LANES), BF16),
            shape((queries, 512), BF16),
            shape((queries // 2, 512), BF16),
            shape((8, queries), F32),
        ),
        in_specs=[smem()] + [vmem()] * 6 + [anywhere()] * len(pieces),
        out_specs=(vmem(),) * 6,
        scratch_shapes=[
            pltpu.VMEM((2, width, 6 * LANES), BF16),
            pltpu.VMEM((queries, LANES), F32),
            pltpu.SemaphoreType.DMA((len(pieces),)),
        ],
        compiler_params=params(),
        cost_estimate=pl.CostEstimate(
            flops=16_000_000_000, bytes_accessed=16_000_000, transcendentals=8_000_000
        ),
        name="attend",
    )(scal, x_full, bias, cos, sin, qcode, kcode, *pieces)


def feed_kernel(n_pieces, rows, layer_last, *refs):
    scal, x_ref, own_ref, sib_ref, vec_ref, bin_ref = refs[:6]
    attn = refs[6 : 6 + n_pieces]
    feed = refs[6 + n_pieces : 6 + 2 * n_pieces]
    at = 6 + 2 * n_pieces
    next_ref, low_ref, r1_ref, r2_ref, e_ref, gp_ref = refs[at : at + 6]
    wo_ref, win_ref, wback_ref, sems = refs[at + 6 :]
    out_copies = start_pieces(
        scal,
        attn,
        sems,
        0,
        lambda piece, offset: (
            piece.at[:, :, pl.ds(4 * LANES, 2 * LANES)],
            wo_ref.at[:, pl.ds(offset, rows), :],
        ),
    )
    width = x_ref.shape[1]
    in_copies = start_pieces(
        scal,
        feed,
        sems,
        n_pieces,
        lambda piece, offset: (
            piece.at[:, :, pl.ds(0, width)],
            win_ref.at[:, pl.ds(offset, rows), :],
        ),
    )
    back_copies = start_pieces(
        scal,
        feed,
        sems,
        2 * n_pieces,
        lambda piece, offset: (
            piece.at[:, :, pl.ds(width, width)],
            wback_ref.at[:, pl.ds(offset, rows), :],
        ),
    )
    first_z = scal[n_pieces]
    for copy in out_copies:
        copy.wait()
    a = jnp.zeros(x_ref.shape, F32)
    for z in range(2):
        a = a + nt(own_ref[:, z * 256 : z * 256 + 256], wo_ref[first_z + z])
        a = a + nt(sib_ref[:, z * 256 : z * 256 + 256], wo_ref[2 - first_z + z])
    r1 = x_ref[...] + a + vec_ref[0:1, :]
    r1_ref[...] = r1
    n1, _ = norm_parts(r1)
    h = n1 * vec_ref[1:2, :] + vec_ref[2:3, :]
    low_ref[...] = h.astype(BF16)
    r2_ref[...] = h + vec_ref[3:4, :]
    for copy in in_copies:
        copy.wait()
    for copy in back_copies:
        copy.wait()

    def one(z, _):
        u = nn(low_ref[...], win_ref[z]) + bin_ref[z]
        cdf = 0.5 * (1.0 + lax.erf(u * (2.0**-0.5)))
        pdf = jnp.exp(u * u * -0.5) * 0.3989422804014327
        e = (u * cdf).astype(BF16)
        e_ref[z] = e
        gp_ref[z] = (cdf + u * pdf).astype(BF16)
        r2_ref[...] += nt(e, wback_ref[z])
        return 0

    lax.fori_loop(0, MP, one, 0)
    n2, _ = norm_parts(r2_ref[...])
    result = n2 * vec_ref[4:5, :] + vec_ref[5:6, :]
    next_ref[...] = result
    low_ref[...] = result.astype(BF16)


def feed_forward(scal, x, own, sib, vec, bias_in, attn, feed):
    rows, width = x.shape
    count = len(attn)
    return pl.pallas_call(
        partial(feed_kernel, count, piece_rows(attn), False),
        out_shape=(
            shape((rows, width), F32),
            shape((rows, width), BF16),
            shape((rows, width), F32),
            shape((rows, width), F32),
            shape((MP, rows, width), BF16),
            shape((MP, rows, width), BF16),
        ),
        in_specs=[smem()] + [vmem()] * 5 + [anywhere()] * (2 * count),
        out_specs=(vmem(),) * 6,
        scratch_shapes=[
            pltpu.VMEM((MP, width, 2 * LANES), BF16),
            pltpu.VMEM((MP, width, width), BF16),
            pltpu.VMEM((MP, width, width), BF16),
            pltpu.SemaphoreType.DMA((3 * count,)),
        ],
        compiler_params=params(),
        cost_estimate=pl.CostEstimate(
            flops=8_000_000_000, bytes_accessed=20_000_000, transcendentals=2_400_000
        ),
        name="feed",
    )(scal, x, own, sib, vec, bias_in, *attn, *feed)


def feed_back_kernel(n_pieces, rows, *refs):
    scal, dy_ref, r1_ref, r2_ref, e_ref, gp_ref, own_ref, sib_ref, vec_ref = refs[:9]
    attn = refs[9 : 9 + n_pieces]
    feed = refs[9 + n_pieces : 9 + 2 * n_pieces]
    at = 9 + 2 * n_pieces
    dr1_ref, dzown_ref, dzsib_ref, dvec_ref, dbin_ref = refs[at : at + 5]
    outs = 2 if n_pieces == 8 else 1
    grads = refs[at + 5 : at + 5 + outs]
    wo_ref, win_ref, wback_ref, df_ref, dft_ref, ht_ref, dw_ref, sems = refs[at + 5 + outs :]
    width = dy_ref.shape[1]
    back_copies = start_pieces(
        scal,
        feed,
        sems,
        2 * n_pieces,
        lambda piece, offset: (
            piece.at[:, :, pl.ds(width, width)],
            wback_ref.at[:, pl.ds(offset, rows), :],
        ),
    )
    in_copies = start_pieces(
        scal,
        feed,
        sems,
        n_pieces,
        lambda piece, offset: (
            piece.at[:, :, pl.ds(0, width)],
            win_ref.at[:, pl.ds(offset, rows), :],
        ),
    )
    out_copies = start_pieces(
        scal,
        attn,
        sems,
        0,
        lambda piece, offset: (
            piece.at[:, :, pl.ds(4 * LANES, 2 * LANES)],
            wo_ref.at[:, pl.ds(offset, rows), :],
        ),
    )
    first_z = scal[n_pieces]
    dy = dy_ref[...]
    n2, scale2 = norm_parts(r2_ref[...])
    dvec_ref[4:5, :] = jnp.sum(dy * n2, axis=0, keepdims=True)
    dvec_ref[5:6, :] = jnp.sum(dy, axis=0, keepdims=True)
    dr2 = norm_back(dy, n2, scale2, vec_ref[4:5, :])
    dvec_ref[3:4, :] = jnp.sum(dr2, axis=0, keepdims=True)
    dr1_ref[...] = dr2
    df = dr2.astype(BF16)
    df_ref[...] = df
    dft_ref[...] = jnp.transpose(df)
    n1, _ = norm_parts(r1_ref[...])
    h = (n1 * vec_ref[1:2, :] + vec_ref[2:3, :]).astype(BF16)
    ht_ref[...] = jnp.transpose(h)
    for copy in back_copies + in_copies:
        copy.wait()

    def one(z, _):
        de = nn(df_ref[...], wback_ref[z])
        du = de * gp_ref[z].astype(F32)
        dbin_ref[z] = jnp.sum(du, axis=0, keepdims=True)
        dub = du.astype(BF16)
        dr1_ref[...] += nt(dub, win_ref[z])
        dw_ref[z, :, 0:width] = nn(ht_ref[...], dub).astype(BF16)
        dw_ref[z, :, width : 2 * width] = nn(dft_ref[...], e_ref[z]).astype(BF16)
        return 0

    lax.fori_loop(0, MP, one, 0)
    dh = dr1_ref[...]
    n1, scale1 = norm_parts(r1_ref[...])
    dvec_ref[1:2, :] = jnp.sum(dh * n1, axis=0, keepdims=True)
    dvec_ref[2:3, :] = jnp.sum(dh, axis=0, keepdims=True)
    dr1 = norm_back(dh, n1, scale1, vec_ref[1:2, :])
    dvec_ref[0:1, :] = jnp.sum(dr1, axis=0, keepdims=True)
    dr1_ref[...] = dr1
    da = dr1.astype(BF16)
    dft_ref[...] = jnp.transpose(da)
    for copy in out_copies:
        copy.wait()
    used = lane_index((da.shape[0], 2 * LANES)) >= HD
    for z in range(2):
        for mixed_ref, dz_ref, z_at in (
            (own_ref, dzown_ref, first_z + z),
            (sib_ref, dzsib_ref, 2 - first_z + z),
        ):
            part = mixed_ref[:, z * 256 : z * 256 + 256]
            dw_ref[z_at, :, 2 * width :] = nn(dft_ref[...], part).astype(BF16)
            dz = nn(da, wo_ref[z_at])
            dz_ref[:, z * 256 : z * 256 + 256] = jnp.where(used, dz, 0.0).astype(BF16)
    flight = []
    for i in range(n_pieces):
        offset = pl.multiple_of(scal[i], 32)
        target = grads[i // 4].at[PIECE_ORDER[i % 4] if n_pieces == 8 else 0]
        copy = pltpu.make_async_copy(dw_ref.at[:, pl.ds(offset, rows), :], target, sems.at[i])
        copy.start()
        flight.append(copy)
    for copy in flight:
        copy.wait()


PIECE_ORDER = (3, 0, 2, 1)


def feed_back(scal, dy, r1, r2, e, gp, own, sib, vec, attn, feed):
    rows, width = dy.shape
    count = len(attn)
    prows = piece_rows(attn)
    lanes = 2 * width + 2 * LANES
    grads = (shape((4, MP, prows, lanes), BF16),) * 2
    if count != 8:
        grads = (shape((1, MP, prows, lanes), BF16),)
    return pl.pallas_call(
        partial(feed_back_kernel, count, prows),
        out_shape=(
            shape((rows, width), F32),
            shape((rows, 512), BF16),
            shape((rows, 512), BF16),
            shape((6, width), F32),
            shape((MP, 1, width), F32),
            *grads,
        ),
        in_specs=[smem()] + [vmem()] * 8 + [anywhere()] * (2 * count),
        out_specs=(vmem(),) * 5 + (anywhere(),) * len(grads),
        scratch_shapes=[
            pltpu.VMEM((MP, width, 2 * LANES), BF16),
            pltpu.VMEM((MP, width, width), BF16),
            pltpu.VMEM((MP, width, width), BF16),
            pltpu.VMEM((rows, width), BF16),
            pltpu.VMEM((width, rows), BF16),
            pltpu.VMEM((width, rows), BF16),
            pltpu.VMEM((MP, width, lanes), BF16),
            pltpu.SemaphoreType.DMA((3 * count,)),
        ],
        compiler_params=params(),
        cost_estimate=pl.CostEstimate(
            flops=16_000_000_000, bytes_accessed=40_000_000, transcendentals=0
        ),
        name="feed_back",
    )(scal, dy, r1, r2, e, gp, own, sib, vec, *attn, *feed)


def attend_back_kernel(n_pieces, rows, *refs):
    (
        scal,
        x_ref,
        cos_ref,
        sin_ref,
        qcode_ref,
        kcode_ref,
        q_ref,
        k_ref,
        v_ref,
        mixed_ref,
        dzown_ref,
        dzsib_ref,
        lse_ref,
    ) = refs[:13]
    pieces = refs[13 : 13 + n_pieces]
    dx_ref, dxs_ref, dbias_ref, parts_ref = refs[13 + n_pieces : 17 + n_pieces]
    (
        w_ref,
        xt_ref,
        dz_ref,
        delta_ref,
        dt_ref,
        dqt_ref,
        pair_ref,
        dw_ref,
        low_ref,
        sums_ref,
        sems,
    ) = refs[17 + n_pieces :]
    first_z = scal[n_pieces]
    copies = start_pieces(
        scal,
        pieces,
        sems,
        0,
        lambda piece, offset: (
            piece.at[pl.ds(first_z, 2)],
            w_ref.at[:, pl.ds(offset, rows), :],
        ),
    )
    keys, width = x_ref.shape
    queries = keys // 2
    block = queries // 2
    for z in range(2):
        for half, source in enumerate((dzown_ref, dzsib_ref)):
            at = pl.ds(half * block, block)
            dz_ref[z, 0, at, :] = source[:, z * 256 + LANES : z * 256 + 256]
            dz_ref[z, 1, at, :] = pltpu.roll(
                source[:, z * 256 : z * 256 + LANES].astype(F32), HD, 1
            ).astype(BF16)
        single = pltpu.roll(mixed_ref[:, z * 256 : z * 256 + LANES].astype(F32), HD, 1)
        pair = mixed_ref[:, z * 256 + LANES : z * 256 + 256].astype(F32)
        prod_one = jnp.transpose(pair * dz_ref[z, 0].astype(F32))
        prod_two = jnp.transpose(single * dz_ref[z, 1].astype(F32))
        delta_ref[3 * z : 3 * z + 1, :] = jnp.sum(prod_one[0:HD], axis=0, keepdims=True)
        delta_ref[3 * z + 1 : 3 * z + 2, :] = jnp.sum(prod_one[HD:], axis=0, keepdims=True)
        delta_ref[3 * z + 2 : 3 * z + 3, :] = jnp.sum(prod_two[0:HD], axis=0, keepdims=True)

    kblock = 256
    low_q = lane_index((queries, LANES)) < HD
    low_k = lane_index((kblock, LANES)) < HD
    for z in range(2):
        for h in range(3):
            tile = h // 2
            q = q_ref[z, tile]
            dz = dz_ref[z, tile]
            if h < 2:
                keep = low_q == (h == 0)
                q = jnp.where(keep, q, BF16(0))
                dz = jnp.where(keep, dz, BF16(0))
            pair_ref[0] = q
            pair_ref[1] = dz
            lse = lse_ref[3 * z + h : 3 * z + h + 1, :]
            delta = delta_ref[3 * z + h : 3 * z + h + 1, :]
            if h != 1:
                dqt_ref[...] = jnp.zeros_like(dqt_ref)

            def one_block(i, _, z=z, h=h, tile=tile, lse=lse, delta=delta):
                at = pl.ds(pl.multiple_of(i * kblock, kblock), kblock)
                kb = k_ref[z, tile, at, :]
                vb = v_ref[z, tile, at, :]
                if h < 2:
                    kb_own = jnp.where(low_k == (h == 0), kb, BF16(0))
                else:
                    kb_own = kb
                visible = kcode_ref[at, :] == qcode_ref[...]
                s = nt(kb, pair_ref[0])
                s = jnp.where(visible, s, NEGATIVE)
                p = jnp.exp(s - lse)
                dp = nt(vb, pair_ref[1])
                ds = (p * (dp - delta)).astype(BF16)
                dv = nn(p.astype(BF16), pair_ref[1])
                dk = nn(ds, pair_ref[0])
                dqt_ref[...] += nn(jnp.transpose(kb_own), ds)
                if h == 1:
                    dt_ref[2, at, :] += dk
                    dt_ref[3, at, :] += dv
                elif h == 0:
                    dt_ref[2, at, :] = dk
                    dt_ref[3, at, :] = dv
                else:
                    dt_ref[1, at, :] = pltpu.roll(dk, HD, 1)
                    dt_ref[4, at, :] = dv
                return 0

            lax.fori_loop(0, keys // kblock, one_block, 0)
            if h >= 1:
                dq = jnp.transpose(dqt_ref[...]) * HD**-0.5
                if h == 1:
                    dt_ref[0, 0:queries, :] = dq
                else:
                    dt_ref[1, 0:queries, :] += dq

        if z == 0:
            xt_ref[...] = jnp.transpose(x_ref[...])
            for copy in copies:
                copy.wait()
        for tile in range(5):
            count = queries if tile == 0 else keys
            t = dt_ref[tile, 0:count, :]
            if tile < 3:
                t = t * cos_ref[0:count, :] - half_swap(t) * sin_ref[0:count, :]
            dbias_ref[z, :, tile * LANES : (tile + 1) * LANES] = jnp.sum(t, axis=0, keepdims=True)
            low_ref[0:count, tile * LANES : (tile + 1) * LANES] = t.astype(BF16)
        dw_ref[z, :, 0:LANES] = nn(
            xt_ref[:, 0:queries], low_ref[0:queries, 0:LANES]
        ).astype(BF16)
        dw_ref[z, :, LANES:] = nn(xt_ref[...], low_ref[:, LANES:]).astype(BF16)
        for i in range(4):
            at = pl.ds(i * block, block)
            part = nt(low_ref[at, LANES:], w_ref[z, :, LANES : 5 * LANES])
            if i < 2:
                part = part + nt(low_ref[at, 0:LANES], w_ref[z, :, 0:LANES])
            if z == 0:
                sums_ref[i] = part
            else:
                target = dx_ref if i % 2 == 0 else dxs_ref
                target[i // 2] = (sums_ref[i] + part).astype(BF16)

    flight = []
    for i in range(min(n_pieces, 4)):
        offset = pl.multiple_of(scal[n_pieces + 1 + i], 32)
        copy = pltpu.make_async_copy(
            dw_ref.at[:, pl.ds(offset, parts_ref.shape[2]), :],
            parts_ref.at[PIECE_ORDER[i] if n_pieces == 8 else 0],
            sems.at[i],
        )
        copy.start()
        flight.append(copy)
    for copy in flight:
        copy.wait()


def attend_back(scal, x_full, tables, saved, mixed, dz_own, dz_sib, pieces):
    cos, sin, _, _, qcode, kcode = tables
    q, k, v, lse = saved
    keys, width = x_full.shape
    queries = keys // 2
    block = queries // 2
    count = len(pieces)
    parts = (4, 2, 2 * piece_rows(pieces), 5 * LANES)
    if count != 8:
        parts = (1, 2, piece_rows(pieces), 5 * LANES)
    return pl.pallas_call(
        partial(attend_back_kernel, count, piece_rows(pieces)),
        out_shape=(
            shape((2, block, width), BF16),
            shape((2, block, width), BF16),
            shape((2, 1, 5 * LANES), F32),
            shape(parts, BF16),
        ),
        in_specs=[smem()] + [vmem()] * 12 + [anywhere()] * count,
        out_specs=(vmem(),) * 3 + (anywhere(),),
        scratch_shapes=[
            pltpu.VMEM((2, width, 6 * LANES), BF16),
            pltpu.VMEM((width, keys), BF16),
            pltpu.VMEM((2, 2, queries, LANES), BF16),
            pltpu.VMEM((8, queries), F32),
            pltpu.VMEM((5, keys, LANES), F32),
            pltpu.VMEM((LANES, queries), F32),
            pltpu.VMEM((2, queries, LANES), BF16),
            pltpu.VMEM((2, width, 5 * LANES), BF16),
            pltpu.VMEM((keys, 5 * LANES), BF16),
            pltpu.VMEM((4, block, width), F32),
            pltpu.SemaphoreType.DMA((count,)),
        ],
        compiler_params=params(),
        cost_estimate=pl.CostEstimate(
            flops=40_000_000_000, bytes_accessed=20_000_000, transcendentals=8_000_000
        ),
        name="attend_back",
    )(scal, x_full, cos, sin, qcode, kcode, q, k, v, mixed, dz_own, dz_sib, lse, *pieces)


def head_tiles(q, k, v, o):
    return jnp.concatenate(
        [
            q[..., :LANES],
            q[..., LANES:],
            k[..., LANES:],
            k[..., :LANES],
            v[..., :LANES],
            v[..., LANES:],
            o[..., LANES:],
            o[..., :LANES],
        ],
        axis=-1,
    )


def head_columns(t):
    q = jnp.concatenate([t[..., 0:128], t[..., 128:192]], axis=-1)
    k = jnp.concatenate([t[..., 256:384], t[..., 192:256]], axis=-1)
    v = jnp.concatenate([t[..., 384:512], t[..., 512:576]], axis=-1)
    return q, k, v


def make_tables(positions, bucket, lengths):
    slot = LEN_MAX // (3 - bucket)
    sequence = positions // slot
    place = positions - sequence * slot
    limit = jnp.sum(
        jnp.where(sequence[:, None] == jnp.arange(3)[None, :], lengths[None, :], 0), axis=1
    )
    lane = jnp.arange(LANES) % HD
    frequency = 10000.0 ** (-2.0 * (lane % (HD // 2)).astype(F32) / HD)
    angles = place.astype(F32)[:, None] * frequency[None, :]
    sign = jnp.where(lane < HD // 2, -1.0, 1.0)
    cos = jnp.cos(angles)
    sin = jnp.sin(angles) * sign[None, :]
    kcode = jnp.where(place < limit, sequence, -1).astype(F32)
    qcode = sequence[: positions.shape[0] // 2].astype(F32)
    return cos, sin, qcode[:, None], kcode[None, :], qcode[None, :], kcode[:, None]


def per_device(
    tokens, w_qkv, b_qkv, w_out, vectors, w_in, b_in, w_back, cotangent, lengths, buckets
):
    layers = w_qkv.shape[0]
    rows, width = tokens.shape
    d = lax.axis_index("dp")
    z = lax.axis_index("mp")
    g, c = d // 2, d % 2

    gathered = []
    for layer_at in range(layers):
        low = w_qkv[layer_at].astype(BF16)
        attn = head_tiles(low[0], low[1], low[2], w_out[layer_at].astype(BF16).T)
        feed = jnp.concatenate(
            [w_in[layer_at].astype(BF16), w_back[layer_at].astype(BF16).T], axis=-1
        )
        gathered.append((gather_bundle(attn), gather_bundle(feed)))
    piece_height = w_qkv.shape[2]
    offsets = row_offsets(g, c, piece_height)
    first = jnp.where(c == 0, 1, 2)
    spans = [(g ^ hop) * 2 * piece_height for hop in (0, first, 3 - first, 3)]
    if len(offsets) == 1:
        spans = [jnp.int32(0)] * 4
    scal = jnp.stack(offsets + [2 * c] + spans).astype(jnp.int32)

    zero = jnp.zeros((layers, LANES // 2), F32)
    v_bias = b_qkv[:, 2]
    bias_tiles = jnp.concatenate(
        [
            b_qkv[:, 0],
            b_qkv[:, 1, LANES:],
            b_qkv[:, 1, :LANES],
            v_bias,
            zero,
        ],
        axis=-1,
    )
    small = gather_small(jnp.concatenate([bias_tiles, b_in], axis=-1))
    bias_all = small[:, :, : 5 * LANES]
    bias_in_all = small[:, :, 5 * LANES :]

    meta = jnp.concatenate([buckets, lengths[0]])
    other_meta = core_swap(meta)
    half = z // 2
    meta = jnp.where(half == c, meta, other_meta)
    place = z % 2
    quarters = [2 * c + place, 2 * (1 - c) + place, 2 * c + 1 - place, 2 * (1 - c) + 1 - place]
    positions = jnp.concatenate([q * rows + jnp.arange(rows, dtype=jnp.int32) for q in quarters])
    tables = make_tables(positions, meta[0], meta[1:])

    tokens = relayout(tokens)
    low = tokens
    stream = tokens.astype(F32)
    states = []
    for layer_at in range(layers):
        attn, feed = gathered[layer_at]
        two = jnp.stack([low, pair_swap(low)])
        others = core_swap(two)
        x_full = jnp.concatenate([two[0], others[0], two[1], others[1]], axis=0)
        bias = lax.dynamic_slice_in_dim(bias_all[:, layer_at], 2 * c, 2, 0)[:, None, :]
        q, k, v, mixed, mixed_sib, lse = attend(scal, x_full, bias, tables, attn)
        others_mixed = core_swap(mixed_sib)
        own_mixed = mixed[:rows]
        stream, low, r1, r2, e, gp = feed_forward(
            scal,
            stream,
            own_mixed,
            others_mixed,
            vectors[layer_at],
            bias_in_all[:, layer_at][:, None, :],
            attn,
            feed,
        )
        states.append((x_full, (q, k, v, lse), mixed, own_mixed, others_mixed, r1, r2, e, gp))
    result = relayout(low)

    gradient = relayout(cotangent).astype(F32)
    masters = []
    vector_grads = []
    in_biases = []
    head_biases = []
    for layer_at in reversed(range(layers)):
        attn, feed = gathered[layer_at]
        x_full, saved, mixed, own_mixed, others_mixed, r1, r2, e, gp = states[layer_at]
        back = feed_back(
            scal, gradient, r1, r2, e, gp, own_mixed, others_mixed, vectors[layer_at], attn, feed
        )
        dr1, dz_own, dz_sib, dvec, dbin = back[:5]
        dz_others = core_swap(dz_sib)
        feed_grad = reduce_all(back[5], back[-1])
        dx, dx_sib, dbias, parts = attend_back(
            scal, x_full, tables, saved, mixed, dz_own, dz_others, attn
        )
        got = dx.astype(F32) + core_swap(dx_sib).astype(F32)
        gradient = dr1 + got[0] + pair_swap(got[1].astype(BF16)).astype(F32)
        head_grad = reduce_heads(parts)
        masters.insert(0, (feed_grad, head_grad))
        vector_grads.insert(0, dvec)
        in_biases.insert(0, dbin[:, 0])
        head_biases.insert(0, sum_head_biases(dbias[:, 0]))
    grad_tokens = relayout(gradient.astype(BF16)).astype(F32)

    layers_of = jnp.stack(in_biases, axis=1)
    grad_vectors, grad_b_in = sum_vectors(jnp.concatenate(vector_grads), layers_of)
    grad_vectors = grad_vectors.reshape(vectors.shape)
    grad_b_qkv = jnp.stack([jnp.stack(head_columns(b)) for b in head_biases])

    grad_qkv = jnp.stack([jnp.stack(head_columns(m[1])) for m in masters])
    grad_in = jnp.stack([m[0][:, :width] for m in masters])
    grad_back = jnp.stack([m[0][:, width : 2 * width].T for m in masters])
    grad_out = jnp.stack(
        [
            jnp.concatenate(
                [m[0][:, 2 * width + LANES :], m[0][:, 2 * width + HD : 2 * width + LANES]], axis=-1
            ).T
            for m in masters
        ]
    )
    return (
        result,
        grad_tokens,
        grad_qkv,
        grad_b_qkv,
        grad_out,
        grad_vectors,
        grad_in,
        grad_b_in,
        grad_back,
    )


def solution(mesh):
    return jax.shard_map(
        per_device,
        mesh=mesh,
        in_specs=(
            P(("dp", "mp"), None),
            P(None, None, "dp", "mp"),
            P(None, None, "mp"),
            P(None, "mp", "dp"),
            P(),
            P(None, "dp", "mp"),
            P(None, "mp"),
            P(None, "mp", "dp"),
            P(("dp", "mp"), None),
            P("dp", None),
            P("dp"),
        ),
        out_specs=(
            P(("dp", "mp"), None),
            P(("dp", "mp"), None),
            P(None, None, "dp", "mp"),
            P(None, None, "mp"),
            P(None, "mp", "dp"),
            P(),
            P(None, "dp", "mp"),
            P(None, "mp"),
            P(None, "mp", "dp"),
        ),
        check_vma=False,
    )
```

time: 1850 us -> 705 us (0.38)
  waiting for transfers between devices: 1040 us -> 284 us
  matrix products: 400 us -> 0 us
  Pallas kernels: 0 us -> 211 us
  local copies, waits for them, and re-layouts: 169 us -> 27 us
  blocking collectives: 114 us -> 0 us
  starting transfers between devices: 2.58 us -> 111 us
  loops' own time: 19.6 us -> 0 us
    reduce_scatter x10 -> x0, waiting for transfers between devices: 708 us -> none  [the longest x2 170 us: forward_layer(): lax.psum_scatter(jnp.dot(active, back_w, preferred_element_type=jnp.float...]
    dot_general x63 -> x0, matrix products: 389 us -> none  [the longest x6 94.1 us: one_block(): jnp.einsum('hqk,qhd->khd', grad_scores, query_block, preferred_element_ty...]
    all_gather x12 -> x0, waiting for transfers between devices: 319 us -> none  [the longest x2 102 us: backward_layer(): lax.all_gather(grad_second.astype(jnp.bfloat16), 'mp', axis=0, tiled=True)]
    ppermute x0 -> x98, waiting for transfers between devices: none -> 284 us  [the longest x26 148 us: plane_swap(): return lax.ppermute(x, 'dp', [(i, i ^ hops[i % 2]) for i in range(n)])]
    pallas_call x0 -> x8, Pallas kernels: none -> 211 us  [the longest x2 78.7 us: attend_back(): pl.pallas_call(partial(attend_back_kernel, count, piece_rows(pieces)), ou...]
    ppermute x0 -> x98, starting transfers between devices: none -> 111 us  [the longest x24 53.1 us: column_shift(): return lax.ppermute(x, 'mp', [(i, (i + k) % MP) for i in range(MP)])]
    psum x2 -> x0, blocking collectives: 63.8 us -> none  [the longest x1 40.4 us: reduce_grads(): vector_sums = lax.psum(vector_grads, ('dp', 'mp'))]
    dynamic_update_slice x12 -> x0, local copies, waits for them, and re-layouts: 54.1 us -> none  [attend_back(): lax.scan(one_block, (zero_rows, zero_rows), jnp.arange(blocks, dtype=jnp....]
  transfers between devices with their start and end apart: 27 -> 98, of which waited for: 20 -> 37; matrix products, arithmetic and copies ran while one was open for 17% -> 10% of each run, Pallas kernels for 0% -> 19%
where the time goes in v1:
time: 705 us; the launch traced here: 695 us
  waiting for transfers between devices  284 us (40%)
  Pallas kernels  211 us (30%)
  starting transfers between devices  111 us (16%)
  other arithmetic  59.4 us (8%)
  local copies, waits for them, and re-layouts  27 us (4%)
    ppermute x26, waiting for transfers between devices, plane_swap(): return lax.ppermute(x, 'dp', [(i, i ^ hops[i % 2]) for i in range(n)])  148 us
    ppermute x24, waiting for transfers between devices, column_shift(): return lax.ppermute(x, 'mp', [(i, (i + k) % MP) for i in range(MP)])  97.7 us
    pallas_call x2, Pallas kernels, attend_back(): pl.pallas_call(partial(attend_back_kernel, count, piece_rows(pieces)), ou...  78.7 us
    ppermute x24, starting transfers between devices, column_shift(): return lax.ppermute(x, 'mp', [(i, (i + k) % MP) for i in range(MP)])  53.1 us
    pallas_call x2, Pallas kernels, attend(): pl.pallas_call(partial(attend_kernel, len(pieces), piece_rows(pieces)), o...  52.1 us
    pallas_call x2, Pallas kernels, feed_back(): pl.pallas_call(partial(feed_back_kernel, count, prows), out_shape=(shape(...  50.6 us
    ppermute x8, waiting for transfers between devices, column_turn(): return lax.ppermute(x, ('dp', 'mp'), pairs)  34.6 us
    ppermute x26, starting transfers between devices, plane_swap(): return lax.ppermute(x, 'dp', [(i, i ^ hops[i % 2]) for i in range(n)])  30.2 us
  transfers between devices with their start and end apart: 98, of which 37 were waited for; matrix products, arithmetic and copies ran while one was open for 10% of the time, Pallas kernels for 19%

profile of v1, /device:TPU:0, one launch (start us, length us, event | category | flops | bytes accessed | tf_op | source)
XLA Modules:
  0.0 695.3 jit_solution(4390462415091769459)
XLA Ops:
  2.7 5.1 collective-permute-start.20
  18.3 25.2 %collective-permute-done.19 = bf16[96,1536]{1,0:T(8,128)(2,1)S(1)} collective-permute-done((bf16[96,1536]{1,0:T(8,128)(2,1)S(1)}, bf16[96,1536]{1,0:T(8,128)(2,1)S(1)}, u32[]{:S(2)}, u32[]{:S(2)}) %collective-permute-start.19) | collective-permute-done | bytes 294944 | tf_op jit(solution)/shard_map/ppermute | solution.py:41
  51.8 11.4 %collective-permute-start.5 = (f32[2,1408]{1,0:T(2,128)S(1)}, f32[2,1408]{1,0:T(2,128)S(1)}, u32[]{:S(2)}, u32[]{:S(2)}) collective-permute-start(f32[2,1408]{1,0:T(2,128)S(1)} %concatenate.170), channel_id=1, source_target_pairs={{0,3},{1,0},{2,1},{3,2},{4,7},{5,4},{6,5},{7,6},{8,11},{9,8},{10,9... | collective-permute-start | bytes 33800 | tf_op jit(solution)/shard_map/ppermute | solution.py:41
  79.1 5.8 collective-permute-done.11.refs_9_.refs_8_.refs_11_.refs_15_
  95.2 8.8 %collective-permute-done.22.refs_16_.refs_19_ = bf16[4,96,1536]{2,1,0:T(8,128)(2,1)} collective-permute-done((bf16[4,96,1536]{2,1,0:T(8,128)(2,1)S(1)}, bf16[4,96,1536]{2,1,0:T(8,128)(2,1)}, u32[]{:S(2)}, u32[]{:S(2)}) %collective-permute-start.22) | collective-permute-done | bytes 1179680 | tf_op jit(solution)/shard_map/ppermute | solution.py:37
  104.8 11.8 %collective-permute-done.23.refs_17_.refs_20_ = bf16[4,96,1536]{2,1,0:T(8,128)(2,1)} collective-permute-done((bf16[4,96,1536]{2,1,0:T(8,128)(2,1)}, bf16[4,96,1536]{2,1,0:T(8,128)(2,1)}, u32[]{:S(2)}, u32[]{:S(2)}) %collective-permute-start.23) | collective-permute-done | bytes 1179680 | tf_op jit(solution)/shard_map/ppermute | solution.py:37
  118.0 25.9 %attend.2 = (bf16[2,2,768,128]{3,2,1,0:T(8,128)(2,1)}, bf16[2,2,1536,128]{3,2,1,0:T(8,128)(2,1)}, bf16[2,2,1536,128]{3,2,1,0:T(8,128)(2,1)}, bf16[768,512]{1,0:T...) custom-call(s32[13]{0:T(128)} %stack.256.refs_0_, bf16[1536,768]{1,0:T(8,128)(2,1)} %pad_maximum_fusion.2.refs_1_, ...), custom_call_target="tpu_custom_call" | custom-call | flops 16000000000 | bytes 16000000 | tf_op jit(solution)/shard_map/attend/pallas_call | solution.py:331
  147.8 6.8 collective-permute-start.43
  159.3 14.8 %feed.2 = (f32[384,768]{1,0:T(8,128)}, bf16[384,768]{1,0:T(8,128)(2,1)}, f32[384,768]{1,0:T(8,128)}, f32[384,768]{1,0:T(8,128)}, bf16[4,384,768]{2,1,0:T(8,128)(2,1)}, /*index=5*/bf16[4,384,768]{2,1,0:T(8,128)(2,1)}) custom-call(s32[13]{0:T(128)} %stack.256.refs_0_, f32[384,768]{1,0:T(8,128)} %convert_element_type.318.refs_1_, ...), custom_call_target="tpu_custom_call" | custom-call | flops 8000000000 | bytes 20000000 | tf_op jit(solution)/shard_map/feed/pallas_call | solution.py:432
  174.3 8.4 %collective-permute-done.42 = bf16[96,1536]{1,0:T(8,128)(2,1)S(1)} collective-permute-done((bf16[96,1536]{1,0:T(8,128)(2,1)S(1)}, bf16[96,1536]{1,0:T(8,128)(2,1)S(1)}, u32[]{:S(2)}, u32[]{:S(2)}) %collective-permute-start.42) | collective-permute-done | bytes 294944 | tf_op jit(solution)/shard_map/ppermute | solution.py:41
  188.4 16.3 %collective-permute-done.32 = bf16[96,768]{1,0:T(8,128)(2,1)S(1)} collective-permute-done((bf16[96,768]{1,0:T(8,128)(2,1)S(1)}, bf16[96,768]{1,0:T(8,128)(2,1)S(1)}, u32[]{:S(2)}, u32[]{:S(2)}) %collective-permute-start.32) | collective-permute-done | bytes 147488 | tf_op jit(solution)/shard_map/ppermute | solution.py:41
  209.9 10.1 %collective-permute-done.33.refs_8_.refs_7_.refs_10_.refs_14_ = bf16[4,96,768]{2,1,0:T(8,128)(2,1)} collective-permute-done((bf16[4,96,768]{2,1,0:T(8,128)(2,1)}, bf16[4,96,768]{2,1,0:T(8,128)(2,1)}, u32[]{:S(2)}, u32[]{:S(2)}) %collective-permute-start.33) | collective-permute-done | bytes 589856 | tf_op jit(solution)/shard_map/ppermute | solution.py:37
  243.3 12.1 %collective-permute-done.46.refs_17_.refs_20_ = bf16[4,96,1536]{2,1,0:T(8,128)(2,1)} collective-permute-done((bf16[4,96,1536]{2,1,0:T(8,128)(2,1)}, bf16[4,96,1536]{2,1,0:T(8,128)(2,1)}, u32[]{:S(2)}, u32[]{:S(2)}) %collective-permute-start.46) | collective-permute-done | bytes 1179680 | tf_op jit(solution)/shard_map/ppermute | solution.py:37
  255.5 26.2 %attend.3 = (bf16[2,2,768,128]{3,2,1,0:T(8,128)(2,1)}, bf16[2,2,1536,128]{3,2,1,0:T(8,128)(2,1)}, bf16[2,2,1536,128]{3,2,1,0:T(8,128)(2,1)}, bf16[768,512]{1,0:T...) custom-call(s32[13]{0:T(128)} %stack.256.refs_0_, bf16[1536,768]{1,0:T(8,128)(2,1)} %pad_maximum_fusion.3.refs_1_, ...), custom_call_target="tpu_custom_call" | custom-call | flops 16000000000 | bytes 16000000 | tf_op jit(solution)/shard_map/attend/pallas_call | solution.py:331
  283.0 8.4 %broadcast_multiply_fusion = (s32[1536,1]{1,0:T(8,128)S(1)}, s32[1536,1]{1,0:T(8,128)}) fusion(s32[]{:T(128)S(6)} %select_n.147, s32[1536,1]{1,0:T(8,128)S(1)} %copy.81, s32[1536,1]{1,0:T(8,128)S(1)} %copy.82, pred[1536,1]{1,0:T(8,128)(4,1)S(1)} %copy-done.11, s32[1536,1]{1,0:T(8,128)S(1)} %copy.77), kind=kLoop, calls=%fused_computation.66 | loop fusion | flops 7680 | bytes 32260 | tf_op jit(solution)/shard_map/mul | solution.py:821
  294.4 15.0 %feed.3 = (f32[384,768]{1,0:T(8,128)}, bf16[384,768]{1,0:T(8,128)(2,1)}, f32[384,768]{1,0:T(8,128)}, f32[384,768]{1,0:T(8,128)}, bf16[4,384,768]{2,1,0:T(8,128)(2,1)}, /*index=5*/bf16[4,384,768]{2,1,0:T(8,128)(2,1)}) custom-call(s32[13]{0:T(128)} %stack.256.refs_0_, f32[384,768]{1,0:T(8,128)} %get-tuple-element.56.refs_1_, ...), custom_call_target="tpu_custom_call" | custom-call | flops 8000000000 | bytes 20000000 | tf_op jit(solution)/shard_map/feed/pallas_call | solution.py:432
  309.3 25.3 %feed_back.2 = (f32[384,768]{1,0:T(8,128)}, bf16[384,512]{1,0:T(8,128)(2,1)}, bf16[384,512]{1,0:T(8,128)(2,1)}, f32[6,768]{1,0:T(8,128)}, f32[4,1,768]{2,1,0:T(1...) custom-call(s32[13]{0:T(128)} %stack.256.refs_0_, f32[384,768]{1,0:T(8,128)} %convert_element_type.329.refs_1_, ...), custom_call_target="tpu_custom_call" | custom-call | flops 16000000000 | bytes 40000000 | tf_op jit(solution)/shard_map/feed_back/pallas_call | solution.py:569
  337.4 39.2 %attend_back.2 = (bf16[2,384,768]{2,1,0:T(8,128)(2,1)}, bf16[2,384,768]{2,1,0:T(8,128)(2,1)}, f32[2,1,640]{2,1,0:T(1,128)}, bf16[4,2,192,640]{3,2,1,0:T(8,128)(2,1)}) custom-call(s32[13]{0:T(128)} %stack.256.refs_0_, bf16[1536,768]{1,0:T(8,128)(2,1)} %pad_maximum_fusion.3.refs_1_, f32[1536,128]{1,0:T(8,128)} %get-tuple-element.207.refs_3_.refs_2_, ...), custom_call_target="tpu_custom_call" | custom-call | flops 40000000000 | bytes 20000000 | tf_op jit(solution)/shard_map/attend_back/pallas_call | solution.py:764
  382.9 10.7 %collective-permute-done.75 = f32[2,640]{1,0:T(2,128)S(1)} collective-permute-done((f32[2,640]{1,0:T(2,128)S(1)}, f32[2,640]{1,0:T(2,128)S(1)}, u32[]{:S(2)}, u32[]{:S(2)}) %collective-permute-start.75) | collective-permute-done | bytes 5152 | tf_op jit(solution)/shard_map/ppermute | solution.py:37
  418.0 20.7 %collective-permute-done.68 = bf16[192,640]{1,0:T(8,128)(2,1)S(1)} collective-permute-done((bf16[192,640]{1,0:T(8,128)(2,1)S(1)}, bf16[192,640]{1,0:T(8,128)(2,1)S(1)}, u32[]{:S(2)}, u32[]{:S(2)}) %collective-permute-start.68) | collective-permute-done | bytes 245792 | tf_op jit(solution)/shard_map/ppermute | solution.py:159
  440.0 25.3 %feed_back.3 = (f32[384,768]{1,0:T(8,128)}, bf16[384,512]{1,0:T(8,128)(2,1)}, bf16[384,512]{1,0:T(8,128)(2,1)}, f32[6,768]{1,0:T(8,128)}, f32[4,1,768]{2,1,0:T(1...) custom-call(s32[13]{0:T(128)} %stack.256.refs_0_, f32[384,768]{1,0:T(8,128)} %fusion.8.refs_1_, ...), custom_call_target="tpu_custom_call" | custom-call | flops 16000000000 | bytes 40000000 | tf_op jit(solution)/shard_map/feed_back/pallas_call | solution.py:569
  475.7 39.5 %attend_back.3 = (bf16[2,384,768]{2,1,0:T(8,128)(2,1)}, bf16[2,384,768]{2,1,0:T(8,128)(2,1)}, f32[2,1,640]{2,1,0:T(1,128)}, bf16[4,2,192,640]{3,2,1,0:T(8,128)(2,1)}) custom-call(s32[13]{0:T(128)} %stack.256.refs_0_, bf16[1536,768]{1,0:T(8,128)(2,1)} %pad_maximum_fusion.2.refs_1_, f32[1536,128]{1,0:T(8,128)} %get-tuple-element.207.refs_3_.refs_2_, ...), custom_call_target="tpu_custom_call" | custom-call | flops 40000000000 | bytes 20000000 | tf_op jit(solution)/shard_map/attend_back/pallas_call | solution.py:764
  543.3 7.6 %collective-permute-done.60 = bf16[2,2,192,640]{3,2,1,0:T(8,128)(2,1)S(1)} collective-permute-done((bf16[2,2,192,640]{3,2,1,0:T(8,128)(2,1)S(1)}, bf16[2,2,192,640]{3,2,1,0:T(8,128)(2,1)S(1)}, u32[]{:S(2)}, u32[]{:S(2)}) %collective-permute-start.60) | collective-permute-done | bytes 983072 | tf_op jit(solution)/shard_map/ppermute | solution.py:37
  555.6 9.7 %collective-permute-done.61 = bf16[2,192,640]{2,1,0:T(8,128)(2,1)S(1)} collective-permute-done((bf16[2,192,640]{2,1,0:T(8,128)(2,1)S(1)}, bf16[2,192,640]{2,1,0:T(8,128)(2,1)S(1)}, u32[]{:S(2)}, u32[]{:S(2)}) %collective-permute-start.61) | collective-permute-done | bytes 491552 | tf_op jit(solution)/shard_map/ppermute | solution.py:37
  568.4 10.3 %collective-permute-done.63 = bf16[192,640]{1,0:T(8,128)(2,1)S(1)} collective-permute-done((bf16[192,640]{1,0:T(8,128)(2,1)S(1)}, bf16[192,640]{1,0:T(8,128)(2,1)S(1)}, u32[]{:S(2)}, u32[]{:S(2)}) %collective-permute-start.63) | collective-permute-done | bytes 245792 | tf_op jit(solution)/shard_map/ppermute | solution.py:159
  578.9 6.8 collective-permute-done.87
  590.7 39.2 %collective-permute-done.81 = bf16[2,4,96,1792]{3,2,1,0:T(8,128)(2,1)S(1)} collective-permute-done((bf16[2,4,96,1792]{3,2,1,0:T(8,128)(2,1)S(1)}, bf16[2,4,96,1792]{3,2,1,0:T(8,128)(2,1)S(1)}, u32[]{:S(2)}, u32[]{:S(2)}) %collective-permute-start.81) | collective-permute-done | bytes 2752544 | tf_op jit(solution)/shard_map/ppermute | solution.py:37
  640.3 7.1 %collective-permute-done.91 = bf16[96,1792]{1,0:T(8,128)(2,1)S(1)} collective-permute-done((bf16[96,1792]{1,0:T(8,128)(2,1)S(1)}, bf16[96,1792]{1,0:T(8,128)(2,1)S(1)}, u32[]{:S(2)}, u32[]{:S(2)}) %collective-permute-start.91) | collective-permute-done | bytes 344096 | tf_op jit(solution)/shard_map/ppermute | solution.py:41
  647.4 13.2 %collective-permute-done.90 = bf16[96,1792]{1,0:T(8,128)(2,1)S(1)} collective-permute-done((bf16[96,1792]{1,0:T(8,128)(2,1)S(1)}, bf16[96,1792]{1,0:T(8,128)(2,1)S(1)}, u32[]{:S(2)}, u32[]{:S(2)}) %collective-permute-start.90) | collective-permute-done | bytes 344096 | tf_op jit(solution)/shard_map/ppermute | solution.py:41
  663.0 7.0 %collective-permute-start.85 = (bf16[96,1792]{1,0:T(8,128)(2,1)S(1)}, bf16[96,1792]{1,0:T(8,128)(2,1)S(1)}, u32[]{:S(2)}, u32[]{:S(2)}) collective-permute-start(bf16[96,1792]{1,0:T(8,128)(2,1)S(1)} %get-tuple-element.157), channel_id=1, source_target_pairs={{0,1},{1,2},{2,3},{3,0},{4,5},{5,6},{6,7},{7,4},{8,9},{9,10},{10,1... | collective-permute-start | bytes 1032200 | tf_op jit(solution)/shard_map/ppermute | solution.py:41
  672.5 6.0 collective-permute-done.85
  678.5 12.2 %collective-permute-done.84 = bf16[96,1792]{1,0:T(8,128)(2,1)S(1)} collective-permute-done((bf16[96,1792]{1,0:T(8,128)(2,1)S(1)}, bf16[96,1792]{1,0:T(8,128)(2,1)S(1)}, u32[]{:S(2)}, u32[]{:S(2)}) %collective-permute-start.84) | collective-permute-done | bytes 344096 | tf_op jit(solution)/shard_map/ppermute | solution.py:41
  (479 shorter events, 200.3 us)
Async XLA Ops:
  7.8 35.7 %collective-permute-start.19 = (bf16[96,1536]{1,0:T(8,128)(2,1)S(1)}, bf16[96,1536]{1,0:T(8,128)(2,1)S(1)}, u32[]{:S(2)}, u32[]{:S(2)}) collective-permute-start(bf16[96,1536]{1,0:T(8,128)(2,1)S(1)} %get-tuple-element.187), channel_id=1, source_target_pairs={{0,2},{1,3},{2,0},{3,1},{4,6},{5,7},{6,4},{7,5},{8,10},{9,11},{10,... | collective-permute-start | bytes 884744 | tf_op jit(solution)/shard_map/ppermute | solution.py:41
  7.8 35.7 %collective-permute-start.18 = (bf16[96,1536]{1,0:T(8,128)(2,1)S(1)}, bf16[96,1536]{1,0:T(8,128)(2,1)S(1)}, u32[]{:S(2)}, u32[]{:S(2)}) collective-permute-start(bf16[96,1536]{1,0:T(8,128)(2,1)S(1)} %get-tuple-element.187), channel_id=1, source_target_pairs={{0,1},{1,2},{2,3},{3,0},{4,5},{5,6},{6,7},{7,4},{8,9},{9,10},{10,1... | collective-permute-start | bytes 884744 | tf_op jit(solution)/shard_map/ppermute | solution.py:41
  8.8 34.9 %collective-permute-start = (bf16[384,768]{1,0:T(8,128)(2,1)}, bf16[384,768]{1,0:T(8,128)(2,1)S(1)}, u32[]{:S(2)}, u32[]{:S(2)}) collective-permute-start(bf16[384,768]{1,0:T(8,128)(2,1)} %param.11), channel_id=1, source_target_pairs={{0,0},{1,1},{2,4},{3,5},{4,2},{5,3},{6,6},{7,7},{8,8},{9,9},{10,12... | collective-permute-start | bytes 1769480 | tf_op jit(solution)/shard_map/ppermute | solution.py:57
  12.1 39.7 %collective-permute-start.9 = (bf16[96,768]{1,0:T(8,128)(2,1)S(1)}, bf16[96,768]{1,0:T(8,128)(2,1)}, u32[]{:S(2)}, u32[]{:S(2)}) collective-permute-start(bf16[96,768]{1,0:T(8,128)(2,1)S(1)} %concatenate.178), channel_id=1, source_target_pairs={{0,3},{1,0},{2,1},{3,2},{4,7},{5,4},{6,5},{7,6},{8,11},{9,8},{10,9... | collective-permute-start | bytes 442376 | tf_op jit(solution)/shard_map/ppermute | solution.py:41
  18.0 45.2 %collective-permute-start.8 = (bf16[96,768]{1,0:T(8,128)(2,1)S(1)}, bf16[96,768]{1,0:T(8,128)(2,1)}, u32[]{:S(2)}, u32[]{:S(2)}) collective-permute-start(bf16[96,768]{1,0:T(8,128)(2,1)S(1)} %concatenate.178), channel_id=1, source_target_pairs={{0,2},{1,3},{2,0},{3,1},{4,6},{5,7},{6,4},{7,5},{8,10},{9,11},{10,... | collective-permute-start | bytes 442376 | tf_op jit(solution)/shard_map/ppermute | solution.py:41
  48.6 37.9 %collective-permute-start.21 = (bf16[4,96,1536]{2,1,0:T(8,128)(2,1)S(1)}, bf16[4,96,1536]{2,1,0:T(8,128)(2,1)}, u32[]{:S(2)}, u32[]{:S(2)}) collective-permute-start(bf16[4,96,1536]{2,1,0:T(8,128)(2,1)S(1)} %pad_maximum_fusion.5.refs_14_.refs_17_), channel_id=1, source_target_pairs={{0,8},{4,20},{8,0},{12,28},{16,24},{20,4},{24,16},{28,12},{1,9},{5... | collective-permute-start | bytes 3538952 | tf_op jit(solution)/shard_map/ppermute | solution.py:37
  86.4 30.2 %collective-permute-start.23 = (bf16[4,96,1536]{2,1,0:T(8,128)(2,1)}, bf16[4,96,1536]{2,1,0:T(8,128)(2,1)}, u32[]{:S(2)}, u32[]{:S(2)}) collective-permute-start(bf16[4,96,1536]{2,1,0:T(8,128)(2,1)} %collective-permute-done.21.refs_15_.refs_18_), channel_id=1, source_target_pairs={{0,16},{4,12},{8,24},{12,4},{16,0},{20,28},{24,8},{28,20},{1,17},{... | collective-permute-start | bytes 3538952 | tf_op jit(solution)/shard_map/ppermute | solution.py:37
  94.6 53.2 %collective-permute-start.24 = (bf16[4,96,1536]{2,1,0:T(8,128)(2,1)S(1)}, bf16[4,96,1536]{2,1,0:T(8,128)(2,1)}, u32[]{:S(2)}, u32[]{:S(2)}) collective-permute-start(bf16[4,96,1536]{2,1,0:T(8,128)(2,1)S(1)} %pad_maximum_fusion.5.refs_14_.refs_17_), channel_id=1, source_target_pairs={{0,4},{4,0},{8,12},{12,8},{16,20},{20,16},{24,28},{28,24},{1,5},{5... | collective-permute-start | bytes 3538952 | tf_op jit(solution)/shard_map/ppermute | solution.py:31
  95.1 59.5 %collective-permute-start.25 = (bf16[4,96,1536]{2,1,0:T(8,128)(2,1)}, bf16[4,96,1536]{2,1,0:T(8,128)(2,1)}, u32[]{:S(2)}, u32[]{:S(2)}) collective-permute-start(bf16[4,96,1536]{2,1,0:T(8,128)(2,1)} %collective-permute-done.21.refs_15_.refs_18_), channel_id=1, source_target_pairs={{0,4},{4,0},{8,12},{12,8},{16,20},{20,16},{24,28},{28,24},{1,5},{5... | collective-permute-start | bytes 3538952 | tf_op jit(solution)/shard_map/ppermute | solution.py:31
  104.0 52.5 %collective-permute-start.26 = (bf16[4,96,1536]{2,1,0:T(8,128)(2,1)}, bf16[4,96,1536]{2,1,0:T(8,128)(2,1)}, u32[]{:S(2)}, u32[]{:S(2)}) collective-permute-start(bf16[4,96,1536]{2,1,0:T(8,128)(2,1)} %collective-permute-done.22.refs_16_.refs_19_), channel_id=1, source_target_pairs={{0,4},{4,0},{8,12},{12,8},{16,20},{20,16},{24,28},{28,24},{1,5},{5... | collective-permute-start | bytes 3538952 | tf_op jit(solution)/shard_map/ppermute | solution.py:31
  116.6 42.0 %collective-permute-start.27 = (bf16[4,96,1536]{2,1,0:T(8,128)(2,1)}, bf16[4,96,1536]{2,1,0:T(8,128)(2,1)}, u32[]{:S(2)}, u32[]{:S(2)}) collective-permute-start(bf16[4,96,1536]{2,1,0:T(8,128)(2,1)} %collective-permute-done.23.refs_17_.refs_20_), channel_id=1, source_target_pairs={{0,4},{4,0},{8,12},{12,8},{16,20},{20,16},{24,28},{28,24},{1,5},{5... | collective-permute-start | bytes 3538952 | tf_op jit(solution)/shard_map/ppermute | solution.py:31
  147.8 26.5 %collective-permute-start.43 = (bf16[96,1536]{1,0:T(8,128)(2,1)S(1)}, bf16[96,1536]{1,0:T(8,128)(2,1)S(1)}, u32[]{:S(2)}, u32[]{:S(2)}) collective-permute-start(bf16[96,1536]{1,0:T(8,128)(2,1)S(1)} %get-tuple-element.175), channel_id=1, source_target_pairs={{0,3},{1,0},{2,1},{3,2},{4,7},{5,4},{6,5},{7,6},{8,11},{9,8},{10,9... | collective-permute-start | bytes 884744 | tf_op jit(solution)/shard_map/ppermute | solution.py:41
  154.6 28.0 %collective-permute-start.42 = (bf16[96,1536]{1,0:T(8,128)(2,1)S(1)}, bf16[96,1536]{1,0:T(8,128)(2,1)S(1)}, u32[]{:S(2)}, u32[]{:S(2)}) collective-permute-start(bf16[96,1536]{1,0:T(8,128)(2,1)S(1)} %get-tuple-element.175), channel_id=1, source_target_pairs={{0,2},{1,3},{2,0},{3,1},{4,6},{5,7},{6,4},{7,5},{8,10},{9,11},{10,... | collective-permute-start | bytes 884744 | tf_op jit(solution)/shard_map/ppermute | solution.py:41
  156.5 26.2 %collective-permute-start.41 = (bf16[96,1536]{1,0:T(8,128)(2,1)S(1)}, bf16[96,1536]{1,0:T(8,128)(2,1)S(1)}, u32[]{:S(2)}, u32[]{:S(2)}) collective-permute-start(bf16[96,1536]{1,0:T(8,128)(2,1)S(1)} %get-tuple-element.175), channel_id=1, source_target_pairs={{0,1},{1,2},{2,3},{3,0},{4,5},{5,6},{6,7},{7,4},{8,9},{9,10},{10,1... | collective-permute-start | bytes 884744 | tf_op jit(solution)/shard_map/ppermute | solution.py:41
  174.2 33.0 %collective-permute-start.28 = (bf16[384,768]{1,0:T(8,128)(2,1)}, bf16[384,768]{1,0:T(8,128)(2,1)S(1)}, u32[]{:S(2)}, u32[]{:S(2)}) collective-permute-start(bf16[384,768]{1,0:T(8,128)(2,1)} %get-tuple-element.57), channel_id=1, source_target_pairs={{0,1},{1,0},{2,3},{3,2},{4,5},{5,4},{6,7},{7,6},{8,9},{9,8},{10,11... | collective-permute-start | bytes 1769480 | tf_op jit(solution)/shard_map/ppermute | solution.py:45
  183.8 39.2 %collective-permute-start.44 = (bf16[4,96,1536]{2,1,0:T(8,128)(2,1)}, bf16[4,96,1536]{2,1,0:T(8,128)(2,1)}, u32[]{:S(2)}, u32[]{:S(2)}) collective-permute-start(bf16[4,96,1536]{2,1,0:T(8,128)(2,1)} %pad_maximum_fusion.7.refs_14_.refs_17_), channel_id=1, source_target_pairs={{0,8},{4,20},{8,0},{12,28},{16,24},{20,4},{24,16},{28,12},{1,9},{5... | collective-permute-start | bytes 3538952 | tf_op jit(solution)/shard_map/ppermute | solution.py:37
  223.0 32.4 %collective-permute-start.46 = (bf16[4,96,1536]{2,1,0:T(8,128)(2,1)}, bf16[4,96,1536]{2,1,0:T(8,128)(2,1)}, u32[]{:S(2)}, u32[]{:S(2)}) collective-permute-start(bf16[4,96,1536]{2,1,0:T(8,128)(2,1)} %collective-permute-done.44.refs_15_.refs_18_), channel_id=1, source_target_pairs={{0,16},{4,12},{8,24},{12,4},{16,0},{20,28},{24,8},{28,20},{1,17},{... | collective-permute-start | bytes 3538952 | tf_op jit(solution)/shard_map/ppermute | solution.py:37
  237.1 44.6 %collective-permute-start.52 = (bf16[384,768]{1,0:T(8,128)(2,1)}, bf16[384,768]{1,0:T(8,128)(2,1)S(1)}, u32[]{:S(2)}, u32[]{:S(2)}) collective-permute-start(bf16[384,768]{1,0:T(8,128)(2,1)} %param.19), channel_id=1, source_target_pairs={{0,0},{1,1},{2,4},{3,5},{4,2},{5,3},{6,6},{7,7},{8,8},{9,9},{10,12... | collective-permute-start | bytes 1769480 | tf_op jit(solution)/shard_map/ppermute | solution.py:57
  238.8 55.5 %collective-permute-start.47 = (bf16[4,96,1536]{2,1,0:T(8,128)(2,1)}, bf16[4,96,1536]{2,1,0:T(8,128)(2,1)}, u32[]{:S(2)}, u32[]{:S(2)}) collective-permute-start(bf16[4,96,1536]{2,1,0:T(8,128)(2,1)} %pad_maximum_fusion.7.refs_14_.refs_17_), channel_id=1, source_target_pairs={{0,4},{4,0},{8,12},{12,8},{16,20},{20,16},{24,28},{28,24},{1,5},{5... | collective-permute-start | bytes 3538952 | tf_op jit(solution)/shard_map/ppermute | solution.py:31
  242.8 51.5 %collective-permute-start.48 = (bf16[4,96,1536]{2,1,0:T(8,128)(2,1)}, bf16[4,96,1536]{2,1,0:T(8,128)(2,1)}, u32[]{:S(2)}, u32[]{:S(2)}) collective-permute-start(bf16[4,96,1536]{2,1,0:T(8,128)(2,1)} %collective-permute-done.44.refs_15_.refs_18_), channel_id=1, source_target_pairs={{0,4},{4,0},{8,12},{12,8},{16,20},{20,16},{24,28},{28,24},{1,5},{5... | collective-permute-start | bytes 3538952 | tf_op jit(solution)/shard_map/ppermute | solution.py:31
  242.8 51.5 %collective-permute-start.49 = (bf16[4,96,1536]{2,1,0:T(8,128)(2,1)}, bf16[4,96,1536]{2,1,0:T(8,128)(2,1)}, u32[]{:S(2)}, u32[]{:S(2)}) collective-permute-start(bf16[4,96,1536]{2,1,0:T(8,128)(2,1)} %collective-permute-done.45.refs_16_.refs_19_), channel_id=1, source_target_pairs={{0,4},{4,0},{8,12},{12,8},{16,20},{20,16},{24,28},{28,24},{1,5},{5... | collective-permute-start | bytes 3538952 | tf_op jit(solution)/shard_map/ppermute | solution.py:31
  255.5 38.9 %collective-permute-start.50 = (bf16[4,96,1536]{2,1,0:T(8,128)(2,1)}, bf16[4,96,1536]{2,1,0:T(8,128)(2,1)}, u32[]{:S(2)}, u32[]{:S(2)}) collective-permute-start(bf16[4,96,1536]{2,1,0:T(8,128)(2,1)} %collective-permute-done.46.refs_17_.refs_20_), channel_id=1, source_target_pairs={{0,4},{4,0},{8,12},{12,8},{16,20},{20,16},{24,28},{28,24},{1,5},{5... | collective-permute-start | bytes 3538952 | tf_op jit(solution)/shard_map/ppermute | solution.py:31
  381.2 26.7 %collective-permute-start.54 = (bf16[2,384,768]{2,1,0:T(8,128)(2,1)}, bf16[2,384,768]{2,1,0:T(8,128)(2,1)}, u32[]{:S(2)}, u32[]{:S(2)}) collective-permute-start(bf16[2,384,768]{2,1,0:T(8,128)(2,1)} %get-tuple-element.73), channel_id=1, source_target_pairs={{0,4},{4,0},{8,12},{12,8},{16,20},{20,16},{24,28},{28,24},{1,5},{5... | collective-permute-start | bytes 3538952 | tf_op jit(solution)/shard_map/ppermute | solution.py:31
  403.8 133.8 %collective-permute-start.86 = (bf16[4,4,96,1792]{3,2,1,0:T(8,128)(2,1)}, bf16[4,4,96,1792]{3,2,1,0:T(8,128)(2,1)}, u32[]{:S(2)}, u32[]{:S(2)}) collective-permute-start(bf16[4,4,96,1792]{3,2,1,0:T(8,128)(2,1)} %get-tuple-element.94), channel_id=1, source_target_pairs={{0,4},{4,0},{8,12},{12,8},{16,20},{20,16},{24,28},{28,24},{1,5},{5... | collective-permute-start | bytes 16515080 | tf_op jit(solution)/shard_map/ppermute | solution.py:31
  409.5 29.2 %collective-permute-start.55 = (bf16[384,768]{1,0:T(8,128)(2,1)S(1)}, bf16[384,768]{1,0:T(8,128)(2,1)S(1)}, u32[]{:S(2)}, u32[]{:S(2)}) collective-permute-start(bf16[384,768]{1,0:T(8,128)(2,1)S(1)} %fusion.18), channel_id=1, source_target_pairs={{0,1},{1,0},{2,3},{3,2},{4,5},{5,4},{6,7},{7,6},{8,9},{9,8},{10,11... | collective-permute-start | bytes 1769480 | tf_op jit(solution)/shard_map/ppermute | solution.py:45
  467.6 84.0 %collective-permute-start.80 = (bf16[4,4,96,1792]{3,2,1,0:T(8,128)(2,1)}, bf16[4,4,96,1792]{3,2,1,0:T(8,128)(2,1)}, u32[]{:S(2)}, u32[]{:S(2)}) collective-permute-start(bf16[4,4,96,1792]{3,2,1,0:T(8,128)(2,1)} %get-tuple-element.92), channel_id=1, source_target_pairs={{0,4},{4,0},{8,12},{12,8},{16,20},{20,16},{24,28},{28,24},{1,5},{5... | collective-permute-start | bytes 16515080 | tf_op jit(solution)/shard_map/ppermute | solution.py:31
  473.4 43.2 %collective-permute-start.94 = (f32[20,768]{1,0:T(8,128)S(1)}, f32[20,768]{1,0:T(8,128)S(1)}, u32[]{:S(2)}, u32[]{:S(2)}) collective-permute-start(f32[20,768]{1,0:T(8,128)S(1)} %add.498), channel_id=1, source_target_pairs={{0,16},{4,12},{8,24},{12,4},{16,0},{20,28},{24,8},{28,20},{1,17},{... | collective-permute-start | bytes 184328 | tf_op jit(solution)/shard_map/ppermute | solution.py:37
  541.2 44.5 %collective-permute-start.87 = (bf16[2,4,96,1792]{3,2,1,0:T(8,128)(2,1)S(1)}, bf16[2,4,96,1792]{3,2,1,0:T(8,128)(2,1)S(1)}, u32[]{:S(2)}, u32[]{:S(2)}) collective-permute-start(bf16[2,4,96,1792]{3,2,1,0:T(8,128)(2,1)S(1)} %pad_maximum_fusion.1), channel_id=1, source_target_pairs={{0,8},{4,20},{8,0},{12,28},{16,24},{20,4},{24,16},{28,12},{1,9},{5... | collective-permute-start | bytes 8257544 | tf_op jit(solution)/shard_map/ppermute | solution.py:37
  554.3 75.6 %collective-permute-start.81 = (bf16[2,4,96,1792]{3,2,1,0:T(8,128)(2,1)S(1)}, bf16[2,4,96,1792]{3,2,1,0:T(8,128)(2,1)S(1)}, u32[]{:S(2)}, u32[]{:S(2)}) collective-permute-start(bf16[2,4,96,1792]{3,2,1,0:T(8,128)(2,1)S(1)} %pad_maximum_fusion), channel_id=1, source_target_pairs={{0,8},{4,20},{8,0},{12,28},{16,24},{20,4},{24,16},{28,12},{1,9},{5... | collective-permute-start | bytes 8257544 | tf_op jit(solution)/shard_map/ppermute | solution.py:37
  587.5 44.8 %collective-permute-start.88 = (bf16[4,96,1792]{2,1,0:T(8,128)(2,1)S(1)}, bf16[4,96,1792]{2,1,0:T(8,128)(2,1)S(1)}, u32[]{:S(2)}, u32[]{:S(2)}) collective-permute-start(bf16[4,96,1792]{2,1,0:T(8,128)(2,1)S(1)} %fusion.3), channel_id=1, source_target_pairs={{0,16},{4,12},{8,24},{12,4},{16,0},{20,28},{24,8},{28,20},{1,17},{... | collective-permute-start | bytes 4128776 | tf_op jit(solution)/shard_map/ppermute | solution.py:37
  589.7 49.5 %collective-permute-start.59 = (bf16[384,768]{1,0:T(8,128)(2,1)S(1)}, bf16[384,768]{1,0:T(8,128)(2,1)S(1)}, u32[]{:S(2)}, u32[]{:S(2)}) collective-permute-start(bf16[384,768]{1,0:T(8,128)(2,1)S(1)} %fusion.6), channel_id=1, source_target_pairs={{0,0},{1,1},{2,4},{3,5},{4,2},{5,3},{6,6},{7,7},{8,8},{9,9},{10,12... | collective-permute-start | bytes 1769480 | tf_op jit(solution)/shard_map/ppermute | solution.py:57
  631.8 29.1 %collective-permute-start.82 = (bf16[4,96,1792]{2,1,0:T(8,128)(2,1)S(1)}, bf16[4,96,1792]{2,1,0:T(8,128)(2,1)S(1)}, u32[]{:S(2)}, u32[]{:S(2)}) collective-permute-start(bf16[4,96,1792]{2,1,0:T(8,128)(2,1)S(1)} %fusion.2), channel_id=1, source_target_pairs={{0,16},{4,12},{8,24},{12,4},{16,0},{20,28},{24,8},{28,20},{1,17},{... | collective-permute-start | bytes 4128776 | tf_op jit(solution)/shard_map/ppermute | solution.py:37
  (133 other events, 1876.0 us)

commit v2 on v1

--- a/solution.py
+++ b/solution.py
@@ -59,24 +59,6 @@
 
 def turn_columns(x, z):
     return jnp.stack([lax.dynamic_index_in_dim(x, (z - k) % MP, 0, False) for k in range(MP)])
-
-
-def gather_small(x):
-    return jnp.stack([x] + [column_shift(x, k) for k in range(1, MP)])
-
-
-def gather_bundle(block):
-    if lax.axis_size("dp") != 8:
-        z = lax.axis_index("mp")
-        whole = lax.all_gather(block, "dp", axis=0, tiled=True)
-        whole = lax.all_gather(whole, "mp", axis=0, tiled=False)
-        return [turn_columns(whole, z)]
-    own = gather_small(block)
-    one = plane_swap(own, True)
-    two = plane_swap(own, False)
-    three = plane_swap(one, False)
-    mine = [own, one, two, three]
-    return mine + [core_swap(m) for m in mine]
 
 
 def row_offsets(g, c, rows):
@@ -204,210 +186,672 @@
     return (gdy - mean_one - n * mean_two) * scale
 
 
-def start_pieces(scal, pieces, sems, base, copies):
-    started = []
-    for i, piece in enumerate(pieces):
-        offset = pl.multiple_of(scal[i], 32)
-        source, target = copies(piece, offset)
-        copy = pltpu.make_async_copy(source, target, sems.at[base + i])
+def vmem():
+    return pl.BlockSpec(memory_space=pltpu.VMEM)
+
+
+def smem():
+    return pl.BlockSpec(memory_space=pltpu.SMEM)
+
+
+def anywhere():
+    return pl.BlockSpec(memory_space=pl.ANY)
+
+
+def params():
+    return pltpu.CompilerParams(vmem_limit_bytes=VMEM_LIMIT)
+
+
+def shape(dims, dtype):
+    return jax.ShapeDtypeStruct(dims, dtype)
+
+
+def project_rows(i, z, x, w_ref, bias, cos, sin, q_ref, k_ref, v_ref):
+    block = x.shape[0]
+    at = pl.ds(i * block, block)
+    p = nn(x, w_ref[z, :, LANES : 5 * LANES]) + bias[:, LANES:]
+    low_half = lane_index((block, LANES)) < HD
+    mixed = p[:, 0:LANES]
+    mixed = mixed * cos + half_swap(mixed) * sin
+    pair = p[:, LANES : 2 * LANES]
+    pair = pair * cos + half_swap(pair) * sin
+    k_ref[z, 0, at, :] = pair.astype(BF16)
+    k_ref[z, 1, at, :] = jnp.where(low_half, pltpu.roll(mixed, HD, 1), 0.0).astype(BF16)
+    v_ref[z, 0, at, :] = p[:, 2 * LANES : 3 * LANES].astype(BF16)
+    v_ref[z, 1, at, :] = jnp.where(low_half, p[:, 3 * LANES :], 0.0).astype(BF16)
+    if i < 2:
+        q = nn(x, w_ref[z, :, 0:LANES]) + bias[:, 0:LANES]
+        q = q * cos + half_swap(q) * sin
+        q_ref[z, 0, at, :] = q.astype(BF16) * BF16(HD**-0.5)
+        q_ref[z, 1, at, :] = jnp.where(low_half, mixed, 0.0).astype(BF16) * BF16(HD**-0.5)
+
+
+def attend_rows(i, qblock, qcode_ref, kcode_ref, q_ref, k_ref, v_ref, mixed_ref, lse_cols):
+    at = pl.ds(pl.multiple_of(i * qblock, qblock), qblock)
+    visible = qcode_ref[at, :] == kcode_ref[...]
+    low_half = lane_index((qblock, LANES)) < HD
+    lane = lane_index((qblock, LANES))
+    for z in range(2):
+        outs = []
+        for h in range(3):
+            tile = h // 2
+            q = q_ref[z, tile, at, :]
+            if h < 2:
+                q = jnp.where(low_half == (h == 0), q, BF16(0))
+            s = nt(q, k_ref[z, tile])
+            s = jnp.where(visible, s, NEGATIVE)
+            m = jnp.max(s, axis=-1, keepdims=True)
+            p = jnp.exp(s - m)
+            l = jnp.sum(p, axis=-1, keepdims=True)
+            o = nn(p.astype(BF16), v_ref[z, tile])
+            outs.append(o / l)
+            lse_cols[at, :] = jnp.where(lane == 3 * z + h, m + jnp.log(l), lse_cols[at, :])
+        mixed_ref[at, pl.ds(z * 256, LANES)] = pltpu.roll(outs[2], HD, 1).astype(BF16)
+        mixed_ref[at, pl.ds(z * 256 + LANES, LANES)] = jnp.where(
+            low_half, outs[0], outs[1]
+        ).astype(BF16)
+
+
+def forward_kernel(n_layers, *refs):
+    n_in, per_layer = 7, 11
+    blocks, tokens, cot, small, meta, frequency, vectors = refs[:n_in]
+    w_all, dy_out, low_out, cos_out, sin_out, qrow_out, kcol_out = refs[n_in : n_in + 7]
+    saved = [
+        refs[n_in + 7 + l * per_layer : n_in + 7 + (l + 1) * per_layer] for l in range(n_layers)
+    ]
+    (
+        xfull,
+        mixed_in,
+        small_all,
+        meta_in,
+        wa,
+        wo,
+        win,
+        wback,
+        cos_ref,
+        sin_ref,
+        qcode_ref,
+        kcode_ref,
+        qrow_ref,
+        kcol_ref,
+        q_ref,
+        k_ref,
+        v_ref,
+        mixed_ref,
+        lse_cols,
+        lse_ref,
+        stream,
+        sum_ref,
+        r1_ref,
+        low_ref,
+        e_ref,
+        gp_ref,
+        z_send,
+        z_recv,
+        p_send,
+        p_recv,
+        c_send,
+        c_recv,
+        x_send,
+        x_recv,
+        t_send,
+        t_recv,
+        l_sem,
+        w_sem,
+        s_sem,
+    ) = refs[n_in + 7 + n_layers * per_layer :]
+    rows = stream.shape[0]
+    width = stream.shape[1]
+    height = blocks.shape[1]
+    chunks = blocks.shape[0]
+
+    d = lax.axis_index("dp")
+    z = lax.axis_index("mp")
+    c = d % 2
+    x = (d // 2) % 2
+    y = d // 4
+    flip_x, flip_y = 1 - 2 * x, 1 - 2 * y
+    one_x, one_y = x + (1 - c) * flip_x, y + c * flip_y
+    two_x, two_y = x + c * flip_x, y + (1 - c) * flip_y
+
+    def device(yy, xx, cc, zz):
+        return (yy * 4 + xx * 2 + cc, zz)
+
+    def rows_of(yy, xx):
+        return pl.ds(pl.multiple_of((yy * 4 + xx * 2 + c) * height, 32), height)
+
+    sibling = device(y, x, 1 - c, z)
+    first = device(one_y, one_x, c, z)
+    second = device(two_y, two_x, c, z)
+    pair_z = z + 1 - 2 * (z % 2)
+    pair = device(y, x, c, pair_z)
+    away = device(y, x, 1 - c, (z + 2) % MP)
+    moved = c != z // 2
+    columns = [device(y, x, c, (z + s) % MP) for s in range(1, MP)]
+    own_rows = rows_of(y, x)
+    first_rows = rows_of(one_y, one_x)
+    second_rows = rows_of(two_y, two_x)
+    third_rows = rows_of(1 - y, 1 - x)
+
+    barrier = pltpu.get_barrier_semaphore()
+    partners = columns + [first, second, sibling, away]
+    for partner in partners:
+        pl.semaphore_signal(
+            barrier, inc=1, device_id=partner, device_id_type=pl.DeviceIdType.MESH
+        )
+    pl.semaphore_wait(barrier, len(partners))
+
+    def remote(source, target, send, recv, to):
+        return pltpu.make_async_remote_copy(
+            src_ref=source,
+            dst_ref=target,
+            send_sem=send,
+            recv_sem=recv,
+            device_id=to,
+            device_id_type=pl.DeviceIdType.MESH,
+        )
+
+    sent = []
+
+    def go(make, *at):
+        make(*at).start()
+        sent.append((make, at))
+
+    def local_copy(k):
+        return pltpu.make_async_copy(blocks.at[k], w_all.at[k, z, own_rows], l_sem.at[k])
+
+    def z_copy(k, s):
+        return remote(
+            blocks.at[k], w_all.at[k, z, own_rows], z_send.at[k, s], z_recv.at[k, s], columns[s]
+        )
+
+    def p_copy(k, n):
+        source = w_all.at[k, :, first_rows if n == 2 else own_rows]
+        return remote(
+            source, source, p_send.at[k, n], p_recv.at[k, n], first if n == 0 else second
+        )
+
+    def c_copy(k, n):
+        source = w_all.at[k, :, (own_rows, first_rows, second_rows, third_rows)[n]]
+        return remote(source, source, c_send.at[k, n], c_recv.at[k, n], sibling)
+
+    def step_send(k):
+        local_copy(k).start()
+        for s in range(MP - 1):
+            go(z_copy, k, s)
+
+    def step_plane(k):
+        local_copy(k).wait()
+        for s in range(MP - 1):
+            z_copy(k, s).wait_recv()
+        go(p_copy, k, 0)
+        go(p_copy, k, 1)
+        go(c_copy, k, 0)
+        if k + 2 < chunks:
+            step_send(k + 2)
+
+    def step_forward(k):
+        p_copy(k, 0).wait_recv()
+        go(p_copy, k, 2)
+        go(c_copy, k, 1)
+        p_copy(k, 1).wait_recv()
+        go(c_copy, k, 2)
+
+    def step_last(k):
+        p_copy(k, 2).wait_recv()
+        go(c_copy, k, 3)
+
+    def step_ready(k):
+        for n in range(4):
+            c_copy(k, n).wait_recv()
+
+    plan = []
+    for k in range(chunks):
+        plan.append(partial(step_plane, k))
+        plan.append(partial(step_forward, k))
+        plan.append(partial(step_last, k))
+    for k in range(chunks - 1):
+        at = plan.index(plan[3 * k + 2])
+        plan[at], plan[at + 1] = plan[at + 1], plan[at]
+    position = [0]
+
+    def take(until):
+        steps = plan[position[0] : until]
+        position[0] = max(position[0], until)
+        return steps
+
+    def run(steps):
+        for step in steps:
+            step()
+
+    def meta_copy():
+        return remote(meta, meta_in, t_send.at[0], t_recv.at[0], sibling)
+
+    def small_copy(s):
+        return remote(small, small_all.at[z], t_send.at[3 + s], t_recv.at[3 + s], columns[s])
+
+    go(meta_copy)
+    token_copy = remote(tokens, xfull.at[0, 0], t_send.at[1], t_recv.at[1], away)
+    token_local = pltpu.make_async_copy(tokens, xfull.at[0, 0], l_sem.at[chunks])
+
+    @pl.when(moved)
+    def _():
+        token_copy.start()
+
+    @pl.when(jnp.logical_not(moved))
+    def _():
+        token_local.start()
+
+    step_send(0)
+    for s in range(MP - 1):
+        go(small_copy, s)
+    step_send(1)
+    small_local = pltpu.make_async_copy(small, small_all.at[z], l_sem.at[chunks + 1])
+    small_local.start()
+
+    meta_copy().wait_recv()
+    info = jnp.where(moved, meta_in[...], meta[...])
+    slot = info[0:1, :]
+    limits = [info[n : n + 1, :] for n in range(1, 4)]
+    half = z % 2
+    quarters = [2 * c + half, 2 * (1 - c) + half, 2 * c + 1 - half, 2 * (1 - c) + 1 - half]
+
+    def codes(place_all, slot, limits):
+        seq = jnp.where(place_all >= slot, 1.0, 0.0) + jnp.where(place_all >= 2.0 * slot, 1.0, 0.0)
+        place = place_all - seq * slot
+        limit = jnp.where(seq == 0.0, limits[0], jnp.where(seq == 1.0, limits[1], limits[2]))
+        return seq, place, jnp.where(place < limit, seq, -1.0)
+
+    sign = jnp.where(lane_index((1, LANES)) % HD < HD // 2, -1.0, 1.0)
+    for i in range(4):
+        at = pl.ds(i * rows, rows)
+        base = quarters[i] * rows
+        index = lax.broadcasted_iota(jnp.int32, (rows, LANES), 0) + base
+        seq, place, kcode = codes(index.astype(F32), slot, limits)
+        angle = place * frequency[...]
+        cos_ref[at, :] = jnp.cos(angle)
+        sin_ref[at, :] = jnp.sin(angle) * sign
+        kcol_ref[at, :] = kcode[:, 0:1]
+        if i < 2:
+            qcode_ref[at, :] = seq[:, 0:1]
+        index = lax.broadcasted_iota(jnp.int32, (1, rows), 1) + base
+        seq, place, kcode = codes(
+            index.astype(F32), slot[:, 0:1], [limit[:, 0:1] for limit in limits]
+        )
+        kcode_ref[:, pl.ds(i * rows, rows)] = kcode
+        if i < 2:
+            qrow_ref[:, pl.ds(i * rows, rows)] = seq
+
+    @pl.when(moved)
+    def _():
+        token_copy.wait_recv()
+
+    @pl.when(jnp.logical_not(moved))
+    def _():
+        token_local.wait()
+
+    def x_copy(l, n):
+        source = xfull.at[l, 2 if n == 2 else 0]
+        target = xfull.at[l, (2, 1, 3)[n]]
+        return remote(
+            source, target, x_send.at[l, n], x_recv.at[l, n], pair if n == 0 else sibling
+        )
+
+    def m_copy(l):
+        return remote(
+            mixed_ref.at[pl.ds(rows, rows)],
+            mixed_in.at[l],
+            x_send.at[l, 3],
+            x_recv.at[l, 3],
+            sibling,
+        )
+
+    stores = {}
+
+    def store(name, source, target):
+        copy = pltpu.make_async_copy(source, target, s_sem.at[len(stores)])
         copy.start()
-        started.append(copy)
-    return started
-
-
-def attend_kernel(n_pieces, rows, *refs):
-    scal, x_ref, bias_ref, cos_ref, sin_ref, qcode_ref, kcode_ref = refs[:7]
-    pieces = refs[7 : 7 + n_pieces]
-    q_ref, k_ref, v_ref, own_ref, sib_ref, lse_ref = refs[7 + n_pieces : 13 + n_pieces]
-    w_ref, lse_cols, sems = refs[13 + n_pieces :]
-    first_z = scal[n_pieces]
-
-    copies = start_pieces(
-        scal,
-        pieces,
-        sems,
-        0,
-        lambda piece, offset: (
-            piece.at[pl.ds(first_z, 2)],
-            w_ref.at[:, pl.ds(offset, rows), :],
+        stores[name] = copy
+
+    waited = set()
+
+    def stored(*names):
+        for name in names:
+            if name in stores and name not in waited:
+                waited.add(name)
+                stores[name].wait()
+
+    stream[...] = xfull[0, 0].astype(F32)
+    store("cos", cos_ref, cos_out)
+    store("sin", sin_ref, sin_out)
+    store("qrow", qrow_ref, qrow_out)
+    store("kcol", kcol_ref, kcol_out)
+
+    cot_copy = remote(cot, dy_out, t_send.at[2], t_recv.at[2], away)
+    cot_local = pltpu.make_async_copy(cot, dy_out, l_sem.at[chunks + 2])
+
+    def load(source, target, n):
+        copy = pltpu.make_async_copy(source, target, w_sem.at[n])
+        copy.start()
+        return copy
+
+    qblock = 256
+    count = 2 * rows // qblock
+    own_z = [(z - 2 * c - k + MP) % MP for k in range(2)]
+    other_z = [(at + 2) % MP for at in own_z]
+    for l in range(n_layers):
+        xs, qs, ks, vs, ms, mis, ls, r1s, r2s, es, gps = saved[l]
+        last = l - 1
+        go(x_copy, l, 0)
+        go(x_copy, l, 1)
+        run(take(9 * l + 3))
+        x_copy(l, 0).wait_recv()
+        go(x_copy, l, 2)
+        run(take(9 * l + 4))
+        step_ready(3 * l)
+        wa_loads = [
+            load(w_all.at[3 * l, own_z[k], :, pl.ds(0, 5 * LANES)], wa.at[k], k) for k in range(2)
+        ]
+        wo_load = load(w_all.at[3 * l, :, :, pl.ds(4 * LANES, 2 * LANES)], wo, 2)
+        if l == 0:
+
+            @pl.when(moved)
+            def _():
+                cot_copy.start()
+
+            @pl.when(jnp.logical_not(moved))
+            def _():
+                cot_local.start()
+
+            for s in range(MP - 1):
+                small_copy(s).wait_recv()
+            small_local.wait()
+        else:
+            m_copy(last).wait_send()
+        stored(("q", last), ("k", last), ("v", last), ("mixed", last), ("lse", last))
+        lse_cols[...] = jnp.zeros_like(lse_cols)
+        for copy in wa_loads:
+            copy.wait()
+        for i in range(4):
+            if i == 1:
+                x_copy(l, 1).wait_recv()
+            if i == 3:
+                run(take(9 * l + 6 - l))
+                x_copy(l, 2).wait_recv()
+            at = pl.ds(i * rows, rows)
+            for k in range(2):
+                bias = small_all[own_z[k], pl.ds(l, 1), pl.ds(0, 5 * LANES)]
+                project_rows(
+                    i, k, xfull[l, i], wa, bias, cos_ref[at, :], sin_ref[at, :], q_ref, k_ref, v_ref
+                )
+        store(("q", l), q_ref, qs)
+        store(("k", l), k_ref, ks)
+        store(("v", l), v_ref, vs)
+        store(("x", l), xfull.at[l], xs)
+        steps = [take(9 * l + 7), take(9 * l + 8 - l), take(9 * l + 9 - l)]
+
+        def one_block(n, _, l=l, steps=steps):
+            attend_rows(
+                count - 1 - n, qblock, qcode_ref, kcode_ref, q_ref, k_ref, v_ref, mixed_ref, lse_cols
+            )
+            for j in range(count):
+
+                @pl.when(n == j)
+                def _(j=j):
+                    if j == 1:
+                        m_copy(l).start()
+                    run(steps[j])
+
+            return 0
+
+        lax.fori_loop(0, count, one_block, 0)
+        lse_ref[...] = jnp.transpose(lse_cols[...])[0:8, :]
+        store(("mixed", l), mixed_ref, ms)
+        store(("lse", l), lse_ref, ls)
+        step_ready(3 * l + 1)
+        win_load = load(w_all.at[3 * l + 1], win, 3)
+        stored(("r1", last), ("r2", last), ("e", last), ("gp", last))
+        wo_load.wait()
+        m_copy(l).wait_recv()
+        store(("mixed_in", l), mixed_in.at[l], mis)
+        a = jnp.zeros((rows, width), F32)
+        for k in range(2):
+            a = a + nt(mixed_ref[0:rows, k * 256 : k * 256 + 256], wo[own_z[k]])
+            a = a + nt(mixed_in[l, :, k * 256 : k * 256 + 256], wo[other_z[k]])
+        vec = vectors[l]
+        r1 = stream[...] + a + vec[0:1, :]
+        r1_ref[...] = r1
+        store(("r1", l), r1_ref, r1s)
+        n1, _ = norm_parts(r1)
+        h = n1 * vec[1:2, :] + vec[2:3, :]
+        low_ref[...] = h.astype(BF16)
+        sum_ref[...] = h + vec[3:4, :]
+        win_load.wait()
+
+        def inner(zz, _, l=l):
+            u = nn(low_ref[...], win[zz]) + small_all[zz, pl.ds(l, 1), pl.ds(5 * LANES, width)]
+            cdf = 0.5 * (1.0 + lax.erf(u * (2.0**-0.5)))
+            pdf = jnp.exp(u * u * -0.5) * 0.3989422804014327
+            e_ref[zz] = (u * cdf).astype(BF16)
+            gp_ref[zz] = (cdf + u * pdf).astype(BF16)
+            return 0
+
+        lax.fori_loop(0, 2, inner, 0)
+        run(take(9 * l + 10 - l))
+        lax.fori_loop(2, MP, inner, 0)
+        run(take(10 if l == 0 else 18))
+        step_ready(3 * l + 2)
+        wback_load = load(w_all.at[3 * l + 2], wback, 4)
+        store(("e", l), e_ref, es)
+        store(("gp", l), gp_ref, gps)
+        wback_load.wait()
+
+        def outer(zz, _):
+            sum_ref[...] += nt(e_ref[zz], wback[zz])
+            return 0
+
+        lax.fori_loop(0, MP, outer, 0)
+        store(("r2", l), sum_ref, r2s)
+        n2, _ = norm_parts(sum_ref[...])
+        result = n2 * vec[4:5, :] + vec[5:6, :]
+        if l + 1 < n_layers:
+            stream[...] = result
+            xfull[l + 1, 0] = result.astype(BF16)
+        else:
+            low_ref[...] = result.astype(BF16)
+            store("low", low_ref, low_out)
+
+    m_copy(n_layers - 1).wait_send()
+    for make, at in sent:
+        make(*at).wait_send()
+    @pl.when(moved)
+    def _():
+        token_copy.wait_send()
+        cot_copy.wait_send()
+        cot_copy.wait_recv()
+
+    @pl.when(jnp.logical_not(moved))
+    def _():
+        cot_local.wait()
+
+    stored(*stores)
+
+
+def forward(blocks, tokens, cot, small, meta, frequency, vectors):
+    n_layers = vectors.shape[0]
+    chunks, height, width = blocks.shape
+    rows = tokens.shape[0]
+    queries, keys = 2 * rows, 4 * rows
+    layer_out = (
+        shape((4, rows, width), BF16),
+        shape((2, 2, queries, LANES), BF16),
+        shape((2, 2, keys, LANES), BF16),
+        shape((2, 2, keys, LANES), BF16),
+        shape((queries, 512), BF16),
+        shape((rows, 512), BF16),
+        shape((8, queries), F32),
+        shape((rows, width), F32),
+        shape((rows, width), F32),
+        shape((MP, rows, width), BF16),
+        shape((MP, rows, width), BF16),
+    )
+    outs = (
+        shape((chunks, MP, 8 * height, width), BF16),
+        shape((rows, width), BF16),
+        shape((rows, width), BF16),
+        shape((keys, LANES), F32),
+        shape((keys, LANES), F32),
+        shape((1, queries), F32),
+        shape((keys, 1), F32),
+    ) + layer_out * n_layers
+    sem = pltpu.SemaphoreType.DMA
+    results = pl.pallas_call(
+        partial(forward_kernel, n_layers),
+        out_shape=outs,
+        in_specs=[anywhere()] * 3 + [vmem()] * 4,
+        out_specs=(anywhere(),) * len(outs),
+        scratch_shapes=[
+            pltpu.VMEM((n_layers, 4, rows, width), BF16),
+            pltpu.VMEM((n_layers, rows, 512), BF16),
+            pltpu.VMEM((MP,) + small.shape, F32),
+            pltpu.VMEM(meta.shape, F32),
+            pltpu.VMEM((2, width, 5 * LANES), BF16),
+            pltpu.VMEM((MP, width, 2 * LANES), BF16),
+            pltpu.VMEM((MP, width, width), BF16),
+            pltpu.VMEM((MP, width, width), BF16),
+            pltpu.VMEM((keys, LANES), F32),
+            pltpu.VMEM((keys, LANES), F32),
+            pltpu.VMEM((queries, 1), F32),
+            pltpu.VMEM((1, keys), F32),
+            pltpu.VMEM((1, queries), F32),
+            pltpu.VMEM((keys, 1), F32),
+            pltpu.VMEM((2, 2, queries, LANES), BF16),
+            pltpu.VMEM((2, 2, keys, LANES), BF16),
+            pltpu.VMEM((2, 2, keys, LANES), BF16),
+            pltpu.VMEM((queries, 512), BF16),
+            pltpu.VMEM((queries, LANES), F32),
+            pltpu.VMEM((8, queries), F32),
+            pltpu.VMEM((rows, width), F32),
+            pltpu.VMEM((rows, width), F32),
+            pltpu.VMEM((rows, width), F32),
+            pltpu.VMEM((rows, width), BF16),
+            pltpu.VMEM((MP, rows, width), BF16),
+            pltpu.VMEM((MP, rows, width), BF16),
+            sem((chunks, 3)),
+            sem((chunks, 3)),
+            sem((chunks, 3)),
+            sem((chunks, 3)),
+            sem((chunks, 4)),
+            sem((chunks, 4)),
+            sem((n_layers, 4)),
+            sem((n_layers, 4)),
+            sem((6,)),
+            sem((6,)),
+            sem((chunks + 3,)),
+            sem((5,)),
+            sem((5 + 11 * n_layers,)),
+        ],
+        compiler_params=pltpu.CompilerParams(
+            vmem_limit_bytes=VMEM_LIMIT, collective_id=0, has_side_effects=True
         ),
-    )
+        cost_estimate=pl.CostEstimate(
+            flops=100_000_000_000, bytes_accessed=100_000_000, transcendentals=20_000_000
+        ),
+        name="forward",
+    )(blocks, tokens, cot, small, meta, frequency, vectors)
+    head = results[:7]
+    states = [results[7 + 11 * l : 18 + 11 * l] for l in range(n_layers)]
+    return head, states
+
+
+def attend_kernel(chunk, *refs):
+    scal, x_ref, bias_ref, cos_ref, sin_ref, qcode_ref, kcode_ref, w_all = refs[:8]
+    q_ref, k_ref, v_ref, mixed_ref, lse_ref, w_ref, lse_cols, sems = refs[8:]
+    copies = [
+        pltpu.make_async_copy(
+            w_all.at[chunk, scal[k], :, pl.ds(0, 5 * LANES)], w_ref.at[k], sems.at[k]
+        )
+        for k in range(2)
+    ]
+    for copy in copies:
+        copy.start()
     for copy in copies:
         copy.wait()
-    keys = x_ref.shape[0]
-    queries = keys // 2
-    block = queries // 2
-
-    for z in range(2):
-
-        def project(i, _, z=z):
-            at = pl.ds(pl.multiple_of(i * block, block), block)
-            cos, sin = cos_ref[at, :], sin_ref[at, :]
-            p = nn(x_ref[at, :], w_ref[z, :, LANES : 5 * LANES]) + bias_ref[z, :, LANES:]
-            low_half = lane_index((block, LANES)) < HD
-            mixed = p[:, 0:LANES]
-            mixed = mixed * cos + half_swap(mixed) * sin
-            pair = p[:, LANES : 2 * LANES]
-            pair = pair * cos + half_swap(pair) * sin
-            k_ref[z, 0, at, :] = pair.astype(BF16)
-            k_ref[z, 1, at, :] = jnp.where(low_half, pltpu.roll(mixed, HD, 1), 0.0).astype(BF16)
-            v_ref[z, 0, at, :] = p[:, 2 * LANES : 3 * LANES].astype(BF16)
-            v_ref[z, 1, at, :] = jnp.where(low_half, p[:, 3 * LANES :], 0.0).astype(BF16)
-
-            @pl.when(i < 2)
-            def _():
-                q = nn(x_ref[at, :], w_ref[z, :, 0:LANES]) + bias_ref[z, :, 0:LANES]
-                q = q * cos + half_swap(q) * sin
-                q_ref[z, 0, at, :] = q.astype(BF16) * BF16(HD**-0.5)
-                q_ref[z, 1, at, :] = jnp.where(low_half, mixed, 0.0).astype(BF16) * BF16(HD**-0.5)
-
-            return 0
-
-        lax.fori_loop(0, 4, project, 0)
-
+    rows = x_ref.shape[1]
+    for i in range(4):
+        at = pl.ds(i * rows, rows)
+        for k in range(2):
+            project_rows(
+                i,
+                k,
+                x_ref[i],
+                w_ref,
+                bias_ref[k],
+                cos_ref[at, :],
+                sin_ref[at, :],
+                q_ref,
+                k_ref,
+                v_ref,
+            )
     lse_cols[...] = jnp.zeros_like(lse_cols)
-    qblock = 256
 
     def one_block(i, _):
-        at = pl.ds(pl.multiple_of(i * qblock, qblock), qblock)
-        visible = qcode_ref[at, :] == kcode_ref[...]
-        low_half = lane_index((qblock, LANES)) < HD
-        lane = lane_index((qblock, LANES))
-        for z in range(2):
-            outs = []
-            for h in range(3):
-                tile = h // 2
-                q = q_ref[z, tile, at, :]
-                if h < 2:
-                    q = jnp.where(low_half == (h == 0), q, BF16(0))
-                s = nt(q, k_ref[z, tile])
-                s = jnp.where(visible, s, NEGATIVE)
-                m = jnp.max(s, axis=-1, keepdims=True)
-                p = jnp.exp(s - m)
-                l = jnp.sum(p, axis=-1, keepdims=True)
-                o = nn(p.astype(BF16), v_ref[z, tile])
-                outs.append(o / l)
-                lse_cols[at, :] = jnp.where(lane == 3 * z + h, m + jnp.log(l), lse_cols[at, :])
-            single = pltpu.roll(outs[2], HD, 1).astype(BF16)
-            pair = jnp.where(low_half, outs[0], outs[1]).astype(BF16)
-            mixed_ref[at, pl.ds(z * 256, LANES)] = single
-            mixed_ref[at, pl.ds(z * 256 + LANES, LANES)] = pair
+        attend_rows(i, 256, qcode_ref, kcode_ref, q_ref, k_ref, v_ref, mixed_ref, lse_cols)
         return 0
 
-    mixed_ref = own_ref
-    lax.fori_loop(0, queries // qblock, one_block, 0)
-    sib_ref[...] = own_ref[pl.ds(block, block), :]
+    lax.fori_loop(0, 2 * rows // 256, one_block, 0)
     lse_ref[...] = jnp.transpose(lse_cols[...])[0:8, :]
 
 
-def vmem():
-    return pl.BlockSpec(memory_space=pltpu.VMEM)
-
-
-def smem():
-    return pl.BlockSpec(memory_space=pltpu.SMEM)
-
-
-def anywhere():
-    return pl.BlockSpec(memory_space=pl.ANY)
-
-
-def params():
-    return pltpu.CompilerParams(vmem_limit_bytes=VMEM_LIMIT)
-
-
-def shape(dims, dtype):
-    return jax.ShapeDtypeStruct(dims, dtype)
-
-
-def piece_rows(pieces):
-    return pieces[0].shape[1]
-
-
-def attend(scal, x_full, bias, tables, pieces):
-    cos, sin, qcode, kcode = tables[:4]
-    keys, width = x_full.shape
-    queries = keys // 2
+def attend(scal, x_full, bias, tables, qcode, kcode, w_all, chunk):
+    cos, sin = tables[:2]
+    _, rows, width = x_full.shape
+    queries, keys = 2 * rows, 4 * rows
     return pl.pallas_call(
-        partial(attend_kernel, len(pieces), piece_rows(pieces)),
+        partial(attend_kernel, chunk),
         out_shape=(
             shape((2, 2, queries, LANES), BF16),
             shape((2, 2, keys, LANES), BF16),
             shape((2, 2, keys, LANES), BF16),
             shape((queries, 512), BF16),
-            shape((queries // 2, 512), BF16),
             shape((8, queries), F32),
         ),
-        in_specs=[smem()] + [vmem()] * 6 + [anywhere()] * len(pieces),
-        out_specs=(vmem(),) * 6,
+        in_specs=[smem()] + [vmem()] * 6 + [anywhere()],
+        out_specs=(vmem(),) * 5,
         scratch_shapes=[
-            pltpu.VMEM((2, width, 6 * LANES), BF16),
+            pltpu.VMEM((2, width, 5 * LANES), BF16),
             pltpu.VMEM((queries, LANES), F32),
-            pltpu.SemaphoreType.DMA((len(pieces),)),
+            pltpu.SemaphoreType.DMA((2,)),
         ],
         compiler_params=params(),
-        cost_estimate=pl.CostEstimate(
-            flops=16_000_000_000, bytes_accessed=16_000_000, transcendentals=8_000_000
+        name="attend",
+    )(scal, x_full, bias, cos, sin, qcode, kcode, w_all)
+
+
+def feed_kernel(chunk, *refs):
+    scal, x_ref, own_ref, sib_ref, vec_ref, bin_ref, w_all = refs[:7]
+    next_ref, low_ref, r1_ref, r2_ref, e_ref, gp_ref, wo_ref, win_ref, wback_ref, sems = refs[7:]
+    copies = [
+        pltpu.make_async_copy(
+            w_all.at[chunk, :, :, pl.ds(4 * LANES, 2 * LANES)], wo_ref, sems.at[0]
         ),
-        name="attend",
-    )(scal, x_full, bias, cos, sin, qcode, kcode, *pieces)
-
-
-def feed_kernel(n_pieces, rows, layer_last, *refs):
-    scal, x_ref, own_ref, sib_ref, vec_ref, bin_ref = refs[:6]
-    attn = refs[6 : 6 + n_pieces]
-    feed = refs[6 + n_pieces : 6 + 2 * n_pieces]
-    at = 6 + 2 * n_pieces
-    next_ref, low_ref, r1_ref, r2_ref, e_ref, gp_ref = refs[at : at + 6]
-    wo_ref, win_ref, wback_ref, sems = refs[at + 6 :]
-    out_copies = start_pieces(
-        scal,
-        attn,
-        sems,
-        0,
-        lambda piece, offset: (
-            piece.at[:, :, pl.ds(4 * LANES, 2 * LANES)],
-            wo_ref.at[:, pl.ds(offset, rows), :],
-        ),
-    )
-    width = x_ref.shape[1]
-    in_copies = start_pieces(
-        scal,
-        feed,
-        sems,
-        n_pieces,
-        lambda piece, offset: (
-            piece.at[:, :, pl.ds(0, width)],
-            win_ref.at[:, pl.ds(offset, rows), :],
-        ),
-    )
-    back_copies = start_pieces(
-        scal,
-        feed,
-        sems,
-        2 * n_pieces,
-        lambda piece, offset: (
-            piece.at[:, :, pl.ds(width, width)],
-            wback_ref.at[:, pl.ds(offset, rows), :],
-        ),
-    )
-    first_z = scal[n_pieces]
-    for copy in out_copies:
+        pltpu.make_async_copy(w_all.at[chunk + 1], win_ref, sems.at[1]),
+        pltpu.make_async_copy(w_all.at[chunk + 2], wback_ref, sems.at[2]),
+    ]
+    for copy in copies:
+        copy.start()
+    for copy in copies:
         copy.wait()
     a = jnp.zeros(x_ref.shape, F32)
-    for z in range(2):
-        a = a + nt(own_ref[:, z * 256 : z * 256 + 256], wo_ref[first_z + z])
-        a = a + nt(sib_ref[:, z * 256 : z * 256 + 256], wo_ref[2 - first_z + z])
+    for k in range(2):
+        a = a + nt(own_ref[:, k * 256 : k * 256 + 256], wo_ref[scal[k]])
+        a = a + nt(sib_ref[:, k * 256 : k * 256 + 256], wo_ref[lax.rem(scal[k] + 2, MP)])
     r1 = x_ref[...] + a + vec_ref[0:1, :]
     r1_ref[...] = r1
     n1, _ = norm_parts(r1)
     h = n1 * vec_ref[1:2, :] + vec_ref[2:3, :]
     low_ref[...] = h.astype(BF16)
     r2_ref[...] = h + vec_ref[3:4, :]
-    for copy in in_copies:
-        copy.wait()
-    for copy in back_copies:
-        copy.wait()
 
     def one(z, _):
         u = nn(low_ref[...], win_ref[z]) + bin_ref[z]
@@ -426,11 +870,10 @@
     low_ref[...] = result.astype(BF16)
 
 
-def feed_forward(scal, x, own, sib, vec, bias_in, attn, feed):
+def feed_forward(scal, x, own, sib, vec, bias_in, w_all, chunk):
     rows, width = x.shape
-    count = len(attn)
     return pl.pallas_call(
-        partial(feed_kernel, count, piece_rows(attn), False),
+        partial(feed_kernel, chunk),
         out_shape=(
             shape((rows, width), F32),
             shape((rows, width), BF16),
@@ -439,63 +882,98 @@
             shape((MP, rows, width), BF16),
             shape((MP, rows, width), BF16),
         ),
-        in_specs=[smem()] + [vmem()] * 5 + [anywhere()] * (2 * count),
+        in_specs=[smem()] + [vmem()] * 5 + [anywhere()],
         out_specs=(vmem(),) * 6,
         scratch_shapes=[
             pltpu.VMEM((MP, width, 2 * LANES), BF16),
             pltpu.VMEM((MP, width, width), BF16),
             pltpu.VMEM((MP, width, width), BF16),
-            pltpu.SemaphoreType.DMA((3 * count,)),
+            pltpu.SemaphoreType.DMA((3,)),
         ],
         compiler_params=params(),
-        cost_estimate=pl.CostEstimate(
-            flops=8_000_000_000, bytes_accessed=20_000_000, transcendentals=2_400_000
-        ),
         name="feed",
-    )(scal, x, own, sib, vec, bias_in, *attn, *feed)
-
-
-def feed_back_kernel(n_pieces, rows, *refs):
-    scal, dy_ref, r1_ref, r2_ref, e_ref, gp_ref, own_ref, sib_ref, vec_ref = refs[:9]
-    attn = refs[9 : 9 + n_pieces]
-    feed = refs[9 + n_pieces : 9 + 2 * n_pieces]
-    at = 9 + 2 * n_pieces
+    )(scal, x, own, sib, vec, bias_in, w_all)
+
+
+def plain_forward(blocks, tokens, cot, small, meta, frequency, vectors):
+    n_layers = vectors.shape[0]
+    rows, width = tokens.shape
+    c, z = lax.axis_index("dp") % 2, lax.axis_index("mp")
+    w_all = lax.all_gather(blocks, "dp", axis=1, tiled=True)
+    w_all = jnp.swapaxes(lax.all_gather(w_all, "mp", axis=0, tiled=False), 0, 1)
+    small_all = lax.all_gather(small, "mp", axis=0, tiled=False)
+    own_z = jnp.stack([(z - 2 * c - k) % MP for k in range(2)]).astype(jnp.int32)
+    info = jnp.where(z // 2 == c, meta, core_swap(meta))
+    place = z % 2
+    quarters = [2 * c + place, 2 * (1 - c) + place, 2 * c + 1 - place, 2 * (1 - c) + 1 - place]
+    positions = jnp.concatenate(
+        [q * rows + jnp.arange(rows, dtype=jnp.int32) for q in quarters]
+    ).astype(F32)
+    slot = info[0, 0]
+    seq = jnp.where(positions >= slot, 1.0, 0.0) + jnp.where(positions >= 2.0 * slot, 1.0, 0.0)
+    place = positions - seq * slot
+    limit = jnp.where(seq == 0.0, info[1, 0], jnp.where(seq == 1.0, info[2, 0], info[3, 0]))
+    kcode = jnp.where(place < limit, seq, -1.0)
+    qcode = seq[: 2 * rows]
+    angles = place[:, None] * frequency
+    sign = jnp.where(jnp.arange(LANES) % HD < HD // 2, -1.0, 1.0)
+    cos, sin = jnp.cos(angles), jnp.sin(angles) * sign[None, :]
+    low = relayout(tokens)
+    stream = low.astype(F32)
+    states = []
+    for l in range(n_layers):
+        two = jnp.stack([low, pair_swap(low)])
+        others = core_swap(two)
+        x_full = jnp.stack([two[0], others[0], two[1], others[1]])
+        bias = jnp.stack(
+            [
+                lax.dynamic_index_in_dim(small_all, own_z[k], 0, False)[l : l + 1, : 5 * LANES]
+                for k in range(2)
+            ]
+        )
+        q, k, v, mixed, lse = attend(
+            own_z, x_full, bias, (cos, sin), qcode[:, None], kcode[None, :], w_all, 3 * l
+        )
+        other = core_swap(mixed[rows:])
+        stream, low, r1, r2, e, gp = feed_forward(
+            own_z,
+            stream,
+            mixed[:rows],
+            other,
+            vectors[l],
+            small_all[:, l : l + 1, 5 * LANES :],
+            w_all,
+            3 * l,
+        )
+        states.append((x_full, q, k, v, mixed, other, lse, r1, r2, e, gp))
+    return (w_all, relayout(cot), low, cos, sin, qcode[None, :], kcode[:, None]), states
+
+
+def feed_back_kernel(n_pieces, rows, chunk, *refs):
+    scal, dy_ref, r1_ref, r2_ref, e_ref, gp_ref, own_ref, sib_ref, vec_ref, w_all = refs[:10]
+    at = 10
     dr1_ref, dzown_ref, dzsib_ref, dvec_ref, dbin_ref = refs[at : at + 5]
     outs = 2 if n_pieces == 8 else 1
     grads = refs[at + 5 : at + 5 + outs]
     wo_ref, win_ref, wback_ref, df_ref, dft_ref, ht_ref, dw_ref, sems = refs[at + 5 + outs :]
     width = dy_ref.shape[1]
-    back_copies = start_pieces(
-        scal,
-        feed,
-        sems,
-        2 * n_pieces,
-        lambda piece, offset: (
-            piece.at[:, :, pl.ds(width, width)],
-            wback_ref.at[:, pl.ds(offset, rows), :],
-        ),
+    columns = [scal[n_pieces + k] for k in range(MP)]
+    first_z = scal[n_pieces + MP]
+
+    def fetch(source, target, base):
+        copies = [
+            pltpu.make_async_copy(source(columns[k]), target.at[k], sems.at[base + k])
+            for k in range(MP)
+        ]
+        for copy in copies:
+            copy.start()
+        return copies
+
+    back_copies = fetch(lambda z: w_all.at[chunk + 2, z], wback_ref, 0)
+    in_copies = fetch(lambda z: w_all.at[chunk + 1, z], win_ref, MP)
+    out_copies = fetch(
+        lambda z: w_all.at[chunk, z, :, pl.ds(4 * LANES, 2 * LANES)], wo_ref, 2 * MP
     )
-    in_copies = start_pieces(
-        scal,
-        feed,
-        sems,
-        n_pieces,
-        lambda piece, offset: (
-            piece.at[:, :, pl.ds(0, width)],
-            win_ref.at[:, pl.ds(offset, rows), :],
-        ),
-    )
-    out_copies = start_pieces(
-        scal,
-        attn,
-        sems,
-        0,
-        lambda piece, offset: (
-            piece.at[:, :, pl.ds(4 * LANES, 2 * LANES)],
-            wo_ref.at[:, pl.ds(offset, rows), :],
-        ),
-    )
-    first_z = scal[n_pieces]
     dy = dy_ref[...]
     n2, scale2 = norm_parts(r2_ref[...])
     dvec_ref[4:5, :] = jnp.sum(dy * n2, axis=0, keepdims=True)
@@ -514,12 +992,13 @@
 
     def one(z, _):
         de = nn(df_ref[...], wback_ref[z])
-        du = de * gp_ref[z].astype(F32)
+        at = scal[n_pieces + z]
+        du = de * gp_ref[at].astype(F32)
         dbin_ref[z] = jnp.sum(du, axis=0, keepdims=True)
         dub = du.astype(BF16)
         dr1_ref[...] += nt(dub, win_ref[z])
         dw_ref[z, :, 0:width] = nn(ht_ref[...], dub).astype(BF16)
-        dw_ref[z, :, width : 2 * width] = nn(dft_ref[...], e_ref[z]).astype(BF16)
+        dw_ref[z, :, width : 2 * width] = nn(dft_ref[...], e_ref[at]).astype(BF16)
         return 0
 
     lax.fori_loop(0, MP, one, 0)
@@ -558,16 +1037,14 @@
 PIECE_ORDER = (3, 0, 2, 1)
 
 
-def feed_back(scal, dy, r1, r2, e, gp, own, sib, vec, attn, feed):
+def feed_back(scal, prows, count, dy, r1, r2, e, gp, own, sib, vec, w_all, chunk):
     rows, width = dy.shape
-    count = len(attn)
-    prows = piece_rows(attn)
     lanes = 2 * width + 2 * LANES
     grads = (shape((4, MP, prows, lanes), BF16),) * 2
     if count != 8:
         grads = (shape((1, MP, prows, lanes), BF16),)
     return pl.pallas_call(
-        partial(feed_back_kernel, count, prows),
+        partial(feed_back_kernel, count, prows, chunk),
         out_shape=(
             shape((rows, width), F32),
             shape((rows, 512), BF16),
@@ -576,7 +1053,7 @@
             shape((MP, 1, width), F32),
             *grads,
         ),
-        in_specs=[smem()] + [vmem()] * 8 + [anywhere()] * (2 * count),
+        in_specs=[smem()] + [vmem()] * 8 + [anywhere()],
         out_specs=(vmem(),) * 5 + (anywhere(),) * len(grads),
         scratch_shapes=[
             pltpu.VMEM((MP, width, 2 * LANES), BF16),
@@ -586,17 +1063,17 @@
             pltpu.VMEM((width, rows), BF16),
             pltpu.VMEM((width, rows), BF16),
             pltpu.VMEM((MP, width, lanes), BF16),
-            pltpu.SemaphoreType.DMA((3 * count,)),
+            pltpu.SemaphoreType.DMA((3 * MP,)),
         ],
         compiler_params=params(),
         cost_estimate=pl.CostEstimate(
             flops=16_000_000_000, bytes_accessed=40_000_000, transcendentals=0
         ),
         name="feed_back",
-    )(scal, dy, r1, r2, e, gp, own, sib, vec, *attn, *feed)
-
-
-def attend_back_kernel(n_pieces, rows, *refs):
+    )(scal, dy, r1, r2, e, gp, own, sib, vec, w_all)
+
+
+def attend_back_kernel(n_pieces, chunk, *refs):
     (
         scal,
         x_ref,
@@ -611,9 +1088,9 @@
         dzown_ref,
         dzsib_ref,
         lse_ref,
-    ) = refs[:13]
-    pieces = refs[13 : 13 + n_pieces]
-    dx_ref, dxs_ref, dbias_ref, parts_ref = refs[13 + n_pieces : 17 + n_pieces]
+        w_all,
+    ) = refs[:14]
+    dx_ref, dxs_ref, dbias_ref, parts_ref = refs[14:18]
     (
         w_ref,
         xt_ref,
@@ -626,18 +1103,17 @@
         low_ref,
         sums_ref,
         sems,
-    ) = refs[17 + n_pieces :]
-    first_z = scal[n_pieces]
-    copies = start_pieces(
-        scal,
-        pieces,
-        sems,
-        0,
-        lambda piece, offset: (
-            piece.at[pl.ds(first_z, 2)],
-            w_ref.at[:, pl.ds(offset, rows), :],
-        ),
-    )
+    ) = refs[18:]
+    copies = [
+        pltpu.make_async_copy(
+            w_all.at[chunk, scal[n_pieces + 9 + k], :, pl.ds(0, 5 * LANES)],
+            w_ref.at[k],
+            sems.at[k],
+        )
+        for k in range(2)
+    ]
+    for copy in copies:
+        copy.start()
     keys, width = x_ref.shape
     queries = keys // 2
     block = queries // 2
@@ -739,7 +1215,7 @@
 
     flight = []
     for i in range(min(n_pieces, 4)):
-        offset = pl.multiple_of(scal[n_pieces + 1 + i], 32)
+        offset = pl.multiple_of(scal[n_pieces + 5 + i], 32)
         copy = pltpu.make_async_copy(
             dw_ref.at[:, pl.ds(offset, parts_ref.shape[2]), :],
             parts_ref.at[PIECE_ORDER[i] if n_pieces == 8 else 0],
@@ -751,28 +1227,27 @@
         copy.wait()
 
 
-def attend_back(scal, x_full, tables, saved, mixed, dz_own, dz_sib, pieces):
-    cos, sin, _, _, qcode, kcode = tables
+def attend_back(scal, prows, count, x_full, tables, saved, mixed, dz_own, dz_sib, w_all, chunk):
+    cos, sin, qcode, kcode = tables
     q, k, v, lse = saved
     keys, width = x_full.shape
     queries = keys // 2
     block = queries // 2
-    count = len(pieces)
-    parts = (4, 2, 2 * piece_rows(pieces), 5 * LANES)
+    parts = (4, 2, 2 * prows, 5 * LANES)
     if count != 8:
-        parts = (1, 2, piece_rows(pieces), 5 * LANES)
+        parts = (1, 2, prows, 5 * LANES)
     return pl.pallas_call(
-        partial(attend_back_kernel, count, piece_rows(pieces)),
+        partial(attend_back_kernel, count, chunk),
         out_shape=(
             shape((2, block, width), BF16),
             shape((2, block, width), BF16),
             shape((2, 1, 5 * LANES), F32),
             shape(parts, BF16),
         ),
-        in_specs=[smem()] + [vmem()] * 12 + [anywhere()] * count,
+        in_specs=[smem()] + [vmem()] * 12 + [anywhere()],
         out_specs=(vmem(),) * 3 + (anywhere(),),
         scratch_shapes=[
-            pltpu.VMEM((2, width, 6 * LANES), BF16),
+            pltpu.VMEM((2, width, 5 * LANES), BF16),
             pltpu.VMEM((width, keys), BF16),
             pltpu.VMEM((2, 2, queries, LANES), BF16),
             pltpu.VMEM((8, queries), F32),
@@ -782,14 +1257,14 @@
             pltpu.VMEM((2, width, 5 * LANES), BF16),
             pltpu.VMEM((keys, 5 * LANES), BF16),
             pltpu.VMEM((4, block, width), F32),
-            pltpu.SemaphoreType.DMA((count,)),
+            pltpu.SemaphoreType.DMA((4,)),
         ],
         compiler_params=params(),
         cost_estimate=pl.CostEstimate(
             flops=40_000_000_000, bytes_accessed=20_000_000, transcendentals=8_000_000
         ),
         name="attend_back",
-    )(scal, x_full, cos, sin, qcode, kcode, q, k, v, mixed, dz_own, dz_sib, lse, *pieces)
+    )(scal, x_full, cos, sin, qcode, kcode, q, k, v, mixed, dz_own, dz_sib, lse, w_all)
 
 
 def head_tiles(q, k, v, o):
@@ -815,24 +1290,6 @@
     return q, k, v
 
 
-def make_tables(positions, bucket, lengths):
-    slot = LEN_MAX // (3 - bucket)
-    sequence = positions // slot
-    place = positions - sequence * slot
-    limit = jnp.sum(
-        jnp.where(sequence[:, None] == jnp.arange(3)[None, :], lengths[None, :], 0), axis=1
-    )
-    lane = jnp.arange(LANES) % HD
-    frequency = 10000.0 ** (-2.0 * (lane % (HD // 2)).astype(F32) / HD)
-    angles = place.astype(F32)[:, None] * frequency[None, :]
-    sign = jnp.where(lane < HD // 2, -1.0, 1.0)
-    cos = jnp.cos(angles)
-    sin = jnp.sin(angles) * sign[None, :]
-    kcode = jnp.where(place < limit, sequence, -1).astype(F32)
-    qcode = sequence[: positions.shape[0] // 2].astype(F32)
-    return cos, sin, qcode[:, None], kcode[None, :], qcode[None, :], kcode[:, None]
-
-
 def per_device(
     tokens, w_qkv, b_qkv, w_out, vectors, w_in, b_in, w_back, cotangent, lengths, buckets
 ):
@@ -842,89 +1299,86 @@
     z = lax.axis_index("mp")
     g, c = d // 2, d % 2
 
-    gathered = []
-    for layer_at in range(layers):
-        low = w_qkv[layer_at].astype(BF16)
-        attn = head_tiles(low[0], low[1], low[2], w_out[layer_at].astype(BF16).T)
-        feed = jnp.concatenate(
-            [w_in[layer_at].astype(BF16), w_back[layer_at].astype(BF16).T], axis=-1
-        )
-        gathered.append((gather_bundle(attn), gather_bundle(feed)))
-    piece_height = w_qkv.shape[2]
-    offsets = row_offsets(g, c, piece_height)
-    first = jnp.where(c == 0, 1, 2)
-    spans = [(g ^ hop) * 2 * piece_height for hop in (0, first, 3 - first, 3)]
-    if len(offsets) == 1:
-        spans = [jnp.int32(0)] * 4
-    scal = jnp.stack(offsets + [2 * c] + spans).astype(jnp.int32)
-
-    zero = jnp.zeros((layers, LANES // 2), F32)
-    v_bias = b_qkv[:, 2]
-    bias_tiles = jnp.concatenate(
+    blocks = []
+    for l in range(layers):
+        low = w_qkv[l].astype(BF16)
+        blocks.append(head_tiles(low[0], low[1], low[2], w_out[l].astype(BF16).T))
+        blocks.append(w_in[l].astype(BF16))
+        blocks.append(w_back[l].astype(BF16).T)
+    blocks = jnp.stack(blocks)
+    height = w_qkv.shape[2]
+    pieces = 8 if lax.axis_size("dp") == 8 else 1
+    piece_rows = height if pieces == 8 else width
+
+    small = jnp.concatenate(
         [
             b_qkv[:, 0],
             b_qkv[:, 1, LANES:],
             b_qkv[:, 1, :LANES],
-            v_bias,
-            zero,
+            b_qkv[:, 2],
+            jnp.zeros((layers, HD), F32),
+            b_in,
         ],
         axis=-1,
     )
-    small = gather_small(jnp.concatenate([bias_tiles, b_in], axis=-1))
-    bias_all = small[:, :, : 5 * LANES]
-    bias_in_all = small[:, :, 5 * LANES :]
-
-    meta = jnp.concatenate([buckets, lengths[0]])
-    other_meta = core_swap(meta)
-    half = z // 2
-    meta = jnp.where(half == c, meta, other_meta)
-    place = z % 2
-    quarters = [2 * c + place, 2 * (1 - c) + place, 2 * c + 1 - place, 2 * (1 - c) + 1 - place]
-    positions = jnp.concatenate([q * rows + jnp.arange(rows, dtype=jnp.int32) for q in quarters])
-    tables = make_tables(positions, meta[0], meta[1:])
-
-    tokens = relayout(tokens)
-    low = tokens
-    stream = tokens.astype(F32)
-    states = []
-    for layer_at in range(layers):
-        attn, feed = gathered[layer_at]
-        two = jnp.stack([low, pair_swap(low)])
-        others = core_swap(two)
-        x_full = jnp.concatenate([two[0], others[0], two[1], others[1]], axis=0)
-        bias = lax.dynamic_slice_in_dim(bias_all[:, layer_at], 2 * c, 2, 0)[:, None, :]
-        q, k, v, mixed, mixed_sib, lse = attend(scal, x_full, bias, tables, attn)
-        others_mixed = core_swap(mixed_sib)
-        own_mixed = mixed[:rows]
-        stream, low, r1, r2, e, gp = feed_forward(
-            scal,
-            stream,
-            own_mixed,
-            others_mixed,
-            vectors[layer_at],
-            bias_in_all[:, layer_at][:, None, :],
-            attn,
-            feed,
-        )
-        states.append((x_full, (q, k, v, lse), mixed, own_mixed, others_mixed, r1, r2, e, gp))
+    small = jnp.pad(small, ((0, 8 - layers), (0, 0)))
+    slot = LEN_MAX // (3 - buckets)
+    meta = jnp.concatenate([slot, lengths[0]]).astype(F32)
+    meta = jnp.broadcast_to(jnp.pad(meta, (0, 4))[:, None], (8, LANES))
+    exponents = jnp.arange(LANES, dtype=jnp.int32) % (HD // 2)
+    frequency = 10000.0 ** (-2.0 * exponents.astype(F32) / HD)[None, :]
+
+    run = forward if pieces == 8 else plain_forward
+    head, states = run(blocks, tokens, cotangent, small, meta, frequency, vectors)
+    w_all, gradient, low, cos, sin, qcode, kcode = head
     result = relayout(low)
-
-    gradient = relayout(cotangent).astype(F32)
+    gradient = gradient.astype(F32)
+
+    first = jnp.where(c == 0, 1, 2)
+    spans = [(g ^ hop) * 2 * height for hop in (0, first, 3 - first, 3)]
+    if pieces == 1:
+        spans = [jnp.int32(0)] * 4
+    column_of = [(z - k) % MP for k in range(MP)]
+    own_z = [(z - 2 * c - k) % MP for k in range(2)]
+    scal = jnp.stack(row_offsets(g, c, height) + column_of + [2 * c] + spans + own_z)
+    scal = scal.astype(jnp.int32)
+
     masters = []
     vector_grads = []
     in_biases = []
     head_biases = []
     for layer_at in reversed(range(layers)):
-        attn, feed = gathered[layer_at]
-        x_full, saved, mixed, own_mixed, others_mixed, r1, r2, e, gp = states[layer_at]
+        x_full, q, k, v, mixed, mixed_in, lse, r1, r2, e, gp = states[layer_at]
         back = feed_back(
-            scal, gradient, r1, r2, e, gp, own_mixed, others_mixed, vectors[layer_at], attn, feed
+            scal,
+            piece_rows,
+            pieces,
+            gradient,
+            r1,
+            r2,
+            e,
+            gp,
+            mixed[:rows],
+            mixed_in,
+            vectors[layer_at],
+            w_all,
+            3 * layer_at,
         )
         dr1, dz_own, dz_sib, dvec, dbin = back[:5]
         dz_others = core_swap(dz_sib)
         feed_grad = reduce_all(back[5], back[-1])
         dx, dx_sib, dbias, parts = attend_back(
-            scal, x_full, tables, saved, mixed, dz_own, dz_others, attn
+            scal,
+            piece_rows,
+            pieces,
+            x_full.reshape(4 * rows, width),
+            (cos, sin, qcode, kcode),
+            (q, k, v, lse),
+            mixed,
+            dz_own,
+            dz_others,
+            w_all,
+            3 * layer_at,
         )
         got = dx.astype(F32) + core_swap(dx_sib).astype(F32)
         gradient = dr1 + got[0] + pair_swap(got[1].astype(BF16)).astype(F32)

time: 705 us -> 577 us (0.82)
  waiting for transfers between devices: 284 us -> 122 us
  Pallas kernels: 211 us -> 309 us
  starting transfers between devices: 111 us -> 78.3 us
  other arithmetic: 59.4 us -> 37 us
  local copies, waits for them, and re-layouts: 27 us -> 19.3 us
    pallas_call x8 -> x5, Pallas kernels: 211 us -> 309 us  [the longest x1 181 us: forward(): pl.pallas_call(partial(forward_kernel, n_layers), out_shape=outs, in_spec...]
    ppermute x26 -> x14, waiting for transfers between devices: 148 us -> 68.4 us  [plane_swap(): return lax.ppermute(x, 'dp', [(i, i ^ hops[i % 2]) for i in range(n)])]
    ppermute x24 -> x9, waiting for transfers between devices: 97.7 us -> 37.8 us  [column_shift(): return lax.ppermute(x, 'mp', [(i, (i + k) % MP) for i in range(MP)])]
    ppermute x24 -> x9, starting transfers between devices: 53.1 us -> 20.9 us  [column_shift(): return lax.ppermute(x, 'mp', [(i, (i + k) % MP) for i in range(MP)])]
    ppermute x8, waiting for transfers between devices: 34.6 us -> 11.8 us  [column_turn(): return lax.ppermute(x, ('dp', 'mp'), pairs)]
    ppermute x32 -> x11, starting transfers between devices: 10.1 us -> 26.3 us  [core_swap(): return lax.ppermute(x, 'dp', [(i, i ^ 1) for i in range(n)])]
    ppermute x26 -> x14, starting transfers between devices: 30.2 us -> 14.7 us  [plane_swap(): return lax.ppermute(x, 'dp', [(i, i ^ hops[i % 2]) for i in range(n)])]
    mul x2 -> x0, other arithmetic: 12.7 us -> none  [the longest x1 8.39 us: make_tables(): place = positions - sequence * slot]
  transfers between devices with their start and end apart: 98 -> 46, of which waited for: 37 -> 19; matrix products, arithmetic and copies ran while one was open for 10% -> 7% of each run, Pallas kernels for 19% -> 11%
where the time goes in v2:
time: 577 us; the launch traced here: 569 us
  Pallas kernels  309 us (54%)
  waiting for transfers between devices  122 us (21%)
  starting transfers between devices  78.3 us (14%)
  other arithmetic  37 us (6%)
  local copies, waits for them, and re-layouts  19.3 us (3%)
    pallas_call x1, Pallas kernels, forward(): pl.pallas_call(partial(forward_kernel, n_layers), out_shape=outs, in_spec...  181 us
    pallas_call x2, Pallas kernels, attend_back(): pl.pallas_call(partial(attend_back_kernel, count, chunk), out_shape=(shap...  78.5 us
    ppermute x14, waiting for transfers between devices, plane_swap(): return lax.ppermute(x, 'dp', [(i, i ^ hops[i % 2]) for i in range(n)])  68.4 us
    pallas_call x2, Pallas kernels, feed_back(): pl.pallas_call(partial(feed_back_kernel, count, prows, chunk), out_shape=...  50.1 us
    ppermute x9, waiting for transfers between devices, column_shift(): return lax.ppermute(x, 'mp', [(i, (i + k) % MP) for i in range(MP)])  37.8 us
    ppermute x11, starting transfers between devices, core_swap(): return lax.ppermute(x, 'dp', [(i, i ^ 1) for i in range(n)])  26.3 us
    ppermute x9, starting transfers between devices, column_shift(): return lax.ppermute(x, 'mp', [(i, (i + k) % MP) for i in range(MP)])  20.9 us
    ppermute x14, starting transfers between devices, plane_swap(): return lax.ppermute(x, 'dp', [(i, i ^ hops[i % 2]) for i in range(n)])  14.7 us
  transfers between devices with their start and end apart: 46, of which 19 were waited for; matrix products, arithmetic and copies ran while one was open for 7% of the time, Pallas kernels for 11%

profile of v2, /device:TPU:0, one launch (start us, length us, event | category | flops | bytes accessed | tf_op | source)
XLA Modules:
  0.0 568.9 jit_solution(16694288855549021469)
XLA Ops:
  7.1 180.5 %forward.1 = (bf16[6,4,768,768]{3,2,1,0:T(8,128)(2,1)}, bf16[384,768]{1,0:T(8,128)(2,1)}, bf16[384,768]{1,0:T(8,128)(2,1)}, f32[1536,128]{1,0:T(8,128)}, f32[153...) custom-call(bf16[6,96,768]{2,1,0:T(8,128)(2,1)} %copy-done.10, ...), custom_call_target="tpu_custom_call" | custom-call | flops 99999997952 | bytes 100000000 | tf_op jit(solution)/shard_map/forward/pallas_call | solution.py:708
  189.4 2.2 convert_element_type.298.refs_1_
  192.1 25.0 %feed_back.2 = (f32[384,768]{1,0:T(8,128)}, bf16[384,512]{1,0:T(8,128)(2,1)}, bf16[384,512]{1,0:T(8,128)(2,1)}, f32[6,768]{1,0:T(8,128)}, f32[4,1,768]{2,1,0:T(1...) custom-call(s32[19]{0:T(128)} %stack.209.refs_0_, f32[384,768]{1,0:T(8,128)} %convert_element_type.298.refs_1_, ...), custom_call_target="tpu_custom_call" | custom-call | flops 16000000000 | bytes 40000000 | tf_op jit(solution)/shard_map/feed_back/pallas_call | solution.py:1046
  220.0 39.1 %attend_back.2 = (bf16[2,384,768]{2,1,0:T(8,128)(2,1)}, bf16[2,384,768]{2,1,0:T(8,128)(2,1)}, f32[2,1,640]{2,1,0:T(1,128)}, bf16[4,2,192,640]{3,2,1,0:T(8,128)(2,1)}) custom-call(s32[19]{0:T(128)} %stack.209.refs_0_, bf16[1536,768]{1,0:T(8,128)(2,1)} %bitcast.218, f32[1536,128]{1,0:T(8,128)} %get-tuple-element.71.refs_2_, ...), custom_call_target="tpu_custom_call" | custom-call | flops 40000000000 | bytes 20000000 | tf_op jit(solution)/shard_map/attend_back/pallas_call | solution.py:1239
  259.6 2.7 collective-permute-done.2
  266.6 2.4 collective-permute-done.23
  270.3 2.4 collective-permute-done.24
  273.4 2.9 collective-permute-start.26
  276.3 4.4 collective-permute-done.26
  281.2 5.9 %collective-permute-start = (bf16[384,768]{1,0:T(8,128)(2,1)}, bf16[384,768]{1,0:T(8,128)(2,1)}, u32[]{:S(2)}, u32[]{:S(2)}) collective-permute-start(bf16[384,768]{1,0:T(8,128)(2,1)} %get-tuple-element.60), channel_id=1, source_target_pairs={{0,0},{1,1},{2,4},{3,5},{4,2},{5,3},{6,6},{7,7},{8,8},{9,9},{10,12... | collective-permute-start | bytes 1769480 | tf_op jit(solution)/shard_map/ppermute | solution.py:57
  288.9 2.3 slice.407
  291.2 2.3 collective-permute-start.13
  294.2 2.3 fusion.8.refs_1_
  296.5 25.2 %feed_back.3 = (f32[384,768]{1,0:T(8,128)}, bf16[384,512]{1,0:T(8,128)(2,1)}, bf16[384,512]{1,0:T(8,128)(2,1)}, f32[6,768]{1,0:T(8,128)}, f32[4,1,768]{2,1,0:T(1...) custom-call(s32[19]{0:T(128)} %stack.209.refs_0_, f32[384,768]{1,0:T(8,128)} %fusion.8.refs_1_, ...), custom_call_target="tpu_custom_call" | custom-call | flops 16000000000 | bytes 40000000 | tf_op jit(solution)/shard_map/feed_back/pallas_call | solution.py:1046
  327.8 39.4 %attend_back.3 = (bf16[2,384,768]{2,1,0:T(8,128)(2,1)}, bf16[2,384,768]{2,1,0:T(8,128)(2,1)}, f32[2,1,640]{2,1,0:T(1,128)}, bf16[4,2,192,640]{3,2,1,0:T(8,128)(2,1)}) custom-call(s32[19]{0:T(128)} %stack.209.refs_0_, bf16[1536,768]{1,0:T(8,128)(2,1)} %bitcast.217, f32[1536,128]{1,0:T(8,128)} %get-tuple-element.71.refs_2_, ...), custom_call_target="tpu_custom_call" | custom-call | flops 40000000000 | bytes 20000000 | tf_op jit(solution)/shard_map/attend_back/pallas_call | solution.py:1239
  379.6 3.8 collective-permute-done.16
  386.6 5.9 %collective-permute-start.5 = (bf16[2,384,768]{2,1,0:T(8,128)(2,1)}, bf16[2,384,768]{2,1,0:T(8,128)(2,1)}, u32[]{:S(2)}, u32[]{:S(2)}) collective-permute-start(bf16[2,384,768]{2,1,0:T(8,128)(2,1)} %get-tuple-element.98), channel_id=1, source_target_pairs={{0,4},{4,0},{8,12},{12,8},{16,20},{20,16},{24,28},{28,24},{1,5},{5... | collective-permute-start | bytes 3538952 | tf_op jit(solution)/shard_map/ppermute | solution.py:31
  393.5 3.5 collective-permute-done.21
  401.1 7.2 %collective-permute-start.22 = (f32[640]{0:T(1024)S(1)}, f32[640]{0:T(1024)}, u32[]{:S(2)}, u32[]{:S(2)}) collective-permute-start(f32[640]{0:T(1024)S(1)} %add.291), channel_id=1, source_target_pairs={{0,4},{4,0},{8,12},{12,8},{16,20},{20,16},{24,28},{28,24},{1,5},{5... | collective-permute-start | bytes 7688 | tf_op jit(solution)/shard_map/ppermute | solution.py:31
  414.3 3.3 add_convert_fusion.2
  418.1 2.8 collective-permute-done.9
  422.2 2.6 add_convert_fusion.5
  426.0 2.1 collective-permute-start.11
  428.8 11.0 %collective-permute-start.17 = (bf16[96,640]{1,0:T(8,128)(2,1)S(1)}, bf16[96,640]{1,0:T(8,128)(2,1)S(1)}, u32[]{:S(2)}, u32[]{:S(2)}) collective-permute-start(bf16[96,640]{1,0:T(8,128)(2,1)S(1)} %copy-done.7), channel_id=1, source_target_pairs={{0,4},{4,0},{8,12},{12,8},{16,20},{20,16},{24,28},{28,24},{1,5},{5... | collective-permute-start | bytes 368648 | tf_op jit(solution)/shard_map/ppermute | solution.py:31
  441.5 9.5 %collective-permute-done.35 = bf16[2,4,96,1792]{3,2,1,0:T(8,128)(2,1)S(1)} collective-permute-done((bf16[2,4,96,1792]{3,2,1,0:T(8,128)(2,1)S(1)}, bf16[2,4,96,1792]{3,2,1,0:T(8,128)(2,1)S(1)}, u32[]{:S(2)}, u32[]{:S(2)}) %collective-permute-start.35) | collective-permute-done | bytes 2752544 | tf_op jit(solution)/shard_map/ppermute | solution.py:37
  454.3 40.9 %collective-permute-done.29 = bf16[2,4,96,1792]{3,2,1,0:T(8,128)(2,1)S(1)} collective-permute-done((bf16[2,4,96,1792]{3,2,1,0:T(8,128)(2,1)S(1)}, bf16[2,4,96,1792]{3,2,1,0:T(8,128)(2,1)S(1)}, u32[]{:S(2)}, u32[]{:S(2)}) %collective-permute-start.29) | collective-permute-done | bytes 2752544 | tf_op jit(solution)/shard_map/ppermute | solution.py:37
  502.4 2.1 collective-permute-start.37
  507.1 8.3 %collective-permute-done.30 = bf16[4,96,1792]{2,1,0:T(8,128)(2,1)S(1)} collective-permute-done((bf16[4,96,1792]{2,1,0:T(8,128)(2,1)S(1)}, bf16[4,96,1792]{2,1,0:T(8,128)(2,1)S(1)}, u32[]{:S(2)}, u32[]{:S(2)}) %collective-permute-start.30) | collective-permute-done | bytes 1376288 | tf_op jit(solution)/shard_map/ppermute | solution.py:37
  517.6 2.1 collective-permute-start.31
  521.1 8.5 %collective-permute-start.33 = (bf16[96,1792]{1,0:T(8,128)(2,1)S(1)}, bf16[96,1792]{1,0:T(8,128)(2,1)S(1)}, u32[]{:S(2)}, u32[]{:S(2)}) collective-permute-start(bf16[96,1792]{1,0:T(8,128)(2,1)S(1)} %get-tuple-element.138), channel_id=1, source_target_pairs={{0,1},{1,2},{2,3},{3,0},{4,5},{5,6},{6,7},{7,4},{8,9},{9,10},{10,1... | collective-permute-start | bytes 1032200 | tf_op jit(solution)/shard_map/ppermute | solution.py:41
  529.6 22.2 %collective-permute-done.38 = bf16[96,1792]{1,0:T(8,128)(2,1)S(1)} collective-permute-done((bf16[96,1792]{1,0:T(8,128)(2,1)S(1)}, bf16[96,1792]{1,0:T(8,128)(2,1)S(1)}, u32[]{:S(2)}, u32[]{:S(2)}) %collective-permute-start.38) | collective-permute-done | bytes 344096 | tf_op jit(solution)/shard_map/ppermute | solution.py:41
  552.1 11.7 %collective-permute-done.32 = bf16[96,1792]{1,0:T(8,128)(2,1)S(1)} collective-permute-done((bf16[96,1792]{1,0:T(8,128)(2,1)S(1)}, bf16[96,1792]{1,0:T(8,128)(2,1)S(1)}, u32[]{:S(2)}, u32[]{:S(2)}) %collective-permute-start.32) | collective-permute-done | bytes 344096 | tf_op jit(solution)/shard_map/ppermute | solution.py:41
  (242 shorter events, 79.4 us)
Async XLA Ops:
  264.7 29.4 %collective-permute-start.3 = (bf16[384,768]{1,0:T(8,128)(2,1)}, bf16[384,768]{1,0:T(8,128)(2,1)}, u32[]{:S(2)}, u32[]{:S(2)}) collective-permute-start(bf16[384,768]{1,0:T(8,128)(2,1)} %fusion.15), channel_id=1, source_target_pairs={{0,1},{1,0},{2,3},{3,2},{4,5},{5,4},{6,7},{7,6},{8,9},{9,8},{10,11... | collective-permute-start | bytes 1769480 | tf_op jit(solution)/shard_map/ppermute | solution.py:45
  273.4 7.3 %collective-permute-start.26 = (f32[640]{0:T(1024)S(1)}, f32[640]{0:T(1024)S(1)}, u32[]{:S(2)}, u32[]{:S(2)}) collective-permute-start(f32[640]{0:T(1024)S(1)} %get-tuple-element.131), channel_id=1, source_target_pairs={{0,3},{1,0},{2,1},{3,2},{4,5},{5,6},{6,7},{7,4},{8,11},{9,8},{10,9... | collective-permute-start | bytes 7688 | tf_op jit(solution)/shard_map/ppermute | solution.py:141
  280.7 12.9 %collective-permute-start.27 = (f32[640]{0:T(1024)S(1)}, f32[640]{0:T(1024)S(1)}, u32[]{:S(2)}, u32[]{:S(2)}) collective-permute-start(f32[640]{0:T(1024)S(1)} %add.295), channel_id=1, source_target_pairs={{0,4},{4,0},{8,12},{12,8},{16,20},{20,16},{24,28},{28,24},{1,5},{5... | collective-permute-start | bytes 7688 | tf_op jit(solution)/shard_map/ppermute | solution.py:31
  281.2 133.1 %collective-permute-start.34 = (bf16[4,4,96,1792]{3,2,1,0:T(8,128)(2,1)}, bf16[4,4,96,1792]{3,2,1,0:T(8,128)(2,1)}, u32[]{:S(2)}, u32[]{:S(2)}) collective-permute-start(bf16[4,4,96,1792]{3,2,1,0:T(8,128)(2,1)} %get-tuple-element.106), channel_id=1, source_target_pairs={{0,4},{4,0},{8,12},{12,8},{16,20},{20,16},{24,28},{28,24},{1,5},{5... | collective-permute-start | bytes 16515080 | tf_op jit(solution)/shard_map/ppermute | solution.py:31
  281.2 96.0 %collective-permute-start = (bf16[384,768]{1,0:T(8,128)(2,1)}, bf16[384,768]{1,0:T(8,128)(2,1)}, u32[]{:S(2)}, u32[]{:S(2)}) collective-permute-start(bf16[384,768]{1,0:T(8,128)(2,1)} %get-tuple-element.60), channel_id=1, source_target_pairs={{0,0},{1,1},{2,4},{3,5},{4,2},{5,3},{6,6},{7,7},{8,8},{9,9},{10,12... | collective-permute-start | bytes 1769480 | tf_op jit(solution)/shard_map/ppermute | solution.py:57
  291.2 32.5 %collective-permute-start.13 = (bf16[2,2,192,640]{3,2,1,0:T(8,128)(2,1)}, bf16[2,2,192,640]{3,2,1,0:T(8,128)(2,1)}, u32[]{:S(2)}, u32[]{:S(2)}) collective-permute-start(bf16[2,2,192,640]{3,2,1,0:T(8,128)(2,1)} %slice.407), channel_id=1, source_target_pairs={{0,8},{4,20},{8,0},{12,28},{16,24},{20,4},{24,16},{28,12},{1,9},{5... | collective-permute-start | bytes 2949128 | tf_op jit(solution)/shard_map/ppermute | solution.py:37
  325.1 43.0 %collective-permute-start.14 = (bf16[2,192,640]{2,1,0:T(8,128)(2,1)S(1)}, bf16[2,192,640]{2,1,0:T(8,128)(2,1)S(1)}, u32[]{:S(2)}, u32[]{:S(2)}) collective-permute-start(bf16[2,192,640]{2,1,0:T(8,128)(2,1)S(1)} %fusion.18), channel_id=1, source_target_pairs={{0,16},{4,12},{8,24},{12,4},{16,0},{20,28},{24,8},{28,20},{1,17},{... | collective-permute-start | bytes 1474568 | tf_op jit(solution)/shard_map/ppermute | solution.py:37
  325.3 96.8 %collective-permute-start.28 = (bf16[4,4,96,1792]{3,2,1,0:T(8,128)(2,1)}, bf16[4,4,96,1792]{3,2,1,0:T(8,128)(2,1)}, u32[]{:S(2)}, u32[]{:S(2)}) collective-permute-start(bf16[4,4,96,1792]{3,2,1,0:T(8,128)(2,1)} %get-tuple-element.104), channel_id=1, source_target_pairs={{0,4},{4,0},{8,12},{12,8},{16,20},{20,16},{24,28},{28,24},{1,5},{5... | collective-permute-start | bytes 16515080 | tf_op jit(solution)/shard_map/ppermute | solution.py:31
  326.1 44.0 %collective-permute-start.41 = (f32[20,768]{1,0:T(8,128)S(1)}, f32[20,768]{1,0:T(8,128)S(1)}, u32[]{:S(2)}, u32[]{:S(2)}) collective-permute-start(f32[20,768]{1,0:T(8,128)S(1)} %fusion.28), channel_id=1, source_target_pairs={{0,8},{4,20},{8,0},{12,28},{16,24},{20,4},{24,16},{28,12},{1,9},{5... | collective-permute-start | bytes 184328 | tf_op jit(solution)/shard_map/ppermute | solution.py:37
  370.1 4.4 collective-permute-start.42
  376.1 7.4 %collective-permute-start.16 = (bf16[192,640]{1,0:T(8,128)(2,1)S(1)}, bf16[192,640]{1,0:T(8,128)(2,1)S(1)}, u32[]{:S(2)}, u32[]{:S(2)}) collective-permute-start(bf16[192,640]{1,0:T(8,128)(2,1)S(1)} %get-tuple-element.150), channel_id=1, source_target_pairs={{0,3},{1,0},{2,1},{3,2},{4,5},{5,6},{6,7},{7,4},{8,11},{9,8},{10,9... | collective-permute-start | bytes 737288 | tf_op jit(solution)/shard_map/ppermute | solution.py:141
  377.2 9.4 %collective-permute-start.43 = (f32[14,768]{1,0:T(8,128)S(1)}, f32[14,768]{1,0:T(8,128)S(1)}, u32[]{:S(2)}, u32[]{:S(2)}) collective-permute-start(f32[14,768]{1,0:T(8,128)S(1)} %get-tuple-element.166), channel_id=1, source_target_pairs={{0,1},{1,2},{2,3},{3,0},{4,5},{5,6},{6,7},{7,4},{8,9},{9,10},{10,1... | collective-permute-start | bytes 129032 | tf_op jit(solution)/shard_map/ppermute | solution.py:41
  378.3 14.4 %collective-permute-start.44 = (f32[14,768]{1,0:T(8,128)S(1)}, f32[14,768]{1,0:T(8,128)S(1)}, u32[]{:S(2)}, u32[]{:S(2)}) collective-permute-start(f32[14,768]{1,0:T(8,128)S(1)} %get-tuple-element.167), channel_id=1, source_target_pairs={{0,2},{1,3},{2,0},{3,1},{4,6},{5,7},{6,4},{7,5},{8,10},{9,11},{10,... | collective-permute-start | bytes 129032 | tf_op jit(solution)/shard_map/ppermute | solution.py:41
  383.4 26.9 %collective-permute-start.8 = (bf16[2,2,192,640]{3,2,1,0:T(8,128)(2,1)S(1)}, bf16[2,2,192,640]{3,2,1,0:T(8,128)(2,1)}, u32[]{:S(2)}, u32[]{:S(2)}) collective-permute-start(bf16[2,2,192,640]{3,2,1,0:T(8,128)(2,1)S(1)} %slice.398), channel_id=1, source_target_pairs={{0,8},{4,20},{8,0},{12,28},{16,24},{20,4},{24,16},{28,12},{1,9},{5... | collective-permute-start | bytes 2949128 | tf_op jit(solution)/shard_map/ppermute | solution.py:37
  386.6 25.7 %collective-permute-start.5 = (bf16[2,384,768]{2,1,0:T(8,128)(2,1)}, bf16[2,384,768]{2,1,0:T(8,128)(2,1)}, u32[]{:S(2)}, u32[]{:S(2)}) collective-permute-start(bf16[2,384,768]{2,1,0:T(8,128)(2,1)} %get-tuple-element.98), channel_id=1, source_target_pairs={{0,4},{4,0},{8,12},{12,8},{16,20},{20,16},{24,28},{28,24},{1,5},{5... | collective-permute-start | bytes 3538952 | tf_op jit(solution)/shard_map/ppermute | solution.py:31
  397.0 4.1 collective-permute-start.45
  401.1 8.4 %collective-permute-start.22 = (f32[640]{0:T(1024)S(1)}, f32[640]{0:T(1024)}, u32[]{:S(2)}, u32[]{:S(2)}) collective-permute-start(f32[640]{0:T(1024)S(1)} %add.291), channel_id=1, source_target_pairs={{0,4},{4,0},{8,12},{12,8},{16,20},{20,16},{24,28},{28,24},{1,5},{5... | collective-permute-start | bytes 7688 | tf_op jit(solution)/shard_map/ppermute | solution.py:31
  411.5 9.4 %collective-permute-start.9 = (bf16[2,192,640]{2,1,0:T(8,128)(2,1)S(1)}, bf16[2,192,640]{2,1,0:T(8,128)(2,1)S(1)}, u32[]{:S(2)}, u32[]{:S(2)}) collective-permute-start(bf16[2,192,640]{2,1,0:T(8,128)(2,1)S(1)} %fusion.17), channel_id=1, source_target_pairs={{0,16},{4,12},{8,24},{12,4},{16,0},{20,28},{24,8},{28,20},{1,17},{... | collective-permute-start | bytes 1474568 | tf_op jit(solution)/shard_map/ppermute | solution.py:37
  414.2 25.8 %collective-permute-start.6 = (bf16[384,768]{1,0:T(8,128)(2,1)S(1)}, bf16[384,768]{1,0:T(8,128)(2,1)S(1)}, u32[]{:S(2)}, u32[]{:S(2)}) collective-permute-start(bf16[384,768]{1,0:T(8,128)(2,1)S(1)} %fusion.16), channel_id=1, source_target_pairs={{0,1},{1,0},{2,3},{3,2},{4,5},{5,4},{6,7},{7,6},{8,9},{9,8},{10,11... | collective-permute-start | bytes 1769480 | tf_op jit(solution)/shard_map/ppermute | solution.py:45
  417.9 33.1 %collective-permute-start.35 = (bf16[2,4,96,1792]{3,2,1,0:T(8,128)(2,1)S(1)}, bf16[2,4,96,1792]{3,2,1,0:T(8,128)(2,1)S(1)}, u32[]{:S(2)}, u32[]{:S(2)}) collective-permute-start(bf16[2,4,96,1792]{3,2,1,0:T(8,128)(2,1)S(1)} %pad_maximum_fusion.1), channel_id=1, source_target_pairs={{0,8},{4,20},{8,0},{12,28},{16,24},{20,4},{24,16},{28,12},{1,9},{5... | collective-permute-start | bytes 8257544 | tf_op jit(solution)/shard_map/ppermute | solution.py:37
  425.1 70.1 %collective-permute-start.29 = (bf16[2,4,96,1792]{3,2,1,0:T(8,128)(2,1)S(1)}, bf16[2,4,96,1792]{3,2,1,0:T(8,128)(2,1)S(1)}, u32[]{:S(2)}, u32[]{:S(2)}) collective-permute-start(bf16[2,4,96,1792]{3,2,1,0:T(8,128)(2,1)S(1)} %pad_maximum_fusion), channel_id=1, source_target_pairs={{0,8},{4,20},{8,0},{12,28},{16,24},{20,4},{24,16},{28,12},{1,9},{5... | collective-permute-start | bytes 8257544 | tf_op jit(solution)/shard_map/ppermute | solution.py:37
  426.0 13.8 %collective-permute-start.11 = (bf16[192,640]{1,0:T(8,128)(2,1)S(1)}, bf16[192,640]{1,0:T(8,128)(2,1)S(1)}, u32[]{:S(2)}, u32[]{:S(2)}) collective-permute-start(bf16[192,640]{1,0:T(8,128)(2,1)S(1)} %get-tuple-element.148), channel_id=1, source_target_pairs={{0,3},{1,0},{2,1},{3,2},{4,5},{5,6},{6,7},{7,4},{8,11},{9,8},{10,9... | collective-permute-start | bytes 737288 | tf_op jit(solution)/shard_map/ppermute | solution.py:141
  428.8 12.3 %collective-permute-start.17 = (bf16[96,640]{1,0:T(8,128)(2,1)S(1)}, bf16[96,640]{1,0:T(8,128)(2,1)S(1)}, u32[]{:S(2)}, u32[]{:S(2)}) collective-permute-start(bf16[96,640]{1,0:T(8,128)(2,1)S(1)} %copy-done.7), channel_id=1, source_target_pairs={{0,4},{4,0},{8,12},{12,8},{16,20},{20,16},{24,28},{28,24},{1,5},{5... | collective-permute-start | bytes 368648 | tf_op jit(solution)/shard_map/ppermute | solution.py:31
  440.2 59.0 %collective-permute-start.7 = (bf16[384,768]{1,0:T(8,128)(2,1)S(1)}, bf16[384,768]{1,0:T(8,128)(2,1)S(1)}, u32[]{:S(2)}, u32[]{:S(2)}) collective-permute-start(bf16[384,768]{1,0:T(8,128)(2,1)S(1)} %fusion.6), channel_id=1, source_target_pairs={{0,0},{1,1},{2,4},{3,5},{4,2},{5,3},{6,6},{7,7},{8,8},{9,9},{10,12... | collective-permute-start | bytes 1769480 | tf_op jit(solution)/shard_map/ppermute | solution.py:57
  452.8 47.5 %collective-permute-start.36 = (bf16[4,96,1792]{2,1,0:T(8,128)(2,1)S(1)}, bf16[4,96,1792]{2,1,0:T(8,128)(2,1)S(1)}, u32[]{:S(2)}, u32[]{:S(2)}) collective-permute-start(bf16[4,96,1792]{2,1,0:T(8,128)(2,1)S(1)} %fusion.3), channel_id=1, source_target_pairs={{0,16},{4,12},{8,24},{12,4},{16,0},{20,28},{24,8},{28,20},{1,17},{... | collective-permute-start | bytes 4128776 | tf_op jit(solution)/shard_map/ppermute | solution.py:37
  497.1 18.4 %collective-permute-start.30 = (bf16[4,96,1792]{2,1,0:T(8,128)(2,1)S(1)}, bf16[4,96,1792]{2,1,0:T(8,128)(2,1)S(1)}, u32[]{:S(2)}, u32[]{:S(2)}) collective-permute-start(bf16[4,96,1792]{2,1,0:T(8,128)(2,1)S(1)} %fusion.2), channel_id=1, source_target_pairs={{0,16},{4,12},{8,24},{12,4},{16,0},{20,28},{24,8},{28,20},{1,17},{... | collective-permute-start | bytes 4128776 | tf_op jit(solution)/shard_map/ppermute | solution.py:37
  502.4 18.6 %collective-permute-start.37 = (bf16[96,1792]{1,0:T(8,128)(2,1)S(1)}, bf16[96,1792]{1,0:T(8,128)(2,1)S(1)}, u32[]{:S(2)}, u32[]{:S(2)}) collective-permute-start(bf16[96,1792]{1,0:T(8,128)(2,1)S(1)} %get-tuple-element.140), channel_id=1, source_target_pairs={{0,3},{1,0},{2,1},{3,2},{4,7},{5,4},{6,5},{7,6},{8,11},{9,8},{10,9... | collective-permute-start | bytes 1032200 | tf_op jit(solution)/shard_map/ppermute | solution.py:41
  504.6 47.3 %collective-permute-start.38 = (bf16[96,1792]{1,0:T(8,128)(2,1)S(1)}, bf16[96,1792]{1,0:T(8,128)(2,1)S(1)}, u32[]{:S(2)}, u32[]{:S(2)}) collective-permute-start(bf16[96,1792]{1,0:T(8,128)(2,1)S(1)} %get-tuple-element.142), channel_id=1, source_target_pairs={{0,2},{1,3},{2,0},{3,1},{4,6},{5,7},{6,4},{7,5},{8,10},{9,11},{10,... | collective-permute-start | bytes 1032200 | tf_op jit(solution)/shard_map/ppermute | solution.py:41
  505.9 45.9 %collective-permute-start.39 = (bf16[96,1792]{1,0:T(8,128)(2,1)S(1)}, bf16[96,1792]{1,0:T(8,128)(2,1)S(1)}, u32[]{:S(2)}, u32[]{:S(2)}) collective-permute-start(bf16[96,1792]{1,0:T(8,128)(2,1)S(1)} %get-tuple-element.141), channel_id=1, source_target_pairs={{0,1},{1,2},{2,3},{3,0},{4,5},{5,6},{6,7},{7,4},{8,9},{9,10},{10,1... | collective-permute-start | bytes 1032200 | tf_op jit(solution)/shard_map/ppermute | solution.py:41
  517.6 34.6 %collective-permute-start.31 = (bf16[96,1792]{1,0:T(8,128)(2,1)S(1)}, bf16[96,1792]{1,0:T(8,128)(2,1)S(1)}, u32[]{:S(2)}, u32[]{:S(2)}) collective-permute-start(bf16[96,1792]{1,0:T(8,128)(2,1)S(1)} %get-tuple-element.137), channel_id=1, source_target_pairs={{0,3},{1,0},{2,1},{3,2},{4,7},{5,4},{6,5},{7,6},{8,11},{9,8},{10,9... | collective-permute-start | bytes 1032200 | tf_op jit(solution)/shard_map/ppermute | solution.py:41
  519.7 44.2 %collective-permute-start.32 = (bf16[96,1792]{1,0:T(8,128)(2,1)S(1)}, bf16[96,1792]{1,0:T(8,128)(2,1)S(1)}, u32[]{:S(2)}, u32[]{:S(2)}) collective-permute-start(bf16[96,1792]{1,0:T(8,128)(2,1)S(1)} %get-tuple-element.139), channel_id=1, source_target_pairs={{0,2},{1,3},{2,0},{3,1},{4,6},{5,7},{6,4},{7,5},{8,10},{9,11},{10,... | collective-permute-start | bytes 1032200 | tf_op jit(solution)/shard_map/ppermute | solution.py:41
  521.1 42.8 %collective-permute-start.33 = (bf16[96,1792]{1,0:T(8,128)(2,1)S(1)}, bf16[96,1792]{1,0:T(8,128)(2,1)S(1)}, u32[]{:S(2)}, u32[]{:S(2)}) collective-permute-start(bf16[96,1792]{1,0:T(8,128)(2,1)S(1)} %get-tuple-element.138), channel_id=1, source_target_pairs={{0,1},{1,2},{2,3},{3,0},{4,5},{5,6},{6,7},{7,4},{8,9},{9,10},{10,1... | collective-permute-start | bytes 1032200 | tf_op jit(solution)/shard_map/ppermute | solution.py:41
  (37 other events, 277.7 us)

commit v3 on v2

--- a/solution.py
+++ b/solution.py
@@ -16,6 +16,7 @@
 LANES = 128
 MP = 4
 VMEM_LIMIT = 60 * 1024 * 1024
+BACK_LIMIT = 63 * 1024 * 1024
 
 
 def nn(a, b):
@@ -506,6 +507,18 @@
             sibling,
         )
 
+    def h_copy(l):
+        return remote(low_ref, saved[l][10].at[1], x_send.at[l, 4], x_recv.at[l, 4], sibling)
+
+    def e_copy(l):
+        return remote(
+            e_ref,
+            saved[l][8].at[:, pl.ds(rows, rows), :],
+            x_send.at[l, 5],
+            x_recv.at[l, 5],
+            sibling,
+        )
+
     stores = {}
 
     def store(name, source, target):
@@ -540,7 +553,7 @@
     own_z = [(z - 2 * c - k + MP) % MP for k in range(2)]
     other_z = [(at + 2) % MP for at in own_z]
     for l in range(n_layers):
-        xs, qs, ks, vs, ms, mis, ls, r1s, r2s, es, gps = saved[l]
+        xs, qs, ks, vs, ms, ls, r1s, r2s, es, gps, hs = saved[l]
         last = l - 1
         go(x_copy, l, 0)
         go(x_copy, l, 1)
@@ -610,10 +623,12 @@
         store(("lse", l), lse_ref, ls)
         step_ready(3 * l + 1)
         win_load = load(w_all.at[3 * l + 1], win, 3)
-        stored(("r1", last), ("r2", last), ("e", last), ("gp", last))
+        stored(("r1", last), ("r2", last), ("e", last), ("gp", last), ("h", last))
+        if l > 0:
+            h_copy(last).wait_send()
+            e_copy(last).wait_send()
         wo_load.wait()
         m_copy(l).wait_recv()
-        store(("mixed_in", l), mixed_in.at[l], mis)
         a = jnp.zeros((rows, width), F32)
         for k in range(2):
             a = a + nt(mixed_ref[0:rows, k * 256 : k * 256 + 256], wo[own_z[k]])
@@ -625,6 +640,8 @@
         n1, _ = norm_parts(r1)
         h = n1 * vec[1:2, :] + vec[2:3, :]
         low_ref[...] = h.astype(BF16)
+        store(("h", l), low_ref, hs.at[0])
+        h_copy(l).start()
         sum_ref[...] = h + vec[3:4, :]
         win_load.wait()
 
@@ -642,7 +659,8 @@
         run(take(10 if l == 0 else 18))
         step_ready(3 * l + 2)
         wback_load = load(w_all.at[3 * l + 2], wback, 4)
-        store(("e", l), e_ref, es)
+        store(("e", l), e_ref, es.at[:, pl.ds(0, rows), :])
+        e_copy(l).start()
         store(("gp", l), gp_ref, gps)
         wback_load.wait()
 
@@ -658,10 +676,16 @@
             stream[...] = result
             xfull[l + 1, 0] = result.astype(BF16)
         else:
+            h_copy(l).wait_send()
+            stored(("h", l))
             low_ref[...] = result.astype(BF16)
             store("low", low_ref, low_out)
 
     m_copy(n_layers - 1).wait_send()
+    e_copy(n_layers - 1).wait_send()
+    for l in range(n_layers):
+        h_copy(l).wait_recv()
+        e_copy(l).wait_recv()
     for make, at in sent:
         make(*at).wait_send()
     @pl.when(moved)
@@ -688,12 +712,12 @@
         shape((2, 2, keys, LANES), BF16),
         shape((2, 2, keys, LANES), BF16),
         shape((queries, 512), BF16),
-        shape((rows, 512), BF16),
         shape((8, queries), F32),
         shape((rows, width), F32),
         shape((rows, width), F32),
+        shape((MP, 2 * rows, width), BF16),
         shape((MP, rows, width), BF16),
-        shape((MP, rows, width), BF16),
+        shape((2, rows, width), BF16),
     )
     outs = (
         shape((chunks, MP, 8 * height, width), BF16),
@@ -743,8 +767,8 @@
             sem((chunks, 3)),
             sem((chunks, 4)),
             sem((chunks, 4)),
-            sem((n_layers, 4)),
-            sem((n_layers, 4)),
+            sem((n_layers, 6)),
+            sem((n_layers, 6)),
             sem((6,)),
             sem((6,)),
             sem((chunks + 3,)),
@@ -762,6 +786,819 @@
     head = results[:7]
     states = [results[7 + 11 * l : 18 + 11 * l] for l in range(n_layers)]
     return head, states
+
+
+def place_of(d, z):
+    c = d % 2
+    x = (d // 2) % 2
+    y = d // 4
+    flip_x, flip_y = 1 - 2 * x, 1 - 2 * y
+    planes = (
+        (y, x),
+        (y + c * flip_y, x + (1 - c) * flip_x),
+        (y + (1 - c) * flip_y, x + c * flip_x),
+        (1 - y, 1 - x),
+    )
+    groups = [2 * yy + xx for yy, xx in planes]
+
+    def device(group, cc, zz):
+        return (group * 2 + cc, zz)
+
+    return c, groups, device
+
+
+def head_back(
+    i,
+    h,
+    kblock,
+    q_ref,
+    k_ref,
+    v_ref,
+    dz_ref,
+    lse_ref,
+    delta_ref,
+    qrow_ref,
+    kcol_ref,
+    pair_ref,
+    dqt_ref,
+    dt_ref,
+):
+    tile = h // 2
+    keys, queries = k_ref.shape[2], q_ref.shape[2]
+    low_q = lane_index((queries, LANES)) < HD
+    low_k = lane_index((kblock, LANES)) < HD
+    q = q_ref[i, tile]
+    dz = dz_ref[i, tile]
+    if h < 2:
+        keep = low_q == (h == 0)
+        q = jnp.where(keep, q, BF16(0))
+        dz = jnp.where(keep, dz, BF16(0))
+    pair_ref[0] = q
+    pair_ref[1] = dz
+    lse = lse_ref[3 * i + h : 3 * i + h + 1, :]
+    delta = delta_ref[3 * i + h : 3 * i + h + 1, :]
+    if h != 1:
+        dqt_ref[...] = jnp.zeros_like(dqt_ref)
+
+    def one_block(n, _):
+        at = pl.ds(pl.multiple_of(n * kblock, kblock), kblock)
+        kb = k_ref[i, tile, at, :]
+        vb = v_ref[i, tile, at, :]
+        kb_own = jnp.where(low_k == (h == 0), kb, BF16(0)) if h < 2 else kb
+        visible = kcol_ref[at, :] == qrow_ref[...]
+        s = nt(kb, pair_ref[0])
+        s = jnp.where(visible, s, NEGATIVE)
+        p = jnp.exp(s - lse)
+        dp = nt(vb, pair_ref[1])
+        ds = (p * (dp - delta)).astype(BF16)
+        dv = nn(p.astype(BF16), pair_ref[1])
+        dk = nn(ds, pair_ref[0])
+        dqt_ref[...] += nn(jnp.transpose(kb_own), ds)
+        if h == 1:
+            dt_ref[2, at, :] += dk
+            dt_ref[3, at, :] += dv
+        elif h == 0:
+            dt_ref[2, at, :] = dk
+            dt_ref[3, at, :] = dv
+        else:
+            dt_ref[1, at, :] = pltpu.roll(dk, HD, 1)
+            dt_ref[4, at, :] = dv
+        return 0
+
+    lax.fori_loop(0, keys // kblock, one_block, 0)
+    if h >= 1:
+        dq = jnp.transpose(dqt_ref[...]) * HD**-0.5
+        if h == 1:
+            dt_ref[0, 0:queries, :] = dq
+        else:
+            dt_ref[1, 0:queries, :] += dq
+
+
+def head_deltas(i, mixed_ref, dz_ref, delta_ref):
+    single = pltpu.roll(mixed_ref[:, i * 256 : i * 256 + LANES].astype(F32), HD, 1)
+    pair = mixed_ref[:, i * 256 + LANES : i * 256 + 256].astype(F32)
+    prod_one = jnp.transpose(pair * dz_ref[i, 0].astype(F32))
+    prod_two = jnp.transpose(single * dz_ref[i, 1].astype(F32))
+    delta_ref[3 * i : 3 * i + 1, :] = jnp.sum(prod_one[0:HD], axis=0, keepdims=True)
+    delta_ref[3 * i + 1 : 3 * i + 2, :] = jnp.sum(prod_one[HD:], axis=0, keepdims=True)
+    delta_ref[3 * i + 2 : 3 * i + 3, :] = jnp.sum(prod_two[0:HD], axis=0, keepdims=True)
+
+
+def norm_back_rows(acc_ref, r_ref, low_ref, gain):
+    rows, width = acc_ref.shape
+    step = 32
+
+    def body(i, sums):
+        at = pl.ds(pl.multiple_of(i * step, step), step)
+        dy = acc_ref[at, :]
+        n, scale = norm_parts(r_ref[at, :])
+        dr = norm_back(dy, n, scale, gain)
+        acc_ref[at, :] = dr
+        low_ref[at, :] = dr.astype(BF16)
+        return (
+            sums[0] + jnp.sum(dy * n, axis=0, keepdims=True),
+            sums[1] + jnp.sum(dy, axis=0, keepdims=True),
+            sums[2] + jnp.sum(dr, axis=0, keepdims=True),
+        )
+
+    zero = jnp.zeros((1, width), F32)
+    return lax.fori_loop(0, rows // step, body, (zero, zero, zero))
+
+
+def backward_kernel(n_layers, *refs):
+    n_in, per_layer = 7, 11
+    w_all, dy_in, cos_in, sin_in, qrow_ref, kcol_ref, vectors = refs[:n_in]
+    saved = [refs[n_in + l * per_layer : n_in + (l + 1) * per_layer] for l in range(n_layers)]
+    at = n_in + n_layers * per_layer
+    tokens_out, feed_out, attn_out, small_out = refs[at : at + 4]
+    (
+        pool,
+        gp_ref,
+        r1_ref,
+        r2_ref,
+        acc_ref,
+        df_ref,
+        dfin_ref,
+        da_ref,
+        dain_ref,
+        h_ref,
+        turn_ref,
+        ht_ref,
+        dft_ref,
+        du_ref,
+        t_ref,
+        one_in,
+        two_in,
+        z_in,
+        dwo_ref,
+        ta_ref,
+        a_one_in,
+        a_two_in,
+        a_z_in,
+        a_c_in,
+        a_sum_ref,
+        a_out_ref,
+        wa,
+        q_ref,
+        k_ref,
+        v_ref,
+        mixed_ref,
+        lse_ref,
+        delta_ref,
+        dz_ref,
+        dt_ref,
+        dqt_ref,
+        pair_ref,
+        cos_ref,
+        sin_ref,
+        dxc_in,
+        dxp_in,
+        back_in,
+        v_stage,
+        v_in,
+        dbin_ref,
+        c_send,
+        c_recv,
+        one_send,
+        one_recv,
+        two_send,
+        two_recv,
+        z_send,
+        z_recv,
+        a_send,
+        a_recv,
+        v_send,
+        v_recv,
+        t_send,
+        t_recv,
+        w_sem,
+        s_sem,
+        o_sem,
+    ) = refs[at + 4 :]
+    part_ref, dxs_ref, dxp_ref = r2_ref, h_ref, df_ref
+    rows, width = acc_ref.shape
+    height = t_ref.shape[2]
+    queries = 2 * rows
+
+    d = lax.axis_index("dp")
+    z = lax.axis_index("mp")
+    c, groups, device = place_of(d, z)
+    sibling = device(groups[0], 1 - c, z)
+    first = device(groups[1], c, z)
+    second = device(groups[2], c, z)
+    away = device(groups[0], 1 - c, (z + 2) % MP)
+    pair = device(groups[0], c, z + 1 - 2 * (z % 2))
+    columns = [device(groups[0], c, (z + s) % MP) for s in range(1, MP)]
+    moved = c != z // 2
+
+    barrier = pltpu.get_barrier_semaphore()
+    partners = columns + [first, second, sibling, away]
+    for partner in partners:
+        pl.semaphore_signal(
+            barrier, inc=1, device_id=partner, device_id_type=pl.DeviceIdType.MESH
+        )
+
+    def remote(source, target, send, recv, to):
+        return pltpu.make_async_remote_copy(
+            src_ref=source,
+            dst_ref=target,
+            send_sem=send,
+            recv_sem=recv,
+            device_id=to,
+            device_id_type=pl.DeviceIdType.MESH,
+        )
+
+    def column(k):
+        return (z - k + MP) % MP
+
+    own_z = [(z - 2 * c - i + MP) % MP for i in range(2)]
+
+    def load(source, target, sem):
+        return pltpu.make_async_copy(source, target, sem)
+
+    def early_loads(l):
+        _, _, _, _, _, _, r1s, r2s, _, _, hs = saved[l]
+        return [
+            load(r2s, r2_ref, s_sem.at[0]),
+            load(r1s, r1_ref, s_sem.at[1]),
+            load(hs, h_ref, s_sem.at[2]),
+        ]
+
+    def weight_loads(l, k):
+        slot = k % 2
+        gps = saved[l][9]
+        return [
+            load(w_all.at[3 * l + 2, column(k)], pool.at[2 + slot], w_sem.at[slot, 0]),
+            load(w_all.at[3 * l + 1, column(k)], pool.at[slot], w_sem.at[slot, 1]),
+            load(gps.at[column(k)], gp_ref.at[slot], w_sem.at[slot, 2]),
+        ]
+
+    def e_load(l, k):
+        slot = k % 2
+        es = saved[l][8]
+        return load(es.at[column(k)], pool.at[4 + slot], w_sem.at[slot, 3])
+
+    def late_loads(l):
+        _, qs, ks, vs, ms, ls = saved[l][:6]
+        return [
+            load(qs, q_ref, s_sem.at[3]),
+            load(ks, k_ref, s_sem.at[4]),
+            load(vs, v_ref, s_sem.at[5]),
+            load(ms, mixed_ref, s_sem.at[6]),
+            load(ls, lse_ref, s_sem.at[7]),
+            load(w_all.at[3 * l, own_z[0]], wa.at[0], s_sem.at[8]),
+            load(w_all.at[3 * l, own_z[1]], wa.at[1], s_sem.at[9]),
+        ]
+
+    def x_loads(l):
+        xs = saved[l][0]
+        return [
+            load(xs.at[n], pool.at[2 + n // 2, pl.ds(n % 2 * rows, rows)], s_sem.at[14 + n])
+            for n in range(4)
+        ]
+
+    dy_load = load(dy_in, df_ref, s_sem.at[11])
+    table_loads = [load(cos_in, cos_ref, s_sem.at[12]), load(sin_in, sin_ref, s_sem.at[13])]
+    dy_load.start()
+    for copy in early_loads(n_layers - 1) + weight_loads(n_layers - 1, 0):
+        copy.start()
+    for copy in table_loads + late_loads(n_layers - 1):
+        copy.start()
+
+    def df_copy(l):
+        return remote(df_ref, dfin_ref, c_send.at[l, 0], c_recv.at[l, 0], sibling)
+
+    def da_copy(l):
+        return remote(da_ref, dain_ref, c_send.at[l, 1], c_recv.at[l, 1], sibling)
+
+    def du_copy(l, k):
+        return remote(
+            du_ref.at[k, pl.ds(0, rows)],
+            du_ref.at[k, pl.ds(rows, rows)],
+            c_send.at[l, 2 + k],
+            c_recv.at[l, 2 + k],
+            sibling,
+        )
+
+    def dxs_copy(l):
+        return remote(dxs_ref, dxc_in, c_send.at[l, 6], c_recv.at[l, 6], sibling)
+
+    def dxp_copy(l):
+        return remote(dxp_ref, dxp_in.at[l], a_send.at[l, 5], a_recv.at[l, 5], pair)
+
+    def one_copy(l, k, n):
+        return remote(
+            t_ref.at[k, groups[1 if n == 0 else 3]],
+            one_in.at[k, n],
+            one_send.at[l, k, n],
+            one_recv.at[l, k, n],
+            first,
+        )
+
+    def two_copy(l, k):
+        return remote(
+            t_ref.at[k, groups[2]], two_in.at[k], two_send.at[l, k], two_recv.at[l, k], second
+        )
+
+    def z_copy(l, k):
+        return remote(
+            t_ref.at[k, groups[0]],
+            z_in.at[l, k - 1],
+            z_send.at[l, k],
+            z_recv.at[l, k],
+            device(groups[0], c, column(k)),
+        )
+
+    def span(group):
+        return pl.ds(pl.multiple_of(group * 2 * height, 32), 2 * height)
+
+    def a_one_copy(l, n):
+        return remote(
+            ta_ref.at[:, span(groups[1 if n == 0 else 3]), :],
+            a_one_in.at[n],
+            a_send.at[l, n],
+            a_recv.at[l, n],
+            first,
+        )
+
+    def a_two_copy(l):
+        return remote(
+            ta_ref.at[:, span(groups[2]), :],
+            a_two_in,
+            a_send.at[l, 2],
+            a_recv.at[l, 2],
+            second,
+        )
+
+    def a_z_copy(l, i):
+        return remote(
+            ta_ref.at[i, span(groups[0]), :],
+            a_z_in.at[i],
+            a_send.at[l, 3 + i],
+            a_recv.at[l, 3 + i],
+            device(groups[0], c, own_z[i]),
+        )
+
+    def a_c_copy(l):
+        return remote(
+            a_out_ref, a_c_in.at[l], c_send.at[l, 7], c_recv.at[l, 7], sibling
+        )
+
+    def v_copy(l, n):
+        to = (sibling, first, second, columns[0], columns[1], columns[2])[n]
+        return remote(
+            v_stage.at[l, min(n, 3)], v_in.at[l, n], v_send.at[l, n], v_recv.at[l, n], to
+        )
+
+    def step_one(l, k):
+        for n in range(2):
+            one_copy(l, k, n).wait_recv()
+        g = groups[2]
+        t_ref[k, g] = (t_ref[k, g].astype(F32) + one_in[k, 1].astype(F32)).astype(BF16)
+        two_copy(l, k).start()
+
+    def step_two(l, k):
+        two_copy(l, k).wait_recv()
+        g = groups[0]
+        t_ref[k, g] = (
+            t_ref[k, g].astype(F32) + one_in[k, 0].astype(F32) + two_in[k].astype(F32)
+        ).astype(BF16)
+        if k > 0:
+            z_copy(l, k).start()
+
+    def step_feed_end(l):
+        total = t_ref[0, groups[0]].astype(F32)
+        for k in range(1, MP):
+            z_copy(l, k).wait_recv()
+            total = total + z_in[l, k - 1].astype(F32)
+        feed_out[l] = total
+
+    def step_a_one(l):
+        for n in range(2):
+            a_one_copy(l, n).wait_recv()
+        for i in range(2):
+            at = span(groups[2])
+            ta_ref[i, at, :] = (
+                ta_ref[i, at, :].astype(F32) + a_one_in[1, i].astype(F32)
+            ).astype(BF16)
+        a_two_copy(l).start()
+
+    def step_a_two(l):
+        a_two_copy(l).wait_recv()
+        for i in range(2):
+            at = span(groups[0])
+            ta_ref[i, at, :] = (
+                ta_ref[i, at, :].astype(F32)
+                + a_one_in[0, i].astype(F32)
+                + a_two_in[i].astype(F32)
+            ).astype(BF16)
+
+        @pl.when(c == 1)
+        def _():
+            a_z_copy(l, 0).start()
+
+        a_z_copy(l, 1).start()
+
+    def step_a_z(l):
+        a_z_copy(l, 1).wait_recv()
+
+        @pl.when(c == 0)
+        def _():
+            a_sum_ref[...] = ta_ref[0, span(groups[0]), :].astype(F32) + a_z_in[1].astype(F32)
+
+        @pl.when(c == 1)
+        def _():
+            a_z_copy(l, 0).wait_recv()
+            a_sum_ref[...] = a_z_in[0].astype(F32) + a_z_in[1].astype(F32)
+
+        other = pl.ds(pl.multiple_of((1 - c) * height, 32), height)
+        a_out_ref[...] = a_sum_ref[other, :].astype(BF16)
+        a_c_copy(l).start()
+
+    def step_a_end(l):
+        a_c_copy(l).wait_recv()
+        own = pl.ds(pl.multiple_of(c * height, 32), height)
+        attn_out[l] = a_sum_ref[own, :] + a_c_in[l].astype(F32)
+
+    def step_v(l, n):
+        v_copy(l, n - 1).wait_recv()
+        v_stage[l, n] = v_stage[l, n - 1] + v_in[l, n - 1]
+        if n < 3:
+            v_copy(l, n).start()
+        else:
+            for s in range(3, 6):
+                v_copy(l, s).start()
+
+    def step_v_end(l):
+        total = v_stage[l, 3, 0:6, :]
+        one = v_stage[l, 3, 6:7, :]
+        two = v_stage[l, 3, 10:11, :]
+        for s in range(1, MP):
+            v_copy(l, 2 + s).wait_recv()
+            got = v_in[l, 2 + s]
+            total = total + got[0:6, :]
+            one = one + got[6 + MP - s : 7 + MP - s, :]
+            two = two + got[10 + MP - s : 11 + MP - s, :]
+        small_out[l, 0:6, :] = total
+        small_out[l, 6:7, :] = one
+        small_out[l, 7:8, :] = two
+
+    kblock = 256
+    for l in reversed(range(n_layers)):
+        top = l == n_layers - 1
+        vec = vectors[l]
+        copies = early_loads(l)
+        if top:
+            dy_load.wait()
+            acc_ref[...] = df_ref[...].astype(F32)
+        else:
+            dxp_copy(l + 1).wait_send()
+            step_a_one(l + 1)
+        for copy in copies:
+            copy.wait()
+        v_stage[l, 0] = jnp.zeros((16, width), F32)
+        sums = norm_back_rows(acc_ref, r2_ref, df_ref, vec[4:5, :])
+        v_stage[l, 0, 4:5, :], v_stage[l, 0, 5:6, :], v_stage[l, 0, 3:4, :] = sums
+        if top:
+            pl.semaphore_wait(barrier, len(partners))
+        df_copy(l).start()
+        if not top:
+            for k in range(MP):
+                du_copy(l + 1, k).wait_send()
+
+        def inner(k, _, l=l):
+            for copy in weight_loads(l, k):
+                copy.wait()
+
+            @pl.when(k + 1 < MP)
+            def _():
+                for copy in weight_loads(l, k + 1):
+                    copy.start()
+
+            slot = k % 2
+            de = nn(df_ref[...], pool[2 + slot])
+            du = de * gp_ref[slot].astype(F32)
+            dbin_ref[k] = jnp.sum(du, axis=0, keepdims=True)
+            dub = du.astype(BF16)
+            du_ref[k, pl.ds(0, rows), :] = dub
+            du_copy(l, k).start()
+            acc_ref[...] += nt(dub, pool[slot])
+            return 0
+
+        lax.fori_loop(0, MP, inner, 0)
+        for copy in x_loads(l):
+            copy.start()
+        e_load(l, 0).start()
+        for k in range(MP):
+            v_stage[l, 0, 6 + k : 7 + k, :] = dbin_ref[k]
+        if not top:
+            step_a_two(l + 1)
+            da_copy(l + 1).wait_send()
+        sums = norm_back_rows(acc_ref, r1_ref, da_ref, vec[1:2, :])
+        v_stage[l, 0, 1:2, :], v_stage[l, 0, 2:3, :], v_stage[l, 0, 0:1, :] = sums
+        da_copy(l).start()
+
+        def turned(source, target, half):
+            turn_ref[...] = jnp.transpose(source)
+            for g in range(4):
+                at = pl.ds(pl.multiple_of((2 * g + c) * height, 32), height)
+                target[pl.ds(g * height, height), pl.ds(half * rows, rows)] = turn_ref[at, :]
+
+        turned(h_ref[0], ht_ref, 0)
+        turned(h_ref[1], ht_ref, 1)
+        turned(df_ref[...], dft_ref, 0)
+        df_copy(l).wait_recv()
+        turned(dfin_ref[...], dft_ref, 1)
+        if not top:
+            for k in range(MP):
+                for n in range(2):
+                    one_copy(l + 1, k, n).wait_send()
+                two_copy(l + 1, k).wait_send()
+                if k > 0:
+                    z_copy(l + 1, k).wait_send()
+
+        def outer(k, _, l=l):
+            e_load(l, k).wait()
+
+            @pl.when(k + 1 < MP)
+            def _():
+                e_load(l, k + 1).start()
+
+            back = nn(dft_ref[...], pool[4 + k % 2]).astype(BF16)
+            t_ref[k, :, :, pl.ds(width, width)] = back.reshape(4, height, width)
+            du_copy(l, k).wait_recv()
+            into = nn(ht_ref[...], du_ref[k]).astype(BF16)
+            t_ref[k, :, :, pl.ds(0, width)] = into.reshape(4, height, width)
+            for n in range(2):
+                one_copy(l, k, n).start()
+            return 0
+
+        lax.fori_loop(0, MP, outer, 0)
+        if not top:
+            step_a_z(l + 1)
+        for copy in late_loads(l):
+            copy.wait()
+        da_copy(l).wait_recv()
+        low_half = lane_index((rows, LANES)) < HD
+        for half, source in enumerate((da_ref, dain_ref)):
+            at = pl.ds(half * rows, rows)
+            for i in range(2):
+                dz = nn(source[...], wa[i, :, 4 * LANES :])
+                dz_ref[i, 0, at, :] = dz[:, LANES:].astype(BF16)
+                dz_ref[i, 1, at, :] = jnp.where(
+                    low_half, pltpu.roll(dz[:, :LANES], HD, 1), 0.0
+                ).astype(BF16)
+            pool[6, :, pl.ds(half * rows, rows)] = jnp.transpose(source[...])
+        for i in range(2):
+            dwo_ref[i] = nn(pool[6], mixed_ref[:, i * 256 : i * 256 + 256]).astype(BF16)
+            head_deltas(i, mixed_ref, dz_ref, delta_ref)
+        for copy in x_loads(l):
+            copy.wait()
+        for half in range(2):
+            pool[half] = jnp.transpose(pool[2 + half])
+        if top:
+            for copy in table_loads:
+                copy.wait()
+        if not top:
+            step_a_end(l + 1)
+
+        steps = [[] for _ in range(6)]
+        for k in range(MP):
+            steps[k].append(partial(step_one, l, k))
+            steps[k + 1].append(partial(step_two, l, k))
+        steps[5].append(partial(step_feed_end, l))
+        if not top:
+            for n in range(1, 4):
+                steps[n - 1].append(partial(step_v, l + 1, n))
+            steps[3].append(partial(step_v_end, l + 1))
+        for i in range(2):
+            for h in range(3):
+                head_back(
+                    i,
+                    h,
+                    kblock,
+                    q_ref,
+                    k_ref,
+                    v_ref,
+                    dz_ref,
+                    lse_ref,
+                    delta_ref,
+                    qrow_ref,
+                    kcol_ref,
+                    pair_ref,
+                    dqt_ref,
+                    dt_ref,
+                )
+                for step in steps[3 * i + h]:
+                    step()
+            for tile in range(5):
+                total = jnp.zeros((1, LANES), F32)
+                for half in range(1 if tile == 0 else 2):
+                    at = pl.ds(half * queries, queries)
+                    t = dt_ref[tile, at, :]
+                    if tile < 3:
+                        t = t * cos_ref[at, :] - half_swap(t) * sin_ref[at, :]
+                    total = total + jnp.sum(t, axis=0, keepdims=True)
+                    pool[2 + 2 * i + half, :, tile * LANES : (tile + 1) * LANES] = t.astype(BF16)
+                for core in range(2):
+                    v_stage[
+                        l, 0, 10 + 2 * core + i : 11 + 2 * core + i, tile * LANES : (tile + 1) * LANES
+                    ] = jnp.where(c == core, total, 0.0)
+        v_copy(l, 0).start()
+
+        def spread(n):
+            half, at = n // 2, pl.ds((n % 2) * rows, rows)
+            total = jnp.zeros((rows, width), F32)
+            for i in range(2):
+                low = pool.at[2 + 2 * i + half]
+                total = total + nt(low[at, LANES : 5 * LANES], wa[i, :, LANES : 5 * LANES])
+                if half == 0:
+                    total = total + nt(low[at, 0:LANES], wa[i, :, 0:LANES])
+            return total
+
+        df_copy(l).wait_send()
+        dxs_ref[1] = spread(3).astype(BF16)
+        dxs_ref[0] = spread(1).astype(BF16)
+        dxs_copy(l).start()
+        part_ref[...] = spread(2)
+        dxs_copy(l).wait_recv()
+        dxp_ref[...] = (part_ref[...] + dxc_in[1].astype(F32)).astype(BF16)
+        dxp_copy(l).start()
+        acc_ref[...] += spread(0) + dxc_in[0].astype(F32)
+        if not top:
+            for n in range(2):
+                a_one_copy(l + 1, n).wait_send()
+            a_two_copy(l + 1).wait_send()
+            a_z_copy(l + 1, 1).wait_send()
+
+            @pl.when(c == 1)
+            def _(l=l):
+                a_z_copy(l + 1, 0).wait_send()
+
+            a_c_copy(l + 1).wait_send()
+        for i in range(2):
+            low = [pool.at[2 + 2 * i + half] for half in range(2)]
+            ta_ref[i, :, 0:LANES] = nn(pool[0], low[0][:, 0:LANES]).astype(BF16)
+            more = nn(pool[0], low[0][:, LANES : 5 * LANES]) + nn(
+                pool[1], low[1][:, LANES : 5 * LANES]
+            )
+            ta_ref[i, :, LANES : 4 * LANES] = more[:, : 3 * LANES].astype(BF16)
+            ta_ref[i, :, 4 * LANES : 5 * LANES] = (
+                more[:, 3 * LANES :] + dwo_ref[i, :, 0:LANES].astype(F32)
+            ).astype(BF16)
+            ta_ref[i, :, 5 * LANES :] = dwo_ref[i, :, LANES:]
+        for n in range(2):
+            a_one_copy(l, n).start()
+        if l > 0:
+            dxs_copy(l).wait_send()
+            for copy in early_loads(l - 1) + weight_loads(l - 1, 0) + late_loads(l - 1):
+                copy.start()
+        dxp_copy(l).wait_recv()
+        acc_ref[...] += dxp_in[l].astype(F32)
+
+    dxp_copy(0).wait_send()
+    df_ref[...] = acc_ref[...].astype(BF16)
+    back_copy = remote(df_ref, back_in, t_send.at[0], t_recv.at[0], away)
+
+    @pl.when(moved)
+    def _():
+        back_copy.start()
+
+    step_v(0, 1)
+    step_a_one(0)
+    step_v(0, 2)
+    step_a_two(0)
+    step_v(0, 3)
+    step_v_end(0)
+
+    @pl.when(moved)
+    def _():
+        back_copy.wait_recv()
+        acc_ref[...] = back_in[...].astype(F32)
+
+    out_copy = pltpu.make_async_copy(acc_ref, tokens_out, o_sem.at[0])
+    out_copy.start()
+    step_a_z(0)
+    step_a_end(0)
+    out_copy.wait()
+
+    @pl.when(moved)
+    def _():
+        back_copy.wait_send()
+
+    da_copy(0).wait_send()
+    dxs_copy(0).wait_send()
+    for k in range(MP):
+        du_copy(0, k).wait_send()
+        for n in range(2):
+            one_copy(0, k, n).wait_send()
+        two_copy(0, k).wait_send()
+        if k > 0:
+            z_copy(0, k).wait_send()
+    for n in range(2):
+        a_one_copy(0, n).wait_send()
+    a_two_copy(0).wait_send()
+    a_z_copy(0, 1).wait_send()
+
+    @pl.when(c == 1)
+    def _():
+        a_z_copy(0, 0).wait_send()
+
+    a_c_copy(0).wait_send()
+    for l in range(n_layers):
+        for n in range(6):
+            v_copy(l, n).wait_send()
+
+
+def backward(w_all, dy, cos, sin, qrow, kcol, vectors, states):
+    n_layers, _, width = vectors.shape
+    rows = dy.shape[0]
+    height = width // 8
+    queries, keys = 2 * rows, 4 * rows
+    sem = pltpu.SemaphoreType.DMA
+    flat = [array for state in states for array in state]
+    return pl.pallas_call(
+        partial(backward_kernel, n_layers),
+        out_shape=(
+            shape((rows, width), F32),
+            shape((n_layers, height, 2 * width), F32),
+            shape((n_layers, height, width), F32),
+            shape((n_layers, 8, width), F32),
+        ),
+        in_specs=[anywhere()] * 4 + [vmem()] * 3 + [anywhere()] * len(flat),
+        out_specs=(anywhere(), vmem(), vmem(), vmem()),
+        scratch_shapes=[
+            pltpu.VMEM((7, width, width), BF16),
+            pltpu.VMEM((2, rows, width), BF16),
+            pltpu.VMEM((rows, width), F32),
+            pltpu.VMEM((rows, width), F32),
+            pltpu.VMEM((rows, width), F32),
+            pltpu.VMEM((rows, width), BF16),
+            pltpu.VMEM((rows, width), BF16),
+            pltpu.VMEM((rows, width), BF16),
+            pltpu.VMEM((rows, width), BF16),
+            pltpu.VMEM((2, rows, width), BF16),
+            pltpu.VMEM((width, rows), BF16),
+            pltpu.VMEM((4 * height, 2 * rows), BF16),
+            pltpu.VMEM((4 * height, 2 * rows), BF16),
+            pltpu.VMEM((MP, 2 * rows, width), BF16),
+            pltpu.VMEM((MP, 4, height, 2 * width), BF16),
+            pltpu.VMEM((MP, 2, height, 2 * width), BF16),
+            pltpu.VMEM((MP, height, 2 * width), BF16),
+            pltpu.VMEM((n_layers, MP - 1, height, 2 * width), BF16),
+            pltpu.VMEM((2, width, 2 * LANES), BF16),
+            pltpu.VMEM((2, width, width), BF16),
+            pltpu.VMEM((2, 2, 2 * height, width), BF16),
+            pltpu.VMEM((2, 2 * height, width), BF16),
+            pltpu.VMEM((2, 2 * height, width), BF16),
+            pltpu.VMEM((n_layers, height, width), BF16),
+            pltpu.VMEM((2 * height, width), F32),
+            pltpu.VMEM((height, width), BF16),
+            pltpu.VMEM((2, width, width), BF16),
+            pltpu.VMEM((2, 2, queries, LANES), BF16),
+            pltpu.VMEM((2, 2, keys, LANES), BF16),
+            pltpu.VMEM((2, 2, keys, LANES), BF16),
+            pltpu.VMEM((queries, 512), BF16),
+            pltpu.VMEM((8, queries), F32),
+            pltpu.VMEM((8, queries), F32),
+            pltpu.VMEM((2, 2, queries, LANES), BF16),
+            pltpu.VMEM((5, keys, LANES), F32),
+            pltpu.VMEM((LANES, queries), F32),
+            pltpu.VMEM((2, queries, LANES), BF16),
+            pltpu.VMEM((keys, LANES), F32),
+            pltpu.VMEM((keys, LANES), F32),
+            pltpu.VMEM((2, rows, width), BF16),
+            pltpu.VMEM((n_layers, rows, width), BF16),
+            pltpu.VMEM((rows, width), BF16),
+            pltpu.VMEM((n_layers, 4, 16, width), F32),
+            pltpu.VMEM((n_layers, 6, 16, width), F32),
+            pltpu.VMEM((MP, 1, width), F32),
+            sem((n_layers, 8)),
+            sem((n_layers, 8)),
+            sem((n_layers, MP, 2)),
+            sem((n_layers, MP, 2)),
+            sem((n_layers, MP)),
+            sem((n_layers, MP)),
+            sem((n_layers, MP)),
+            sem((n_layers, MP)),
+            sem((n_layers, 6)),
+            sem((n_layers, 6)),
+            sem((n_layers, 6)),
+            sem((n_layers, 6)),
+            sem((1,)),
+            sem((1,)),
+            sem((2, 4)),
+            sem((18,)),
+            sem((1,)),
+        ],
+        compiler_params=pltpu.CompilerParams(
+            vmem_limit_bytes=BACK_LIMIT, collective_id=1, has_side_effects=True
+        ),
+        cost_estimate=pl.CostEstimate(
+            flops=200_000_000_000, bytes_accessed=100_000_000, transcendentals=20_000_000
+        ),
+        name="backward",
+    )(w_all, dy, cos, sin, qrow, kcol, vectors, *flat)
 
 
 def attend_kernel(chunk, *refs):
@@ -1328,8 +2165,34 @@
     exponents = jnp.arange(LANES, dtype=jnp.int32) % (HD // 2)
     frequency = 10000.0 ** (-2.0 * exponents.astype(F32) / HD)[None, :]
 
-    run = forward if pieces == 8 else plain_forward
-    head, states = run(blocks, tokens, cotangent, small, meta, frequency, vectors)
+    if pieces == 8:
+        head, states = forward(blocks, tokens, cotangent, small, meta, frequency, vectors)
+        w_all, dy, low, cos, sin, qrow, kcol = head
+        result = relayout(low)
+        grad_tokens, feed_grads, attn_grads, small_grads = backward(
+            w_all, dy, cos, sin, qrow, kcol, vectors, states
+        )
+        grad_qkv = jnp.stack(head_columns(attn_grads), axis=1)
+        grad_in = feed_grads[:, :, :width]
+        grad_back = jnp.swapaxes(feed_grads[:, :, width:], 1, 2)
+        grad_out = jnp.concatenate(
+            [attn_grads[:, :, 5 * LANES :], attn_grads[:, :, 4 * LANES + HD : 5 * LANES]], axis=-1
+        )
+        grad_out = jnp.swapaxes(grad_out, 1, 2)
+        grad_b_qkv = jnp.stack(head_columns(small_grads[:, 7, :]), axis=1)
+        return (
+            result,
+            grad_tokens,
+            grad_qkv,
+            grad_b_qkv,
+            grad_out,
+            small_grads[:, :6],
+            grad_in,
+            small_grads[:, 6],
+            grad_back,
+        )
+
+    head, states = plain_forward(blocks, tokens, cotangent, small, meta, frequency, vectors)
     w_all, gradient, low, cos, sin, qcode, kcode = head
     result = relayout(low)
     gradient = gradient.astype(F32)

time: 577 us -> 463 us (0.80)
  the two profiles are of different devices: /device:TPU:0 before, /device:TPU:27 now
where the time goes in v3:
time: 463 us; the launch traced here: 455 us
  Pallas kernels  429 us (93%)
  local copies, waits for them, and re-layouts  16.4 us (4%)
  starting transfers between devices  5.98 us (1%)
    pallas_call x1, Pallas kernels, backward(): pl.pallas_call(partial(backward_kernel, n_layers), out_shape=(shape((rows...  251 us
    pallas_call x1, Pallas kernels, forward(): pl.pallas_call(partial(forward_kernel, n_layers), out_shape=outs, in_spec...  178 us
  transfers between devices with their start and end apart: 1, of which 0 were waited for; matrix products, arithmetic and copies ran while one was open for 2% of the time, Pallas kernels for 55%

profile of v3, /device:TPU:27, one launch (start us, length us, event | category | flops | bytes accessed | tf_op | source)
XLA Modules:
  0.0 455.4 jit_solution(12288233505333181244)
XLA Ops:
  1.4 0.5 fusion.4.refs_5_
  1.9 0.7 slice_bitcast_fusion.18
  2.6 0.7 slice_bitcast_fusion.17
  3.3 0.7 slice_bitcast_fusion.15
  4.0 1.0 copy.20
  5.0 0.0 copy-start.4
  5.1 1.1 convert.16
  6.3 0.1 add_convert_fusion
  6.4 0.1 concatenate.37
  6.5 0.6 pad.8.refs_3_
  7.2 0.6 copy.21.refs_6_
  7.9 0.1 concatenate.35
  8.0 0.1 concatenate.36
  8.2 0.0 copy-start.6
  8.2 0.7 broadcast_in_dim.5.refs_4_
  9.0 0.2 copy-done.6
  9.1 177.7 %forward.1 = (bf16[6,4,768,768]{3,2,1,0:T(8,128)(2,1)}, bf16[384,768]{1,0:T(8,128)(2,1)}, bf16[384,768]{1,0:T(8,128)(2,1)}, f32[1536,128]{1,0:T(8,128)}, f32[153...) custom-call(bf16[6,96,768]{2,1,0:T(8,128)(2,1)} %copy-done.6, ...), custom_call_target="tpu_custom_call" | custom-call | flops 99999997952 | bytes 100000000 | tf_op jit(solution)/shard_map/forward/pallas_call | solution.py:732
  186.8 6.0 %collective-permute-start = (bf16[384,768]{1,0:T(8,128)(2,1)}, bf16[384,768]{1,0:T(8,128)(2,1)}, u32[]{:S(2)}, u32[]{:S(2)}) collective-permute-start(bf16[384,768]{1,0:T(8,128)(2,1)} %get-tuple-element.42), channel_id=1, source_target_pairs={{0,0},{1,1},{2,4},{3,5},{4,2},{5,3},{6,6},{7,7},{8,8},{9,9},{10,12... | collective-permute-start | bytes 1769480 | tf_op jit(solution)/shard_map/ppermute | solution.py:58
  192.8 250.8 %backward.1 = (f32[384,768]{1,0:T(8,128)}, f32[2,96,1536]{2,1,0:T(8,128)}, f32[2,96,768]{2,1,0:T(8,128)}, f32[2,8,768]{2,1,0:T(8,128)}) custom-call(bf16[6,4,768,768]{3,2,1,0:T(8,128)(2,1)} %get-tuple-element.43.refs_0_, bf16[384,768]{1,0:T(8,128)(2,1)} %get-tuple-element.44.refs_1_, f32[1536,128]{1,0:T(8,128)} %get-tuple-element.45.refs_2_, ...), custom_call_target="tpu_custom_call" | custom-call | flops 199999995904 | bytes 100000000 | tf_op jit(solution)/shard_map/backward/pallas_call | solution.py:1520
  443.6 0.9 fusion.7
  444.6 0.1 slice.207
  444.6 1.0 fusion.5
  445.6 1.1 fusion.6
  446.6 0.6 copy.30
  447.2 1.4 copy.25
  448.7 0.8 copy.24
  449.6 0.1 pad_maximum_fusion
  449.6 0.9 copy.23
  450.5 0.6 pad_maximum_fusion.1
  451.1 1.1 slice_bitcast_fusion
  452.2 1.9 copy.40
  454.1 1.0 copy.41
  (42 shorter events, 0.3 us)
Async XLA Ops:
  0.6 5.7 %copy-start.8 = (s32[1,3]{1,0:T(1,128)S(1)}, s32[1,3]{1,0:T(1,128)}, u32[]{:S(2)}) copy-start(s32[1,3]{1,0:T(1,128)} %param.20) | copy-start | bytes 40
  0.7 5.8 %copy-start.7 = (f32[2,768]{1,0:T(2,128)S(1)}, f32[2,768]{1,0:T(2,128)}, u32[]{:S(2)}) copy-start(f32[2,768]{1,0:T(2,128)} %param.17) | copy-start | bytes 18436
  0.7 6.5 %copy-start.5 = (f32[2,6,768]{2,0,1:T(2,128)S(1)}, f32[2,6,768]{2,0,1:T(2,128)}, u32[]{:S(2)}) copy-start(f32[2,6,768]{2,0,1:T(2,128)} %param.15) | copy-start | bytes 110596
  0.7 7.1 %copy-start.3 = (f32[2,96,768]{2,1,0:T(8,128)S(1)}, f32[2,96,768]{2,1,0:T(8,128)}, u32[]{:S(2)}) copy-start(f32[2,96,768]{2,1,0:T(8,128)} %param.16) | copy-start | bytes 1769476
  5.0 2.8 copy-start.4
  8.2 0.9 copy-start.6
  186.8 265.4 %collective-permute-start = (bf16[384,768]{1,0:T(8,128)(2,1)}, bf16[384,768]{1,0:T(8,128)(2,1)}, u32[]{:S(2)}, u32[]{:S(2)}) collective-permute-start(bf16[384,768]{1,0:T(8,128)(2,1)} %get-tuple-element.42), channel_id=1, source_target_pairs={{0,0},{1,1},{2,4},{3,5},{4,2},{5,3},{6,6},{7,7},{8,8},{9,9},{10,12... | collective-permute-start | bytes 1769480 | tf_op jit(solution)/shard_map/ppermute | solution.py:58
  443.6 5.9 %copy-start.2 = (f32[2,96,768]{2,1,0:T(8,128)S(1)}, f32[2,96,768]{2,1,0:T(8,128)}, u32[]{:S(2)}) copy-start(f32[2,96,768]{2,1,0:T(8,128)} %get-tuple-element.72) | copy-start | bytes 1769476
  449.5 1.6 copy-start.1
  451.1 3.0 copy-start

commit v4 on v3

--- a/solution.py
+++ b/solution.py
@@ -15,6 +15,7 @@
 BF16 = jnp.bfloat16
 LANES = 128
 MP = 4
+SPLIT = 2
 VMEM_LIMIT = 60 * 1024 * 1024
 BACK_LIMIT = 63 * 1024 * 1024
 
@@ -227,7 +228,9 @@
         q_ref[z, 1, at, :] = jnp.where(low_half, mixed, 0.0).astype(BF16) * BF16(HD**-0.5)
 
 
-def attend_rows(i, qblock, qcode_ref, kcode_ref, q_ref, k_ref, v_ref, mixed_ref, lse_cols):
+def attend_rows(
+    i, qblock, qcode_ref, kcode_ref, q_ref, k_ref, v_ref, mixed_ref, lse_cols, between=None
+):
     at = pl.ds(pl.multiple_of(i * qblock, qblock), qblock)
     visible = qcode_ref[at, :] == kcode_ref[...]
     low_half = lane_index((qblock, LANES)) < HD
@@ -251,6 +254,17 @@
         mixed_ref[at, pl.ds(z * 256 + LANES, LANES)] = jnp.where(
             low_half, outs[0], outs[1]
         ).astype(BF16)
+        if between is not None:
+            between(z)
+
+
+def mirrored(z):
+    return [z, z + 1 - 2 * (z % 2), (z + 2) % MP, MP - 1 - z]
+
+
+def head_columns_of(z, c):
+    base = (z + 2 * c) % MP
+    return [base, base + 1 - 2 * (base % 2)]
 
 
 def forward_kernel(n_layers, *refs):
@@ -304,7 +318,7 @@
     rows = stream.shape[0]
     width = stream.shape[1]
     height = blocks.shape[1]
-    chunks = blocks.shape[0]
+    parts = blocks.shape[0] * SPLIT
 
     d = lax.axis_index("dp")
     z = lax.axis_index("mp")
@@ -318,22 +332,22 @@
     def device(yy, xx, cc, zz):
         return (yy * 4 + xx * 2 + cc, zz)
 
-    def rows_of(yy, xx):
-        return pl.ds(pl.multiple_of((yy * 4 + xx * 2 + c) * height, 32), height)
+    part_rows = height // SPLIT
+    planes = ((y, x), (one_y, one_x), (two_y, two_x), (1 - y, 1 - x))
+
+    def rows_of(k, n):
+        yy, xx = planes[n]
+        start = (yy * 4 + xx * 2 + c) * height + k % SPLIT * part_rows
+        return pl.ds(pl.multiple_of(start, 16), part_rows)
 
     sibling = device(y, x, 1 - c, z)
     first = device(one_y, one_x, c, z)
     second = device(two_y, two_x, c, z)
-    pair_z = z + 1 - 2 * (z % 2)
-    pair = device(y, x, c, pair_z)
+    pair = device(y, x, c, z + 1 - 2 * (z % 2))
     away = device(y, x, 1 - c, (z + 2) % MP)
     moved = c != z // 2
-    columns = [device(y, x, c, (z + s) % MP) for s in range(1, MP)]
-    own_rows = rows_of(y, x)
-    first_rows = rows_of(one_y, one_x)
-    second_rows = rows_of(two_y, two_x)
-    third_rows = rows_of(1 - y, 1 - x)
-
+    mirror = mirrored(z)
+    columns = [device(y, x, c, mirror[m]) for m in range(1, MP)]
     barrier = pltpu.get_barrier_semaphore()
     partners = columns + [first, second, sibling, away]
     for partner in partners:
@@ -358,37 +372,50 @@
         make(*at).start()
         sent.append((make, at))
 
+    def block(k):
+        return blocks.at[k // SPLIT, pl.ds(k % SPLIT * part_rows, part_rows)]
+
     def local_copy(k):
-        return pltpu.make_async_copy(blocks.at[k], w_all.at[k, z, own_rows], l_sem.at[k])
-
-    def z_copy(k, s):
+        return pltpu.make_async_copy(block(k), w_all.at[k // SPLIT, z, rows_of(k, 0)], l_sem.at[k])
+
+    def z_copy(k, n):
+        if n == 2:
+            source = target = w_all.at[k // SPLIT, mirror[2], rows_of(k, 0)]
+        else:
+            source, target = block(k), w_all.at[k // SPLIT, z, rows_of(k, 0)]
         return remote(
-            blocks.at[k], w_all.at[k, z, own_rows], z_send.at[k, s], z_recv.at[k, s], columns[s]
+            source, target, z_send.at[k, n], z_recv.at[k, n], columns[1 if n == 1 else 0]
         )
 
     def p_copy(k, n):
-        source = w_all.at[k, :, first_rows if n == 2 else own_rows]
+        source = w_all.at[k // SPLIT, :, rows_of(k, 1 if n == 2 else 0)]
         return remote(
             source, source, p_send.at[k, n], p_recv.at[k, n], first if n == 0 else second
         )
 
     def c_copy(k, n):
-        source = w_all.at[k, :, (own_rows, first_rows, second_rows, third_rows)[n]]
+        source = w_all.at[k // SPLIT, :, rows_of(k, n)]
         return remote(source, source, c_send.at[k, n], c_recv.at[k, n], sibling)
 
     def step_send(k):
         local_copy(k).start()
-        for s in range(MP - 1):
-            go(z_copy, k, s)
+        go(z_copy, k, 1)
+        go(z_copy, k, 0)
+
+    def step_across(k):
+        z_copy(k, 1).wait_recv()
+        go(z_copy, k, 2)
 
     def step_plane(k):
         local_copy(k).wait()
-        for s in range(MP - 1):
-            z_copy(k, s).wait_recv()
+        z_copy(k, 0).wait_recv()
+        z_copy(k, 2).wait_recv()
         go(p_copy, k, 0)
         go(p_copy, k, 1)
         go(c_copy, k, 0)
-        if k + 2 < chunks:
+        if k + 1 < parts:
+            step_across(k + 1)
+        if k + 2 < parts:
             step_send(k + 2)
 
     def step_forward(k):
@@ -402,22 +429,23 @@
         p_copy(k, 2).wait_recv()
         go(c_copy, k, 3)
 
-    def step_ready(k):
-        for n in range(4):
-            c_copy(k, n).wait_recv()
-
-    plan = []
-    for k in range(chunks):
-        plan.append(partial(step_plane, k))
-        plan.append(partial(step_forward, k))
-        plan.append(partial(step_last, k))
-    for k in range(chunks - 1):
-        at = plan.index(plan[3 * k + 2])
-        plan[at], plan[at + 1] = plan[at + 1], plan[at]
+    def step_ready(chunk):
+        for k in range(chunk * SPLIT, (chunk + 1) * SPLIT):
+            for n in range(4):
+                c_copy(k, n).wait_recv()
+
+    turns = parts + 2
     position = [0]
 
     def take(until):
-        steps = plan[position[0] : until]
+        steps = []
+        for n in range(position[0], until):
+            if n < parts:
+                steps.append(partial(step_plane, n))
+            if 0 <= n - 2:
+                steps.append(partial(step_last, n - 2))
+            if 0 <= n - 1 < parts:
+                steps.append(partial(step_forward, n - 1))
         position[0] = max(position[0], until)
         return steps
 
@@ -431,9 +459,13 @@
     def small_copy(s):
         return remote(small, small_all.at[z], t_send.at[3 + s], t_recv.at[3 + s], columns[s])
 
+    step_send(0)
     go(meta_copy)
+    for n in range(MP - 1):
+        go(small_copy, n)
     token_copy = remote(tokens, xfull.at[0, 0], t_send.at[1], t_recv.at[1], away)
-    token_local = pltpu.make_async_copy(tokens, xfull.at[0, 0], l_sem.at[chunks])
+    token_local = pltpu.make_async_copy(tokens, xfull.at[0, 0], l_sem.at[parts])
+    step_across(0)
 
     @pl.when(moved)
     def _():
@@ -443,11 +475,8 @@
     def _():
         token_local.start()
 
-    step_send(0)
-    for s in range(MP - 1):
-        go(small_copy, s)
     step_send(1)
-    small_local = pltpu.make_async_copy(small, small_all.at[z], l_sem.at[chunks + 1])
+    small_local = pltpu.make_async_copy(small, small_all.at[z], l_sem.at[parts + 1])
     small_local.start()
 
     meta_copy().wait_recv()
@@ -483,6 +512,8 @@
         if i < 2:
             qrow_ref[:, pl.ds(i * rows, rows)] = seq
 
+    run(take(1))
+
     @pl.when(moved)
     def _():
         token_copy.wait_recv()
@@ -541,7 +572,7 @@
     store("kcol", kcol_ref, kcol_out)
 
     cot_copy = remote(cot, dy_out, t_send.at[2], t_recv.at[2], away)
-    cot_local = pltpu.make_async_copy(cot, dy_out, l_sem.at[chunks + 2])
+    cot_local = pltpu.make_async_copy(cot, dy_out, l_sem.at[parts + 2])
 
     def load(source, target, n):
         copy = pltpu.make_async_copy(source, target, w_sem.at[n])
@@ -550,17 +581,17 @@
 
     qblock = 256
     count = 2 * rows // qblock
-    own_z = [(z - 2 * c - k + MP) % MP for k in range(2)]
+    own_z = head_columns_of(z, c)
     other_z = [(at + 2) % MP for at in own_z]
     for l in range(n_layers):
         xs, qs, ks, vs, ms, ls, r1s, r2s, es, gps, hs = saved[l]
         last = l - 1
         go(x_copy, l, 0)
         go(x_copy, l, 1)
-        run(take(9 * l + 3))
+        run(take(2 if l == 0 else 9))
         x_copy(l, 0).wait_recv()
         go(x_copy, l, 2)
-        run(take(9 * l + 4))
+        run(take(4 if l == 0 else 10))
         step_ready(3 * l)
         wa_loads = [
             load(w_all.at[3 * l, own_z[k], :, pl.ds(0, 5 * LANES)], wa.at[k], k) for k in range(2)
@@ -589,7 +620,7 @@
             if i == 1:
                 x_copy(l, 1).wait_recv()
             if i == 3:
-                run(take(9 * l + 6 - l))
+                run(take(5 if l == 0 else 10))
                 x_copy(l, 2).wait_recv()
             at = pl.ds(i * rows, rows)
             for k in range(2):
@@ -601,20 +632,32 @@
         store(("k", l), k_ref, ks)
         store(("v", l), v_ref, vs)
         store(("x", l), xfull.at[l], xs)
-        steps = [take(9 * l + 7), take(9 * l + 8 - l), take(9 * l + 9 - l)]
+        ends = (5, 5, 6, 6, 6, 7) if l == 0 else (11, 11, 11, 12, 12, 13)
+        steps = [take(end) for end in ends]
 
         def one_block(n, _, l=l, steps=steps):
+            def between(k):
+                for j in range(count):
+                    if steps[2 * j + k] or (j, k) == (1, 1):
+
+                        @pl.when(n == j)
+                        def _(j=j):
+                            if (j, k) == (1, 1):
+                                m_copy(l).start()
+                            run(steps[2 * j + k])
+
             attend_rows(
-                count - 1 - n, qblock, qcode_ref, kcode_ref, q_ref, k_ref, v_ref, mixed_ref, lse_cols
+                count - 1 - n,
+                qblock,
+                qcode_ref,
+                kcode_ref,
+                q_ref,
+                k_ref,
+                v_ref,
+                mixed_ref,
+                lse_cols,
+                between,
             )
-            for j in range(count):
-
-                @pl.when(n == j)
-                def _(j=j):
-                    if j == 1:
-                        m_copy(l).start()
-                    run(steps[j])
-
             return 0
 
         lax.fori_loop(0, count, one_block, 0)
@@ -654,9 +697,9 @@
             return 0
 
         lax.fori_loop(0, 2, inner, 0)
-        run(take(9 * l + 10 - l))
+        run(take(7 if l == 0 else 13))
         lax.fori_loop(2, MP, inner, 0)
-        run(take(10 if l == 0 else 18))
+        run(take(8 if l == 0 else turns))
         step_ready(3 * l + 2)
         wback_load = load(w_all.at[3 * l + 2], wback, 4)
         store(("e", l), e_ref, es.at[:, pl.ds(0, rows), :])
@@ -761,17 +804,17 @@
             pltpu.VMEM((rows, width), BF16),
             pltpu.VMEM((MP, rows, width), BF16),
             pltpu.VMEM((MP, rows, width), BF16),
-            sem((chunks, 3)),
-            sem((chunks, 3)),
-            sem((chunks, 3)),
-            sem((chunks, 3)),
-            sem((chunks, 4)),
-            sem((chunks, 4)),
+            sem((chunks * SPLIT, 3)),
+            sem((chunks * SPLIT, 3)),
+            sem((chunks * SPLIT, 3)),
+            sem((chunks * SPLIT, 3)),
+            sem((chunks * SPLIT, 4)),
+            sem((chunks * SPLIT, 4)),
             sem((n_layers, 6)),
             sem((n_layers, 6)),
             sem((6,)),
             sem((6,)),
-            sem((chunks + 3,)),
+            sem((chunks * SPLIT + 3,)),
             sem((5,)),
             sem((5 + 11 * n_layers,)),
         ],
@@ -906,11 +949,21 @@
 
 
 def backward_kernel(n_layers, *refs):
-    n_in, per_layer = 7, 11
-    w_all, dy_in, cos_in, sin_in, qrow_ref, kcol_ref, vectors = refs[:n_in]
+    n_in, per_layer = 8, 11
+    w_all, dy_in, cos_in, sin_in, low_in, qrow_ref, kcol_ref, vectors = refs[:n_in]
     saved = [refs[n_in + l * per_layer : n_in + (l + 1) * per_layer] for l in range(n_layers)]
     at = n_in + n_layers * per_layer
-    tokens_out, feed_out, attn_out, small_out = refs[at : at + 4]
+    (
+        tokens_out,
+        result_out,
+        qkv_out,
+        bqkv_out,
+        outw_out,
+        vec_out,
+        in_out,
+        bin_out,
+        back_out,
+    ) = refs[at : at + 9]
     (
         pool,
         gp_ref,
@@ -957,6 +1010,8 @@
         v_stage,
         v_in,
         dbin_ref,
+        across_ref,
+        feed_sum,
         c_send,
         c_recv,
         one_send,
@@ -967,6 +1022,8 @@
         z_recv,
         a_send,
         a_recv,
+        x_send,
+        x_recv,
         v_send,
         v_recv,
         t_send,
@@ -974,10 +1031,10 @@
         w_sem,
         s_sem,
         o_sem,
-    ) = refs[at + 4 :]
+    ) = refs[at + 9 :]
     part_ref, dxs_ref, dxp_ref = r2_ref, h_ref, df_ref
     rows, width = acc_ref.shape
-    height = t_ref.shape[2]
+    height = t_ref.shape[3]
     queries = 2 * rows
 
     d = lax.axis_index("dp")
@@ -988,7 +1045,9 @@
     second = device(groups[2], c, z)
     away = device(groups[0], 1 - c, (z + 2) % MP)
     pair = device(groups[0], c, z + 1 - 2 * (z % 2))
-    columns = [device(groups[0], c, (z + s) % MP) for s in range(1, MP)]
+    mirror = mirrored(z)
+    columns = [device(groups[0], c, mirror[m]) for m in range(1, MP)]
+    across = columns[1]
     moved = c != z // 2
 
     barrier = pltpu.get_barrier_semaphore()
@@ -1009,9 +1068,10 @@
         )
 
     def column(k):
-        return (z - k + MP) % MP
-
-    own_z = [(z - 2 * c - i + MP) % MP for i in range(2)]
+        base = (z + 2 * (k // 2)) % MP
+        return base + (k % 2) * (1 - 2 * (base % 2))
+
+    own_z = head_columns_of(z, c)
 
     def load(source, target, sem):
         return pltpu.make_async_copy(source, target, sem)
@@ -1033,10 +1093,10 @@
             load(gps.at[column(k)], gp_ref.at[slot], w_sem.at[slot, 2]),
         ]
 
-    def e_load(l, k):
-        slot = k % 2
+    def e_load(l, n):
+        slot = n % 2
         es = saved[l][8]
-        return load(es.at[column(k)], pool.at[4 + slot], w_sem.at[slot, 3])
+        return load(es.at[column(MP - 1 - n)], pool.at[4 + slot], w_sem.at[slot, 3])
 
     def late_loads(l):
         _, qs, ks, vs, ms, ls = saved[l][:6]
@@ -1060,7 +1120,9 @@
     dy_load = load(dy_in, df_ref, s_sem.at[11])
     table_loads = [load(cos_in, cos_ref, s_sem.at[12]), load(sin_in, sin_ref, s_sem.at[13])]
     dy_load.start()
-    for copy in early_loads(n_layers - 1) + weight_loads(n_layers - 1, 0):
+    for copy in early_loads(n_layers - 1) + [e_load(n_layers - 1, 0)]:
+        copy.start()
+    for copy in weight_loads(n_layers - 1, 0):
         copy.start()
     for copy in table_loads + late_loads(n_layers - 1):
         copy.start()
@@ -1080,53 +1142,59 @@
             sibling,
         )
 
-    def dxs_copy(l):
-        return remote(dxs_ref, dxc_in, c_send.at[l, 6], c_recv.at[l, 6], sibling)
+    def dxs_copy(l, n):
+        return remote(
+            dxs_ref.at[n], dxc_in.at[n], c_send.at[l, 6 + n], c_recv.at[l, 6 + n], sibling
+        )
 
     def dxp_copy(l):
-        return remote(dxp_ref, dxp_in.at[l], a_send.at[l, 5], a_recv.at[l, 5], pair)
-
-    def one_copy(l, k, n):
+        return remote(dxp_ref, dxp_in.at[l], x_send.at[l], x_recv.at[l], pair)
+
+    def one_copy(l, h, k, n):
         return remote(
-            t_ref.at[k, groups[1 if n == 0 else 3]],
-            one_in.at[k, n],
-            one_send.at[l, k, n],
-            one_recv.at[l, k, n],
+            t_ref.at[h, k, groups[1 if n == 0 else 3]],
+            one_in.at[h, k, n],
+            one_send.at[l, h, k, n],
+            one_recv.at[l, h, k, n],
             first,
         )
 
-    def two_copy(l, k):
+    def two_copy(l, h, k):
         return remote(
-            t_ref.at[k, groups[2]], two_in.at[k], two_send.at[l, k], two_recv.at[l, k], second
-        )
-
-    def z_copy(l, k):
+            t_ref.at[h, k, groups[2]],
+            two_in.at[h, k],
+            two_send.at[l, h, k],
+            two_recv.at[l, h, k],
+            second,
+        )
+
+    def z_copy(l, h, k):
         return remote(
-            t_ref.at[k, groups[0]],
-            z_in.at[l, k - 1],
-            z_send.at[l, k],
-            z_recv.at[l, k],
-            device(groups[0], c, column(k)),
+            across_ref.at[h] if k == 2 else t_ref.at[h, k, groups[0]],
+            z_in.at[l, h, k - 1],
+            z_send.at[l, h, k],
+            z_recv.at[l, h, k],
+            across if k == 2 else pair,
         )
 
     def span(group):
         return pl.ds(pl.multiple_of(group * 2 * height, 32), 2 * height)
 
-    def a_one_copy(l, n):
+    def a_one_copy(l, i, n):
         return remote(
-            ta_ref.at[:, span(groups[1 if n == 0 else 3]), :],
-            a_one_in.at[n],
-            a_send.at[l, n],
-            a_recv.at[l, n],
+            ta_ref.at[i, span(groups[1 if n == 0 else 3]), :],
+            a_one_in.at[i, n],
+            a_send.at[l, i, n],
+            a_recv.at[l, i, n],
             first,
         )
 
-    def a_two_copy(l):
+    def a_two_copy(l, i):
         return remote(
-            ta_ref.at[:, span(groups[2]), :],
-            a_two_in,
-            a_send.at[l, 2],
-            a_recv.at[l, 2],
+            ta_ref.at[i, span(groups[2]), :],
+            a_two_in.at[i],
+            a_send.at[l, i, 2],
+            a_recv.at[l, i, 2],
             second,
         )
 
@@ -1134,15 +1202,13 @@
         return remote(
             ta_ref.at[i, span(groups[0]), :],
             a_z_in.at[i],
-            a_send.at[l, 3 + i],
-            a_recv.at[l, 3 + i],
-            device(groups[0], c, own_z[i]),
+            a_send.at[l, i, 3],
+            a_recv.at[l, i, 3],
+            pair if i == 1 else across,
         )
 
     def a_c_copy(l):
-        return remote(
-            a_out_ref, a_c_in.at[l], c_send.at[l, 7], c_recv.at[l, 7], sibling
-        )
+        return remote(a_out_ref, a_c_in.at[l], c_send.at[l, 8], c_recv.at[l, 8], sibling)
 
     def v_copy(l, n):
         to = (sibling, first, second, columns[0], columns[1], columns[2])[n]
@@ -1150,66 +1216,82 @@
             v_stage.at[l, min(n, 3)], v_in.at[l, n], v_send.at[l, n], v_recv.at[l, n], to
         )
 
-    def step_one(l, k):
+    def step_one(l, h, k):
         for n in range(2):
-            one_copy(l, k, n).wait_recv()
+            one_copy(l, h, k, n).wait_recv()
         g = groups[2]
-        t_ref[k, g] = (t_ref[k, g].astype(F32) + one_in[k, 1].astype(F32)).astype(BF16)
-        two_copy(l, k).start()
-
-    def step_two(l, k):
-        two_copy(l, k).wait_recv()
+        t_ref[h, k, g] = (t_ref[h, k, g].astype(F32) + one_in[h, k, 1].astype(F32)).astype(BF16)
+        two_copy(l, h, k).start()
+
+    def step_two(l, h, k):
+        two_copy(l, h, k).wait_recv()
         g = groups[0]
-        t_ref[k, g] = (
-            t_ref[k, g].astype(F32) + one_in[k, 0].astype(F32) + two_in[k].astype(F32)
-        ).astype(BF16)
-        if k > 0:
-            z_copy(l, k).start()
-
-    def step_feed_end(l):
-        total = t_ref[0, groups[0]].astype(F32)
-        for k in range(1, MP):
-            z_copy(l, k).wait_recv()
-            total = total + z_in[l, k - 1].astype(F32)
-        feed_out[l] = total
-
-    def step_a_one(l):
+        total = (
+            t_ref[h, k, g].astype(F32) + one_in[h, k, 0].astype(F32) + two_in[h, k].astype(F32)
+        )
+        if k == 0:
+            feed_sum[h] = total
+            return
+        if k == 2:
+            z_copy(l, h, 3).wait_recv()
+            if l + 1 < n_layers:
+                z_copy(l + 1, h, 2).wait_send()
+            across_ref[h] = (total + z_in[l, h, 2].astype(F32)).astype(BF16)
+        else:
+            t_ref[h, k, g] = total.astype(BF16)
+        z_copy(l, h, k).start()
+
+    def step_feed_end(l, h):
+        total = feed_sum[h]
+        for k in range(1, MP - 1):
+            z_copy(l, h, k).wait_recv()
+            total = total + z_in[l, h, k - 1].astype(F32)
+        if h == 1:
+            in_out[l] = total
+        else:
+            back_out[l] = jnp.transpose(total)
+
+    def feed_sent(l, h):
+        for k in range(MP):
+            for n in range(2):
+                one_copy(l, h, k, n).wait_send()
+            two_copy(l, h, k).wait_send()
+            if k in (1, 3):
+                z_copy(l, h, k).wait_send()
+
+    def step_a_one(l, i):
         for n in range(2):
-            a_one_copy(l, n).wait_recv()
-        for i in range(2):
-            at = span(groups[2])
-            ta_ref[i, at, :] = (
-                ta_ref[i, at, :].astype(F32) + a_one_in[1, i].astype(F32)
-            ).astype(BF16)
-        a_two_copy(l).start()
-
-    def step_a_two(l):
-        a_two_copy(l).wait_recv()
-        for i in range(2):
-            at = span(groups[0])
-            ta_ref[i, at, :] = (
-                ta_ref[i, at, :].astype(F32)
-                + a_one_in[0, i].astype(F32)
-                + a_two_in[i].astype(F32)
-            ).astype(BF16)
-
-        @pl.when(c == 1)
-        def _():
-            a_z_copy(l, 0).start()
-
-        a_z_copy(l, 1).start()
+            a_one_copy(l, i, n).wait_recv()
+        at = span(groups[2])
+        ta_ref[i, at, :] = (ta_ref[i, at, :].astype(F32) + a_one_in[i, 1].astype(F32)).astype(BF16)
+        a_two_copy(l, i).start()
+
+    def step_a_two(l, i):
+        a_two_copy(l, i).wait_recv()
+        at = span(groups[0])
+        total = (
+            ta_ref[i, at, :].astype(F32)
+            + a_one_in[i, 0].astype(F32)
+            + a_two_in[i].astype(F32)
+        )
+        if i == 1:
+            ta_ref[i, at, :] = total.astype(BF16)
+            a_z_copy(l, 1).start()
+        else:
+            a_z_copy(l, 1).wait_recv()
+            total = total + a_z_in[1].astype(F32)
+            a_sum_ref[...] = total
+
+            @pl.when(c == 1)
+            def _():
+                ta_ref[i, at, :] = total.astype(BF16)
+                a_z_copy(l, 0).start()
 
     def step_a_z(l):
-        a_z_copy(l, 1).wait_recv()
-
-        @pl.when(c == 0)
-        def _():
-            a_sum_ref[...] = ta_ref[0, span(groups[0]), :].astype(F32) + a_z_in[1].astype(F32)
-
         @pl.when(c == 1)
         def _():
             a_z_copy(l, 0).wait_recv()
-            a_sum_ref[...] = a_z_in[0].astype(F32) + a_z_in[1].astype(F32)
+            a_sum_ref[...] = a_z_in[0].astype(F32)
 
         other = pl.ds(pl.multiple_of((1 - c) * height, 32), height)
         a_out_ref[...] = a_sum_ref[other, :].astype(BF16)
@@ -1218,7 +1300,29 @@
     def step_a_end(l):
         a_c_copy(l).wait_recv()
         own = pl.ds(pl.multiple_of(c * height, 32), height)
-        attn_out[l] = a_sum_ref[own, :] + a_c_in[l].astype(F32)
+        total = a_sum_ref[own, :] + a_c_in[l].astype(F32)
+        tile = [total[:, n * LANES : (n + 1) * LANES] for n in range(6)]
+        turned_one = pltpu.roll(tile[1], HD, 1)
+        turned_four = pltpu.roll(tile[4], HD, 1)
+        for n, (two, one) in enumerate(
+            ((tile[0], tile[1]), (tile[2], turned_one), (tile[3], tile[4]))
+        ):
+            qkv_out[l, n, :, 0:LANES] = two
+            qkv_out[l, n, :, LANES:] = one[:, :HD]
+        outw_out[l, 0:LANES, :] = jnp.transpose(tile[5])
+        outw_out[l, LANES:, :] = jnp.transpose(turned_four)[:HD]
+
+    def a_sent(l, i):
+        for n in range(2):
+            a_one_copy(l, i, n).wait_send()
+        a_two_copy(l, i).wait_send()
+        if i == 1:
+            a_z_copy(l, 1).wait_send()
+        else:
+
+            @pl.when(c == 1)
+            def _():
+                a_z_copy(l, 0).wait_send()
 
     def step_v(l, n):
         v_copy(l, n - 1).wait_recv()
@@ -1237,12 +1341,19 @@
             v_copy(l, 2 + s).wait_recv()
             got = v_in[l, 2 + s]
             total = total + got[0:6, :]
-            one = one + got[6 + MP - s : 7 + MP - s, :]
-            two = two + got[10 + MP - s : 11 + MP - s, :]
-        small_out[l, 0:6, :] = total
-        small_out[l, 6:7, :] = one
-        small_out[l, 7:8, :] = two
-
+            one = one + got[6 + s : 7 + s, :]
+            two = two + got[10 + s : 11 + s, :]
+        vec_out[l] = total
+        bin_out[l] = one
+        turned_one = pltpu.roll(two[:, LANES : 2 * LANES], HD, 1)
+        for n, at in enumerate((0, 2, 3)):
+            bqkv_out[l, n : n + 1, 0:LANES] = two[:, at * LANES : (at + 1) * LANES]
+        bqkv_out[l, 0:1, LANES:] = two[:, LANES : LANES + HD]
+        bqkv_out[l, 1:2, LANES:] = turned_one[:, :HD]
+        bqkv_out[l, 2:3, LANES:] = two[:, 4 * LANES : 4 * LANES + HD]
+
+    result_copy = remote(low_in, result_out, t_send.at[1], t_recv.at[1], away)
+    result_local = pltpu.make_async_copy(low_in, result_out, o_sem.at[1])
     kblock = 256
     for l in reversed(range(n_layers)):
         top = l == n_layers - 1
@@ -1253,7 +1364,6 @@
             acc_ref[...] = df_ref[...].astype(F32)
         else:
             dxp_copy(l + 1).wait_send()
-            step_a_one(l + 1)
         for copy in copies:
             copy.wait()
         v_stage[l, 0] = jnp.zeros((16, width), F32)
@@ -1262,6 +1372,46 @@
         if top:
             pl.semaphore_wait(barrier, len(partners))
         df_copy(l).start()
+        if top:
+
+            @pl.when(moved)
+            def _():
+                result_copy.start()
+
+            @pl.when(jnp.logical_not(moved))
+            def _():
+                result_local.start()
+
+        def turned(source, target, half):
+            turn_ref[...] = jnp.transpose(source)
+            for g in range(4):
+                at = pl.ds(pl.multiple_of((2 * g + c) * height, 32), height)
+                target[pl.ds(g * height, height), pl.ds(half * rows, rows)] = turn_ref[at, :]
+
+        turned(df_ref[...], dft_ref, 0)
+        turned(h_ref[0], ht_ref, 0)
+        turned(h_ref[1], ht_ref, 1)
+        if not top:
+            feed_sent(l + 1, 0)
+            step_v(l + 1, 1)
+        df_copy(l).wait_recv()
+        turned(dfin_ref[...], dft_ref, 1)
+
+        def back_grads(n, _, l=l):
+            e_load(l, n).wait()
+
+            @pl.when(n + 1 < MP)
+            def _():
+                e_load(l, n + 1).start()
+
+            k = MP - 1 - n
+            grad = nn(dft_ref[...], pool[4 + n % 2]).astype(BF16)
+            t_ref[0, k] = grad.reshape(4, height, width)
+            for to in range(2):
+                one_copy(l, 0, k, to).start()
+            return 0
+
+        lax.fori_loop(0, MP, back_grads, 0)
         if not top:
             for k in range(MP):
                 du_copy(l + 1, k).wait_send()
@@ -1288,54 +1438,37 @@
         lax.fori_loop(0, MP, inner, 0)
         for copy in x_loads(l):
             copy.start()
-        e_load(l, 0).start()
         for k in range(MP):
             v_stage[l, 0, 6 + k : 7 + k, :] = dbin_ref[k]
         if not top:
-            step_a_two(l + 1)
+            step_a_one(l + 1, 0)
+            for h in range(2):
+                step_feed_end(l + 1, h)
+            step_v(l + 1, 2)
             da_copy(l + 1).wait_send()
+        for k in (3, 2, 1, 0):
+            step_one(l, 0, k)
         sums = norm_back_rows(acc_ref, r1_ref, da_ref, vec[1:2, :])
         v_stage[l, 0, 1:2, :], v_stage[l, 0, 2:3, :], v_stage[l, 0, 0:1, :] = sums
         da_copy(l).start()
-
-        def turned(source, target, half):
-            turn_ref[...] = jnp.transpose(source)
-            for g in range(4):
-                at = pl.ds(pl.multiple_of((2 * g + c) * height, 32), height)
-                target[pl.ds(g * height, height), pl.ds(half * rows, rows)] = turn_ref[at, :]
-
-        turned(h_ref[0], ht_ref, 0)
-        turned(h_ref[1], ht_ref, 1)
-        turned(df_ref[...], dft_ref, 0)
-        df_copy(l).wait_recv()
-        turned(dfin_ref[...], dft_ref, 1)
         if not top:
-            for k in range(MP):
-                for n in range(2):
-                    one_copy(l + 1, k, n).wait_send()
-                two_copy(l + 1, k).wait_send()
-                if k > 0:
-                    z_copy(l + 1, k).wait_send()
-
-        def outer(k, _, l=l):
-            e_load(l, k).wait()
-
-            @pl.when(k + 1 < MP)
-            def _():
-                e_load(l, k + 1).start()
-
-            back = nn(dft_ref[...], pool[4 + k % 2]).astype(BF16)
-            t_ref[k, :, :, pl.ds(width, width)] = back.reshape(4, height, width)
+            feed_sent(l + 1, 1)
+
+        def in_grads(n, _, l=l):
+            k = MP - 1 - n
             du_copy(l, k).wait_recv()
-            into = nn(ht_ref[...], du_ref[k]).astype(BF16)
-            t_ref[k, :, :, pl.ds(0, width)] = into.reshape(4, height, width)
-            for n in range(2):
-                one_copy(l, k, n).start()
+            grad = nn(ht_ref[...], du_ref[k]).astype(BF16)
+            t_ref[1, k] = grad.reshape(4, height, width)
+            for to in range(2):
+                one_copy(l, 1, k, to).start()
             return 0
 
-        lax.fori_loop(0, MP, outer, 0)
+        lax.fori_loop(0, MP, in_grads, 0)
         if not top:
-            step_a_z(l + 1)
+            step_a_two(l + 1, 0)
+            step_v(l + 1, 3)
+        for k in (3, 1, 0):
+            step_two(l, 0, k)
         for copy in late_loads(l):
             copy.wait()
         da_copy(l).wait_recv()
@@ -1359,19 +1492,35 @@
         if top:
             for copy in table_loads:
                 copy.wait()
+        steps = [[] for _ in range(6)]
         if not top:
-            step_a_end(l + 1)
-
-        steps = [[] for _ in range(6)]
-        for k in range(MP):
-            steps[k].append(partial(step_one, l, k))
-            steps[k + 1].append(partial(step_two, l, k))
-        steps[5].append(partial(step_feed_end, l))
-        if not top:
-            for n in range(1, 4):
-                steps[n - 1].append(partial(step_v, l + 1, n))
-            steps[3].append(partial(step_v_end, l + 1))
-        for i in range(2):
+            steps[0] = [partial(step_v_end, l + 1), partial(step_a_z, l + 1)]
+            steps[1] = [partial(step_a_end, l + 1)]
+        steps[1].append(partial(step_two, l, 0, 2))
+        steps[1] += [partial(step_one, l, 1, k) for k in (3, 2, 1, 0)]
+        steps[3] = [partial(step_two, l, 1, k) for k in (3, 1, 0)]
+        steps[4] = [partial(step_two, l, 1, 2), partial(step_a_one, l, 1)]
+        steps[5] = [partial(step_a_two, l, 1)]
+
+        def weight_grads(i, l=l, top=top):
+            if not top:
+                a_sent(l + 1, i)
+                if i == 0:
+                    a_c_copy(l + 1).wait_send()
+            low = [pool.at[2 + 2 * i + half] for half in range(2)]
+            ta_ref[i, :, 0:LANES] = nn(pool[0], low[0][:, 0:LANES]).astype(BF16)
+            more = nn(pool[0], low[0][:, LANES : 5 * LANES]) + nn(
+                pool[1], low[1][:, LANES : 5 * LANES]
+            )
+            ta_ref[i, :, LANES : 4 * LANES] = more[:, : 3 * LANES].astype(BF16)
+            ta_ref[i, :, 4 * LANES : 5 * LANES] = (
+                more[:, 3 * LANES :] + dwo_ref[i, :, 0:LANES].astype(F32)
+            ).astype(BF16)
+            ta_ref[i, :, 5 * LANES :] = dwo_ref[i, :, LANES:]
+            for n in range(2):
+                a_one_copy(l, i, n).start()
+
+        for turn, i in enumerate((1, 0)):
             for h in range(3):
                 head_back(
                     i,
@@ -1389,7 +1538,7 @@
                     dqt_ref,
                     dt_ref,
                 )
-                for step in steps[3 * i + h]:
+                for step in steps[3 * turn + h]:
                     step()
             for tile in range(5):
                 total = jnp.zeros((1, LANES), F32)
@@ -1404,6 +1553,8 @@
                     v_stage[
                         l, 0, 10 + 2 * core + i : 11 + 2 * core + i, tile * LANES : (tile + 1) * LANES
                     ] = jnp.where(c == core, total, 0.0)
+            if i == 1:
+                weight_grads(1)
         v_copy(l, 0).start()
 
         def spread(n):
@@ -1418,40 +1569,22 @@
 
         df_copy(l).wait_send()
         dxs_ref[1] = spread(3).astype(BF16)
-        dxs_ref[0] = spread(1).astype(BF16)
-        dxs_copy(l).start()
+        dxs_copy(l, 1).start()
         part_ref[...] = spread(2)
-        dxs_copy(l).wait_recv()
+        dxs_copy(l, 1).wait_recv()
         dxp_ref[...] = (part_ref[...] + dxc_in[1].astype(F32)).astype(BF16)
         dxp_copy(l).start()
-        acc_ref[...] += spread(0) + dxc_in[0].astype(F32)
-        if not top:
+        dxs_ref[0] = spread(1).astype(BF16)
+        dxs_copy(l, 0).start()
+        acc_ref[...] += spread(0)
+        weight_grads(0)
+        dxs_copy(l, 0).wait_recv()
+        acc_ref[...] += dxc_in[0].astype(F32)
+        if l > 0:
             for n in range(2):
-                a_one_copy(l + 1, n).wait_send()
-            a_two_copy(l + 1).wait_send()
-            a_z_copy(l + 1, 1).wait_send()
-
-            @pl.when(c == 1)
-            def _(l=l):
-                a_z_copy(l + 1, 0).wait_send()
-
-            a_c_copy(l + 1).wait_send()
-        for i in range(2):
-            low = [pool.at[2 + 2 * i + half] for half in range(2)]
-            ta_ref[i, :, 0:LANES] = nn(pool[0], low[0][:, 0:LANES]).astype(BF16)
-            more = nn(pool[0], low[0][:, LANES : 5 * LANES]) + nn(
-                pool[1], low[1][:, LANES : 5 * LANES]
-            )
-            ta_ref[i, :, LANES : 4 * LANES] = more[:, : 3 * LANES].astype(BF16)
-            ta_ref[i, :, 4 * LANES : 5 * LANES] = (
-                more[:, 3 * LANES :] + dwo_ref[i, :, 0:LANES].astype(F32)
-            ).astype(BF16)
-            ta_ref[i, :, 5 * LANES :] = dwo_ref[i, :, LANES:]
-        for n in range(2):
-            a_one_copy(l, n).start()
-        if l > 0:
-            dxs_copy(l).wait_send()
-            for copy in early_loads(l - 1) + weight_loads(l - 1, 0) + late_loads(l - 1):
+                dxs_copy(l, n).wait_send()
+            first_loads = early_loads(l - 1) + [e_load(l - 1, 0)] + weight_loads(l - 1, 0)
+            for copy in first_loads + late_loads(l - 1):
                 copy.start()
         dxp_copy(l).wait_recv()
         acc_ref[...] += dxp_in[l].astype(F32)
@@ -1465,9 +1598,11 @@
         back_copy.start()
 
     step_v(0, 1)
-    step_a_one(0)
+    for h in range(2):
+        step_feed_end(0, h)
+    step_a_one(0, 0)
     step_v(0, 2)
-    step_a_two(0)
+    step_a_two(0, 0)
     step_v(0, 3)
     step_v_end(0)
 
@@ -1485,32 +1620,30 @@
     @pl.when(moved)
     def _():
         back_copy.wait_send()
+        result_copy.wait_send()
+        result_copy.wait_recv()
+
+    @pl.when(jnp.logical_not(moved))
+    def _():
+        result_local.wait()
 
     da_copy(0).wait_send()
-    dxs_copy(0).wait_send()
+    for n in range(2):
+        dxs_copy(0, n).wait_send()
     for k in range(MP):
         du_copy(0, k).wait_send()
-        for n in range(2):
-            one_copy(0, k, n).wait_send()
-        two_copy(0, k).wait_send()
-        if k > 0:
-            z_copy(0, k).wait_send()
-    for n in range(2):
-        a_one_copy(0, n).wait_send()
-    a_two_copy(0).wait_send()
-    a_z_copy(0, 1).wait_send()
-
-    @pl.when(c == 1)
-    def _():
-        a_z_copy(0, 0).wait_send()
-
+    for h in range(2):
+        feed_sent(0, h)
+        z_copy(0, h, 2).wait_send()
+    for i in range(2):
+        a_sent(0, i)
     a_c_copy(0).wait_send()
     for l in range(n_layers):
         for n in range(6):
             v_copy(l, n).wait_send()
 
 
-def backward(w_all, dy, cos, sin, qrow, kcol, vectors, states):
+def backward(w_all, dy, cos, sin, low, qrow, kcol, vectors, states):
     n_layers, _, width = vectors.shape
     rows = dy.shape[0]
     height = width // 8
@@ -1521,12 +1654,17 @@
         partial(backward_kernel, n_layers),
         out_shape=(
             shape((rows, width), F32),
-            shape((n_layers, height, 2 * width), F32),
+            shape((rows, width), BF16),
+            shape((n_layers, 3, height, 3 * HD), F32),
+            shape((n_layers, 3, 3 * HD), F32),
+            shape((n_layers, 3 * HD, height), F32),
+            shape((n_layers, 6, width), F32),
             shape((n_layers, height, width), F32),
-            shape((n_layers, 8, width), F32),
+            shape((n_layers, 1, width), F32),
+            shape((n_layers, width, height), F32),
         ),
-        in_specs=[anywhere()] * 4 + [vmem()] * 3 + [anywhere()] * len(flat),
-        out_specs=(anywhere(), vmem(), vmem(), vmem()),
+        in_specs=[anywhere()] * 5 + [vmem()] * 3 + [anywhere()] * len(flat),
+        out_specs=(anywhere(), anywhere()) + (vmem(),) * 7,
         scratch_shapes=[
             pltpu.VMEM((7, width, width), BF16),
             pltpu.VMEM((2, rows, width), BF16),
@@ -1542,10 +1680,10 @@
             pltpu.VMEM((4 * height, 2 * rows), BF16),
             pltpu.VMEM((4 * height, 2 * rows), BF16),
             pltpu.VMEM((MP, 2 * rows, width), BF16),
-            pltpu.VMEM((MP, 4, height, 2 * width), BF16),
-            pltpu.VMEM((MP, 2, height, 2 * width), BF16),
-            pltpu.VMEM((MP, height, 2 * width), BF16),
-            pltpu.VMEM((n_layers, MP - 1, height, 2 * width), BF16),
+            pltpu.VMEM((2, MP, 4, height, width), BF16),
+            pltpu.VMEM((2, MP, 2, height, width), BF16),
+            pltpu.VMEM((2, MP, height, width), BF16),
+            pltpu.VMEM((n_layers, 2, MP - 1, height, width), BF16),
             pltpu.VMEM((2, width, 2 * LANES), BF16),
             pltpu.VMEM((2, width, width), BF16),
             pltpu.VMEM((2, 2, 2 * height, width), BF16),
@@ -1573,23 +1711,27 @@
             pltpu.VMEM((n_layers, 4, 16, width), F32),
             pltpu.VMEM((n_layers, 6, 16, width), F32),
             pltpu.VMEM((MP, 1, width), F32),
-            sem((n_layers, 8)),
-            sem((n_layers, 8)),
-            sem((n_layers, MP, 2)),
-            sem((n_layers, MP, 2)),
-            sem((n_layers, MP)),
-            sem((n_layers, MP)),
-            sem((n_layers, MP)),
-            sem((n_layers, MP)),
+            pltpu.VMEM((2, height, width), BF16),
+            pltpu.VMEM((2, height, width), F32),
+            sem((n_layers, 9)),
+            sem((n_layers, 9)),
+            sem((n_layers, 2, MP, 2)),
+            sem((n_layers, 2, MP, 2)),
+            sem((n_layers, 2, MP)),
+            sem((n_layers, 2, MP)),
+            sem((n_layers, 2, MP)),
+            sem((n_layers, 2, MP)),
+            sem((n_layers, 2, 4)),
+            sem((n_layers, 2, 4)),
+            sem((n_layers,)),
+            sem((n_layers,)),
             sem((n_layers, 6)),
             sem((n_layers, 6)),
-            sem((n_layers, 6)),
-            sem((n_layers, 6)),
-            sem((1,)),
-            sem((1,)),
+            sem((2,)),
+            sem((2,)),
             sem((2, 4)),
             sem((18,)),
-            sem((1,)),
+            sem((2,)),
         ],
         compiler_params=pltpu.CompilerParams(
             vmem_limit_bytes=BACK_LIMIT, collective_id=1, has_side_effects=True
@@ -1598,7 +1740,7 @@
             flops=200_000_000_000, bytes_accessed=100_000_000, transcendentals=20_000_000
         ),
         name="backward",
-    )(w_all, dy, cos, sin, qrow, kcol, vectors, *flat)
+    )(w_all, dy, cos, sin, low, qrow, kcol, vectors, *flat)
 
 
 def attend_kernel(chunk, *refs):
@@ -2168,28 +2310,18 @@
     if pieces == 8:
         head, states = forward(blocks, tokens, cotangent, small, meta, frequency, vectors)
         w_all, dy, low, cos, sin, qrow, kcol = head
-        result = relayout(low)
-        grad_tokens, feed_grads, attn_grads, small_grads = backward(
-            w_all, dy, cos, sin, qrow, kcol, vectors, states
-        )
-        grad_qkv = jnp.stack(head_columns(attn_grads), axis=1)
-        grad_in = feed_grads[:, :, :width]
-        grad_back = jnp.swapaxes(feed_grads[:, :, width:], 1, 2)
-        grad_out = jnp.concatenate(
-            [attn_grads[:, :, 5 * LANES :], attn_grads[:, :, 4 * LANES + HD : 5 * LANES]], axis=-1
-        )
-        grad_out = jnp.swapaxes(grad_out, 1, 2)
-        grad_b_qkv = jnp.stack(head_columns(small_grads[:, 7, :]), axis=1)
+        grads = backward(w_all, dy, cos, sin, low, qrow, kcol, vectors, states)
+        grad_tokens, result, grad_qkv, grad_b_qkv, grad_out, grad_vec, grad_in = grads[:7]
         return (
             result,
             grad_tokens,
             grad_qkv,
             grad_b_qkv,
             grad_out,
-            small_grads[:, :6],
+            grad_vec,
             grad_in,
-            small_grads[:, 6],
-            grad_back,
+            grads[7].reshape(layers, width),
+            grads[8],
         )
 
     head, states = plain_forward(blocks, tokens, cotangent, small, meta, frequency, vectors)

time: 463 us -> 420 us (0.907)
  the two profiles are of different devices: /device:TPU:27 before, /device:TPU:0 now
where the time goes in v4:
time: 420 us; the launch traced here: 412 us
  Pallas kernels  388 us (92%)
  local copies, waits for them, and re-layouts  19.4 us (5%)
    pallas_call x1, Pallas kernels, backward(): pl.pallas_call(partial(backward_kernel, n_layers), out_shape=(shape((rows...  208 us
    pallas_call x1, Pallas kernels, forward(): pl.pallas_call(partial(forward_kernel, n_layers), out_shape=outs, in_spec...  180 us
    unnamed x30, local copies, waits for them, and re-layouts  15 us

profile of v4, /device:TPU:0, one launch (start us, length us, event | category | flops | bytes accessed | tf_op | source)
XLA Modules:
  0.0 412.0 jit_solution(13079232224992446010)
XLA Ops:
  0.6 0.0 copy-start.1
  1.4 0.7 add_convert_fusion
  2.2 0.5 fusion.4.refs_5_
  2.7 0.7 slice_bitcast_fusion.13
  3.4 0.7 slice_bitcast_fusion.12
  4.0 0.7 broadcast_in_dim.5.refs_4_
  4.7 0.7 slice_bitcast_fusion.10
  5.4 0.8 concatenate.16
  6.2 0.6 pad.8.refs_3_
  6.8 1.4 copy.21.refs_6_.refs_7_
  8.2 1.0 copy.20
  9.3 1.1 convert.18
  10.4 0.0 copy-done.1
  10.5 0.0 copy-done.2
  10.6 0.1 concatenate.15
  10.7 0.1 concatenate.14
  10.9 0.0 copy-start.6
  10.9 0.9 copy-done.6
  11.8 180.4 %forward.1 = (bf16[6,4,768,768]{3,2,1,0:T(8,128)(2,1)}, bf16[384,768]{1,0:T(8,128)(2,1)}, bf16[384,768]{1,0:T(8,128)(2,1)}, f32[1536,128]{1,0:T(8,128)}, f32[153...) custom-call(bf16[6,96,768]{2,1,0:T(8,128)(2,1)} %copy-done.6, ...), custom_call_target="tpu_custom_call" | custom-call | flops 99999997952 | bytes 100000000 | tf_op jit(solution)/shard_map/forward/pallas_call | solution.py:775
  192.2 207.9 %backward.1 = (f32[384,768]{1,0:T(8,128)}, bf16[384,768]{1,0:T(8,128)(2,1)}, f32[2,3,96,192]{3,2,1,0:T(8,128)}, f32[2,3,192]{2,1,0:T(4,128)}, f32[2,192,96]{2,1,...) custom-call(bf16[6,4,768,768]{3,2,1,0:T(8,128)(2,1)} %get-tuple-element, ...), custom_call_target="tpu_custom_call" | custom-call | flops 199999995904 | bytes 100000000 | tf_op jit(solution)/shard_map/backward/pallas_call | solution.py:1653
  400.2 1.4 copy.23
  401.5 1.3 copy.28
  402.8 1.4 copy.24
  404.3 2.2 copy.25
  406.5 2.0 copy.40
  408.5 0.0 copy-done
  408.5 1.0 copy.41
  409.5 0.8 copy.42
  410.3 0.0 copy-done.5
  410.3 0.7 copy.43
  411.0 0.0 copy-done.3
  411.0 0.8 copy.44
  (26 shorter events, 0.2 us)
Async XLA Ops:
  0.6 9.8 %copy-start.1 = (f32[2,768,96]{1,2,0:T(8,128)S(1)}, f32[2,768,96]{1,2,0:T(8,128)}, u32[]{:S(2)}) copy-start(f32[2,768,96]{1,2,0:T(8,128)} %param.18) | copy-start | bytes 1769476
  0.7 9.8 %copy-start.2 = (f32[2,3,96,192]{3,2,1,0:T(8,128)S(1)}, f32[2,3,96,192]{3,2,1,0:T(8,128)}, u32[]{:S(2)}) copy-start(f32[2,3,96,192]{3,2,1,0:T(8,128)} %param.12) | copy-start | bytes 1327108
  10.9 0.9 copy-start.6
  400.1 8.3 %copy-start = (f32[384,768]{1,0:T(8,128)S(1)}, f32[384,768]{1,0:T(8,128)}, u32[]{:S(2)}) copy-start(f32[384,768]{1,0:T(8,128)} %get-tuple-element.114) | copy-start | bytes 3538948
  406.5 3.0 copy-start.4
  408.5 1.8 copy-start.5
  408.5 2.5 copy-start.3

commit v5 on v4

--- a/solution.py
+++ b/solution.py
@@ -440,12 +440,16 @@
     def take(until):
         steps = []
         for n in range(position[0], until):
-            if n < parts:
+            if n < 2:
                 steps.append(partial(step_plane, n))
             if 0 <= n - 2:
                 steps.append(partial(step_last, n - 2))
             if 0 <= n - 1 < parts:
                 steps.append(partial(step_forward, n - 1))
+            if n == 2:
+                steps.append(partial(step_plane, 2))
+            if 2 <= n < parts - 1:
+                steps.append(partial(step_plane, n + 1))
         position[0] = max(position[0], until)
         return steps
 
@@ -588,10 +592,13 @@
         last = l - 1
         go(x_copy, l, 0)
         go(x_copy, l, 1)
-        run(take(2 if l == 0 else 9))
-        x_copy(l, 0).wait_recv()
-        go(x_copy, l, 2)
-        run(take(4 if l == 0 else 10))
+        if l == 0:
+            run(take(2))
+            x_copy(l, 0).wait_recv()
+            go(x_copy, l, 2)
+            run(take(4))
+        else:
+            run(take(10))
         step_ready(3 * l)
         wa_loads = [
             load(w_all.at[3 * l, own_z[k], :, pl.ds(0, 5 * LANES)], wa.at[k], k) for k in range(2)
@@ -619,8 +626,11 @@
         for i in range(4):
             if i == 1:
                 x_copy(l, 1).wait_recv()
+            if i == 2 and l > 0:
+                x_copy(l, 0).wait_recv()
+                go(x_copy, l, 2)
             if i == 3:
-                run(take(5 if l == 0 else 10))
+                run(take(5 if l == 0 else 11))
                 x_copy(l, 2).wait_recv()
             at = pl.ds(i * rows, rows)
             for k in range(2):
@@ -632,19 +642,22 @@
         store(("k", l), k_ref, ks)
         store(("v", l), v_ref, vs)
         store(("x", l), xfull.at[l], xs)
-        ends = (5, 5, 6, 6, 6, 7) if l == 0 else (11, 11, 11, 12, 12, 13)
+        ends = (5, 5, 6, 6, 6, 7) if l == 0 else (11, 12, 12, 12, 13, 13)
         steps = [take(end) for end in ends]
 
         def one_block(n, _, l=l, steps=steps):
             def between(k):
                 for j in range(count):
-                    if steps[2 * j + k] or (j, k) == (1, 1):
+                    if steps[2 * j + k] or (j, k) in ((1, 1), (2, 0)):
 
                         @pl.when(n == j)
                         def _(j=j):
                             if (j, k) == (1, 1):
                                 m_copy(l).start()
                             run(steps[2 * j + k])
+                            if (j, k) == (2, 0):
+                                step_ready(3 * l + 1)
+                                load(w_all.at[3 * l + 1], win, 3)
 
             attend_rows(
                 count - 1 - n,
@@ -664,8 +677,7 @@
         lse_ref[...] = jnp.transpose(lse_cols[...])[0:8, :]
         store(("mixed", l), mixed_ref, ms)
         store(("lse", l), lse_ref, ls)
-        step_ready(3 * l + 1)
-        win_load = load(w_all.at[3 * l + 1], win, 3)
+        win_load = pltpu.make_async_copy(w_all.at[3 * l + 1], win, w_sem.at[3])
         stored(("r1", last), ("r2", last), ("e", last), ("gp", last), ("h", last))
         if l > 0:
             h_copy(last).wait_send()
@@ -697,11 +709,11 @@
             return 0
 
         lax.fori_loop(0, 2, inner, 0)
-        run(take(7 if l == 0 else 13))
-        lax.fori_loop(2, MP, inner, 0)
         run(take(8 if l == 0 else turns))
+        lax.fori_loop(2, MP - 1, inner, 0)
         step_ready(3 * l + 2)
         wback_load = load(w_all.at[3 * l + 2], wback, 4)
+        lax.fori_loop(MP - 1, MP, inner, 0)
         store(("e", l), e_ref, es.at[:, pl.ds(0, rows), :])
         e_copy(l).start()
         store(("gp", l), gp_ref, gps)
@@ -1147,8 +1159,21 @@
             dxs_ref.at[n], dxc_in.at[n], c_send.at[l, 6 + n], c_recv.at[l, 6 + n], sibling
         )
 
-    def dxp_copy(l):
-        return remote(dxp_ref, dxp_in.at[l], x_send.at[l], x_recv.at[l], pair)
+    halves = [pl.ds(n * (rows // 2), rows // 2) for n in range(2)]
+
+    def dxp_copy(l, n):
+        return remote(
+            dxp_ref.at[halves[n]],
+            dxp_in.at[l, halves[n]],
+            x_send.at[l, n],
+            x_recv.at[l, n],
+            pair,
+        )
+
+    def back_copy(n):
+        return remote(
+            df_ref.at[halves[n]], back_in.at[halves[n]], t_send.at[2 * n], t_recv.at[2 * n], away
+        )
 
     def one_copy(l, h, k, n):
         return remote(
@@ -1363,7 +1388,8 @@
             dy_load.wait()
             acc_ref[...] = df_ref[...].astype(F32)
         else:
-            dxp_copy(l + 1).wait_send()
+            for n in range(2):
+                dxp_copy(l + 1, n).wait_send()
         for copy in copies:
             copy.wait()
         v_stage[l, 0] = jnp.zeros((16, width), F32)
@@ -1441,16 +1467,17 @@
         for k in range(MP):
             v_stage[l, 0, 6 + k : 7 + k, :] = dbin_ref[k]
         if not top:
+            step_a_two(l + 1, 1)
             step_a_one(l + 1, 0)
             for h in range(2):
                 step_feed_end(l + 1, h)
             step_v(l + 1, 2)
             da_copy(l + 1).wait_send()
-        for k in (3, 2, 1, 0):
-            step_one(l, 0, k)
         sums = norm_back_rows(acc_ref, r1_ref, da_ref, vec[1:2, :])
         v_stage[l, 0, 1:2, :], v_stage[l, 0, 2:3, :], v_stage[l, 0, 0:1, :] = sums
         da_copy(l).start()
+        for k in (3, 2, 1, 0):
+            step_one(l, 0, k)
         if not top:
             feed_sent(l + 1, 1)
 
@@ -1467,8 +1494,6 @@
         if not top:
             step_a_two(l + 1, 0)
             step_v(l + 1, 3)
-        for k in (3, 1, 0):
-            step_two(l, 0, k)
         for copy in late_loads(l):
             copy.wait()
         da_copy(l).wait_recv()
@@ -1496,11 +1521,11 @@
         if not top:
             steps[0] = [partial(step_v_end, l + 1), partial(step_a_z, l + 1)]
             steps[1] = [partial(step_a_end, l + 1)]
-        steps[1].append(partial(step_two, l, 0, 2))
+        steps[0] += [partial(step_two, l, 0, k) for k in (3, 1, 0)]
         steps[1] += [partial(step_one, l, 1, k) for k in (3, 2, 1, 0)]
+        steps[2].append(partial(step_two, l, 0, 2))
         steps[3] = [partial(step_two, l, 1, k) for k in (3, 1, 0)]
-        steps[4] = [partial(step_two, l, 1, 2), partial(step_a_one, l, 1)]
-        steps[5] = [partial(step_a_two, l, 1)]
+        steps[5] = [partial(step_two, l, 1, 2), partial(step_a_one, l, 1)]
 
         def weight_grads(i, l=l, top=top):
             if not top:
@@ -1573,7 +1598,8 @@
         part_ref[...] = spread(2)
         dxs_copy(l, 1).wait_recv()
         dxp_ref[...] = (part_ref[...] + dxc_in[1].astype(F32)).astype(BF16)
-        dxp_copy(l).start()
+        for n in range(2):
+            dxp_copy(l, n).start()
         dxs_ref[0] = spread(1).astype(BF16)
         dxs_copy(l, 0).start()
         acc_ref[...] += spread(0)
@@ -1586,18 +1612,19 @@
             first_loads = early_loads(l - 1) + [e_load(l - 1, 0)] + weight_loads(l - 1, 0)
             for copy in first_loads + late_loads(l - 1):
                 copy.start()
-        dxp_copy(l).wait_recv()
-        acc_ref[...] += dxp_in[l].astype(F32)
-
-    dxp_copy(0).wait_send()
-    df_ref[...] = acc_ref[...].astype(BF16)
-    back_copy = remote(df_ref, back_in, t_send.at[0], t_recv.at[0], away)
-
-    @pl.when(moved)
-    def _():
-        back_copy.start()
+        for n in range(2):
+            dxp_copy(l, n).wait_recv()
+            acc_ref[halves[n], :] += dxp_in[l, halves[n], :].astype(F32)
+            if l == 0:
+                dxp_copy(0, n).wait_send()
+                df_ref[halves[n], :] = acc_ref[halves[n], :].astype(BF16)
+
+                @pl.when(moved)
+                def _(n=n):
+                    back_copy(n).start()
 
     step_v(0, 1)
+    step_a_two(0, 1)
     for h in range(2):
         step_feed_end(0, h)
     step_a_one(0, 0)
@@ -1608,7 +1635,8 @@
 
     @pl.when(moved)
     def _():
-        back_copy.wait_recv()
+        for n in range(2):
+            back_copy(n).wait_recv()
         acc_ref[...] = back_in[...].astype(F32)
 
     out_copy = pltpu.make_async_copy(acc_ref, tokens_out, o_sem.at[0])
@@ -1619,7 +1647,8 @@
 
     @pl.when(moved)
     def _():
-        back_copy.wait_send()
+        for n in range(2):
+            back_copy(n).wait_send()
         result_copy.wait_send()
         result_copy.wait_recv()
 
@@ -1723,12 +1752,12 @@
             sem((n_layers, 2, MP)),
             sem((n_layers, 2, 4)),
             sem((n_layers, 2, 4)),
-            sem((n_layers,)),
-            sem((n_layers,)),
+            sem((n_layers, 2)),
+            sem((n_layers, 2)),
             sem((n_layers, 6)),
             sem((n_layers, 6)),
-            sem((2,)),
-            sem((2,)),
+            sem((3,)),
+            sem((3,)),
             sem((2, 4)),
             sem((18,)),
             sem((2,)),

time: 420 us -> 401 us (0.955)
  Pallas kernels: 388 us -> 369 us
    pallas_call x1, Pallas kernels: 180 us -> 170 us  [forward(): pl.pallas_call(partial(forward_kernel, n_layers), out_shape=outs, in_spec...]
    pallas_call x1, Pallas kernels: 208 us -> 200 us  [backward(): pl.pallas_call(partial(backward_kernel, n_layers), out_shape=(shape((rows...]
where the time goes in v5:
time: 401 us; the launch traced here: 393 us
  Pallas kernels  369 us (92%)
  local copies, waits for them, and re-layouts  19.4 us (5%)
    pallas_call x1, Pallas kernels, backward(): pl.pallas_call(partial(backward_kernel, n_layers), out_shape=(shape((rows...  200 us
    pallas_call x1, Pallas kernels, forward(): pl.pallas_call(partial(forward_kernel, n_layers), out_shape=outs, in_spec...  170 us
    unnamed x30, local copies, waits for them, and re-layouts  15 us

profile of v5, /device:TPU:0, one launch (start us, length us, event | category | flops | bytes accessed | tf_op | source)
XLA Modules:
  0.0 393.3 jit_solution(926079177046588757)
XLA Ops:
  0.6 0.0 copy-start.1
  0.7 0.0 copy-start.2
  1.4 0.7 add_convert_fusion
  2.2 0.5 fusion.4.refs_5_
  2.7 0.7 slice_bitcast_fusion.13
  3.4 0.7 slice_bitcast_fusion.12
  4.0 0.7 broadcast_in_dim.5.refs_4_
  4.7 0.7 slice_bitcast_fusion.10
  5.4 0.8 concatenate.16
  6.2 0.6 pad.8.refs_3_
  6.8 1.4 copy.21.refs_6_.refs_7_
  8.2 1.0 copy.20
  9.3 1.1 convert.18
  10.4 0.0 copy-done.1
  10.5 0.0 copy-done.2
  10.6 0.1 concatenate.15
  10.7 0.1 concatenate.14
  10.9 0.0 copy-start.6
  10.9 0.9 copy-done.6
  11.8 169.7 %forward.1 = (bf16[6,4,768,768]{3,2,1,0:T(8,128)(2,1)}, bf16[384,768]{1,0:T(8,128)(2,1)}, bf16[384,768]{1,0:T(8,128)(2,1)}, f32[1536,128]{1,0:T(8,128)}, f32[153...) custom-call(bf16[6,96,768]{2,1,0:T(8,128)(2,1)} %copy-done.6, ...), custom_call_target="tpu_custom_call" | custom-call | flops 99999997952 | bytes 100000000 | tf_op jit(solution)/shard_map/forward/pallas_call | solution.py:787
  181.6 199.6 %backward.1 = (f32[384,768]{1,0:T(8,128)}, bf16[384,768]{1,0:T(8,128)(2,1)}, f32[2,3,96,192]{3,2,1,0:T(8,128)}, f32[2,3,192]{2,1,0:T(4,128)}, f32[2,192,96]{2,1,...) custom-call(bf16[6,4,768,768]{3,2,1,0:T(8,128)(2,1)} %get-tuple-element, ...), custom_call_target="tpu_custom_call" | custom-call | flops 199999995904 | bytes 100000000 | tf_op jit(solution)/shard_map/backward/pallas_call | solution.py:1682
  381.2 0.0 copy-start
  381.2 1.4 copy.23
  382.6 1.3 copy.28
  383.9 1.4 copy.24
  385.3 2.2 copy.25
  387.5 2.0 copy.40
  389.5 0.0 copy-done
  389.5 1.0 copy.41
  390.5 0.8 copy.42
  391.3 0.7 copy.43
  392.0 0.8 copy.44
  (26 shorter events, 0.2 us)
Async XLA Ops:
  0.6 9.8 %copy-start.1 = (f32[2,768,96]{1,2,0:T(8,128)S(1)}, f32[2,768,96]{1,2,0:T(8,128)}, u32[]{:S(2)}) copy-start(f32[2,768,96]{1,2,0:T(8,128)} %param.18) | copy-start | bytes 1769476
  0.7 9.8 %copy-start.2 = (f32[2,3,96,192]{3,2,1,0:T(8,128)S(1)}, f32[2,3,96,192]{3,2,1,0:T(8,128)}, u32[]{:S(2)}) copy-start(f32[2,3,96,192]{3,2,1,0:T(8,128)} %param.12) | copy-start | bytes 1327108
  10.9 0.9 copy-start.6
  381.2 8.3 %copy-start = (f32[384,768]{1,0:T(8,128)S(1)}, f32[384,768]{1,0:T(8,128)}, u32[]{:S(2)}) copy-start(f32[384,768]{1,0:T(8,128)} %get-tuple-element.114) | copy-start | bytes 3538948
  387.5 3.0 copy-start.4
  389.5 1.8 copy-start.5
  389.5 2.5 copy-start.3

commit v6 on v5

--- a/solution.py
+++ b/solution.py
@@ -920,7 +920,7 @@
             dt_ref[4, at, :] = dv
         return 0
 
-    lax.fori_loop(0, keys // kblock, one_block, 0)
+    lax.fori_loop(0, keys // kblock, one_block, 0, unroll=2)
     if h >= 1:
         dq = jnp.transpose(dqt_ref[...]) * HD**-0.5
         if h == 1:

time: 401 us -> 398 us (level)
  no operation moved by 1% of the time
where the time goes in v6:
time: 398 us; the launch traced here: 391 us
  Pallas kernels  367 us (92%)
  local copies, waits for them, and re-layouts  19.4 us (5%)
    pallas_call x1, Pallas kernels, backward(): pl.pallas_call(partial(backward_kernel, n_layers), out_shape=(shape((rows...  197 us
    pallas_call x1, Pallas kernels, forward(): pl.pallas_call(partial(forward_kernel, n_layers), out_shape=outs, in_spec...  169 us
    unnamed x30, local copies, waits for them, and re-layouts  15 us

profile of v6, /device:TPU:0, one launch (start us, length us, event | category | flops | bytes accessed | tf_op | source)
XLA Modules:
  0.0 390.7 jit_solution(7015986874107407771)
XLA Ops:
  0.6 0.0 copy-start.1
  0.7 0.0 copy-start.2
  1.4 0.7 add_convert_fusion
  2.2 0.5 fusion.4.refs_5_
  2.7 0.7 slice_bitcast_fusion.13
  3.4 0.7 slice_bitcast_fusion.12
  4.0 0.7 broadcast_in_dim.5.refs_4_
  4.7 0.7 slice_bitcast_fusion.10
  5.4 0.8 concatenate.16
  6.2 0.6 pad.8.refs_3_
  6.8 1.4 copy.21.refs_6_.refs_7_
  8.2 1.0 copy.20
  9.3 1.1 convert.18
  10.4 0.0 copy-done.1
  10.5 0.0 copy-done.2
  10.6 0.1 concatenate.15
  10.7 0.1 concatenate.14
  10.9 0.0 copy-start.6
  10.9 0.9 copy-done.6
  11.8 169.5 %forward.1 = (bf16[6,4,768,768]{3,2,1,0:T(8,128)(2,1)}, bf16[384,768]{1,0:T(8,128)(2,1)}, bf16[384,768]{1,0:T(8,128)(2,1)}, f32[1536,128]{1,0:T(8,128)}, f32[153...) custom-call(bf16[6,96,768]{2,1,0:T(8,128)(2,1)} %copy-done.6, ...), custom_call_target="tpu_custom_call" | custom-call | flops 99999997952 | bytes 100000000 | tf_op jit(solution)/shard_map/forward/pallas_call | solution.py:787
  181.3 197.3 %backward.1 = (f32[384,768]{1,0:T(8,128)}, bf16[384,768]{1,0:T(8,128)(2,1)}, f32[2,3,96,192]{3,2,1,0:T(8,128)}, f32[2,3,192]{2,1,0:T(4,128)}, f32[2,192,96]{2,1,...) custom-call(bf16[6,4,768,768]{3,2,1,0:T(8,128)(2,1)} %get-tuple-element, ...), custom_call_target="tpu_custom_call" | custom-call | flops 199999995904 | bytes 100000000 | tf_op jit(solution)/shard_map/backward/pallas_call | solution.py:1682
  378.6 0.0 copy-start
  378.6 1.4 copy.23
  380.0 1.3 copy.28
  381.3 1.4 copy.24
  382.7 2.2 copy.25
  384.9 2.0 copy.40
  386.9 1.0 copy.41
  387.9 0.0 copy-done.4
  388.0 0.8 copy.42
  388.8 0.7 copy.43
  389.4 0.8 copy.44
  (26 shorter events, 0.2 us)
Async XLA Ops:
  0.6 9.8 %copy-start.1 = (f32[2,768,96]{1,2,0:T(8,128)S(1)}, f32[2,768,96]{1,2,0:T(8,128)}, u32[]{:S(2)}) copy-start(f32[2,768,96]{1,2,0:T(8,128)} %param.18) | copy-start | bytes 1769476
  0.7 9.8 %copy-start.2 = (f32[2,3,96,192]{3,2,1,0:T(8,128)S(1)}, f32[2,3,96,192]{3,2,1,0:T(8,128)}, u32[]{:S(2)}) copy-start(f32[2,3,96,192]{3,2,1,0:T(8,128)} %param.12) | copy-start | bytes 1327108
  10.9 0.9 copy-start.6
  378.6 8.3 %copy-start = (f32[384,768]{1,0:T(8,128)S(1)}, f32[384,768]{1,0:T(8,128)}, u32[]{:S(2)}) copy-start(f32[384,768]{1,0:T(8,128)} %get-tuple-element.114) | copy-start | bytes 3538948
  384.9 3.0 copy-start.4
  386.9 1.8 copy-start.5
  386.9 2.5 copy-start.3
